TPU v7x, 128 devices: a whole 4x4x4 slice. The times are simulated.
128 devices in a mesh: shard: 8 (over z_hi, x), rep: 16 (over y, z_lo, core).
Axes of the slice: x: 4, y: 4, z: 4 (z_hi: 2, z_lo: 2; z = z_hi * 2 + z_lo), core: 2. Of those that a mesh axis runs over, the one named last changes fastest.
Arguments:
- latents: bfloat16 [1024, 256, 384], P(('shard', 'rep')), may hold values from -6 to 6
- conditions: bfloat16 [1024, 384], P(('shard', 'rep')), may hold values from -6 to 6
- counts: int32 [128], P(('shard', 'rep')), may hold values from 0 to 8, as said below
- mod_weight: bfloat16 [384, 2304], P('shard'), may hold values from -0.3125 to 0.3125
- mod_bias: bfloat16 [2304], P('shard'), may hold values from -3 to 3
- qkv_weight: bfloat16 [384, 1152], P('shard'), may hold values from -0.3125 to 0.3125
- qv_bias: bfloat16 [768], P('shard'), may hold values from -3 to 3
- proj_weight: bfloat16 [384, 384], P('shard'), may hold values from -1.25 to 1.25
- proj_bias: bfloat16 [384], P('shard'), may hold values from -3 to 3
- up_weight: bfloat16 [384, 1536], P('shard'), may hold values from -0.3125 to 0.3125
- up_bias: bfloat16 [1536], P('shard'), may hold values from -3 to 3
- down_weight: bfloat16 [1536, 384], P('shard'), may hold values from -0.15625 to 0.15625
- down_bias: bfloat16 [384], P('shard'), may hold values from -3 to 3
- grad_out: bfloat16 [1024, 256, 384], P(('shard', 'rep')), may hold values from -6 to 6
Outputs:
- output: bfloat16 [1024, 256, 384], P(('shard', 'rep'))
- grad_latents: bfloat16 [1024, 256, 384], P(('shard', 'rep'))
- grad_conditions: bfloat16 [1024, 384], P(('shard', 'rep'))
- grad_mod_weight: float32 [384, 2304], P('shard')
- grad_mod_bias: float32 [2304], P('shard')
- grad_qkv_weight: float32 [384, 1152], P('shard')
- grad_qv_bias: float32 [768], P('shard')
- grad_proj_weight: float32 [384, 384], P('shard')
- grad_proj_bias: float32 [384], P('shard')
- grad_up_weight: float32 [384, 1536], P('shard')
- grad_up_bias: float32 [1536], P('shard')
- grad_down_weight: float32 [1536, 384], P('shard')
- grad_down_bias: float32 [384], P('shard')
Inputs may be any that keep to these rules, and one draw needn't show every extreme that they name: Device d (shard index slowest, then rep) holds its latents in its first counts[d] of 8 slots; the other slots are padding. Some device holds 8 latents and some holds none.
All inputs are finite; a program needn't handle non-finite values.
Results may differ from a plain program's by a relative error of at most 0.023.
Values may be sent and summed in bfloat16 or wider, within the bound.
No kernel may reach another device: no remote copies, remote signals or barrier semaphores. Data moves between devices by JAX's collectives and lax.ppermute only.
A program may use at most 192 MiB of HBM per device.

v0:
```python
import functools

import jax
import jax.numpy as jnp
from jax import lax
from jax.experimental import pallas as pl
from jax.experimental.pallas import tpu as pltpu
from jax.sharding import PartitionSpec as P

D = 384
HEADS = 6
HEAD_DIM = 64
FF = 1536
TOK = 256
CAP = 8
PAIR = 2
STEPS = CAP // PAIR
TWIN = 128
BF = jnp.bfloat16
F32 = jnp.float32
MIB = 1024 * 1024

LANES_ONE = 2048
QKV_W = 3 * D
MOD_ONE = 2 * D
BIAS_ONE = QKV_W + MOD_ONE
LANES_TWO = 5120
MOD_TWO = 4 * D
AT_MOD = FF
AT_PROJ = AT_MOD + MOD_TWO
AT_DOWN = AT_PROJ + D
BIAS_TWO = AT_DOWN + FF
ROW_QKV, ROW_MOD, ROW_PROJ, ROW_UP, ROW_DOWN = 0, 9, 27, 30, 42


def dot(left, right):
    return jnp.dot(left, right, preferred_element_type=F32)


def dot_tn(left, right):
    return lax.dot_general(left, right, (((0,), (0,)), ((), ())), preferred_element_type=F32)


def dot_nt(left, right):
    return lax.dot_general(left, right, (((1,), (1,)), ((), ())), preferred_element_type=F32)


def normalize(value):
    center = jnp.mean(value, axis=-1, keepdims=True)
    centered = value - center
    spread = jnp.mean(centered * centered, axis=-1, keepdims=True)
    inverse = lax.rsqrt(spread + 1e-06)
    return centered * inverse, inverse


def norm_back(grad, normed, inverse):
    first = jnp.mean(grad, axis=-1, keepdims=True)
    second = jnp.mean(grad * normed, axis=-1, keepdims=True)
    return inverse * (grad - first - normed * second)


def spread(rows, size):
    width = 8 * size
    lane = lax.broadcasted_iota(jnp.int32, (8, width), 1)
    total = jnp.zeros((8, width), F32)
    for owner, row in enumerate(rows):
        padded = jnp.concatenate([row, jnp.zeros((1, width - row.shape[1]), F32)], axis=1)
        padded = jnp.where(lane < size, jnp.broadcast_to(padded, (8, width)), 0.0)
        total += pltpu.roll(padded, owner * size, 1) if owner else padded
    return total[0:1]


def all_biases(raw):
    def rows(first, count):
        return [
            jnp.concatenate([block[first + i : first + i + 1] for i in range(count)], axis=1)
            for block in raw
        ]

    qv = spread(rows(0, 1), 96)
    full = [qv[:, :D], jnp.zeros((1, D), F32), qv[:, D:]]
    full += [spread(rows(1, 3), 288), spread(rows(4, 1), 48)]
    full += [spread(rows(5, 2), 192), spread(rows(7, 1), 48)]
    full = jnp.concatenate(full, axis=1)
    cut = [full[:, 128 * i : 128 * i + 128] for i in range(45)]
    return jnp.concatenate(cut + [jnp.zeros((3, 128), F32)], axis=0)


def bias_row(bias, first, count):
    return jnp.concatenate([bias[first + i : first + i + 1, :] for i in range(count)], axis=1)


def silu(cond):
    return cond * (1.0 / (1.0 + jnp.exp(-cond)))


def assemble(info, pieces, full):
    column, z_high, core = info[1], info[2], info[3]
    for k in range(4):
        spot = lax.rem(column + k, 4) * 48
        mine = (z_high ^ core) * 192 + spot
        other = (1 - (z_high ^ core)) * 192 + spot
        full[pl.ds(pl.multiple_of(mine, 16), 48), :] = pieces[k][...]
        full[pl.ds(pl.multiple_of(other, 16), 48), :] = pieces[4 + k][...]


def forward_kernel(
    info, latents, conditions, p0, p1, p2, p3, p4, p5, p6, p7,
    weights, bias_out, mod_out, qkv_out, expo_out, mixed_out, rinv_out, hidden_out,
):
    step = pl.program_id(0)

    @pl.when(step == 0)
    def _():
        assemble(info, (p0, p1, p2, p3, p4, p5, p6, p7), weights)
        total = all_biases(
            [
                weights[48 * k : 48 * k + 16, BIAS_ONE : BIAS_ONE + 128].astype(F32)[:8]
                for k in range(8)
            ]
        )
        bias_out[...] = total
        cond_low = silu(conditions[...].astype(F32)).astype(BF)
        mod_out[...] = dot(cond_low, weights[:, QKV_W : QKV_W + MOD_ONE]) + bias_row(
            total, ROW_MOD, 6
        )

    @pl.when(PAIR * step < info[0])
    def _():
        hidden = []
        for i in range(PAIR):
            mod = mod_out[pl.ds(PAIR * step + i, 1), :]
            normed, _ = normalize(latents[i].astype(F32))
            hidden.append((normed * (1.0 + mod[:, D : 2 * D]) + mod[:, :D]).astype(BF))
            hidden_out[PAIR * step + i] = hidden[i]
        full_bias = bias_row(bias_out[0:16, :], ROW_QKV, 9)
        qkv_all = dot(jnp.concatenate(hidden, axis=0), weights[:, :QKV_W])
        qkv_all = (qkv_all + full_bias).astype(BF)
        low = lax.broadcasted_iota(jnp.int32, (TOK, 128), 1) < HEAD_DIM
        ones = jnp.ones((TOK, 128), BF)
        for i in range(PAIR):
            slot = PAIR * step + i
            qkv = qkv_all[TOK * i : TOK * i + TOK]
            qkv_out[slot] = qkv
            for pair in range(HEADS // 2):
                at = 128 * pair
                query = qkv[:, at : at + 128] * jnp.asarray(HEAD_DIM**-0.5, BF)
                key = qkv[:, D + at : D + at + 128]
                value = jnp.concatenate([qkv[:, 2 * D + at : 2 * D + at + 128], ones], axis=1)
                parts = []
                for half in range(2):
                    chosen = jnp.where(low if half == 0 else ~low, query, jnp.zeros_like(query))
                    scores = dot_nt(chosen, key)
                    expo = jnp.exp(scores - jnp.max(scores, axis=-1, keepdims=True)).astype(BF)
                    expo_out[slot, 2 * pair + half] = expo
                    parts.append(dot(expo, value))
                total = jnp.where(low, parts[0][:, 128:], parts[1][:, 128:])
                inverse = 1.0 / total
                rinv_out[slot, :, at : at + 128] = inverse
                mixed_out[slot, :, at : at + 128] = (
                    jnp.where(low, parts[0][:, :128], parts[1][:, :128]) * inverse
                ).astype(BF)


def middle_kernel(
    info, latents, conditions, mixed_in, grad_out, bias_in, p0, p1, p2, p3, p4, p5, p6, p7,
    weights, out, grad_mid_out, grad_mixed_out, grad_mod, keep, send,
    mod, acc_up, acc_down, acc_proj, acc_bias,
):
    step = pl.program_id(0)

    @pl.when(step == 0)
    def _():
        assemble(info, (p0, p1, p2, p3, p4, p5, p6, p7), weights)
        cond_low = silu(conditions[...].astype(F32)).astype(BF)
        mod[...] = dot(cond_low, weights[:, AT_MOD : AT_MOD + MOD_TWO]) + bias_row(
            bias_in[...], ROW_MOD + 6, 12
        )
        acc_up[...] = jnp.zeros_like(acc_up)
        acc_down[...] = jnp.zeros_like(acc_down)
        acc_proj[...] = jnp.zeros_like(acc_proj)
        acc_bias[...] = jnp.zeros_like(acc_bias)
        grad_mod[...] = jnp.zeros_like(grad_mod)

    @pl.when(PAIR * step >= info[0])
    def _():
        out[...] = jnp.zeros((PAIR, TOK, D), BF)

    @pl.when(PAIR * step < info[0])
    def _():
        bias = bias_in[...]
        w_proj = weights[:, AT_PROJ : AT_PROJ + D]
        up_bias = bias_row(bias, ROW_UP, 12)
        mixed = mixed_in[pl.ds(PAIR * step, PAIR)].reshape(PAIR * TOK, D)
        branch_all = dot(mixed, w_proj) + bias_row(bias, ROW_PROJ, 3)
        rows = [mod[pl.ds(PAIR * step + i, 1), :] for i in range(PAIR)]
        span = [slice(TOK * i, TOK * i + TOK) for i in range(PAIR)]
        middle, normed, inverse, hidden, cot, g_two = [], [], [], [], [], []
        for i in range(PAIR):
            row = rows[i]
            middle.append(latents[i].astype(F32) + row[:, :D] * branch_all[span[i]])
            value, scale = normalize(middle[i])
            normed.append(value)
            inverse.append(scale)
            hidden.append((value * (1.0 + row[:, 2 * D : 3 * D]) + row[:, D : 2 * D]).astype(BF))
            held = (PAIR * step + i < info[0]).astype(F32)
            cot.append(grad_out[i].astype(F32) * held)
            g_two.append((cot[i] * row[:, 3 * D :]).astype(BF))
        hidden = jnp.concatenate(hidden, axis=0)
        g_two = jnp.concatenate(g_two, axis=0)
        branch_two = bias_row(bias, ROW_DOWN, 3)
        d_hidden = jnp.zeros((PAIR * TOK, D), F32)
        root = 0.7978845608028654
        cube = root * 0.044715
        for chunk in range(4):
            at = D * chunk
            w_up = weights[:, at : at + D]
            w_down = jnp.concatenate(
                [
                    weights[48 * s : 48 * s + 48, AT_DOWN + D * q : AT_DOWN + D * q + D]
                    for s in (2 * chunk, 2 * chunk + 1)
                    for q in range(4)
                ],
                axis=0,
            )
            upward = dot(hidden, w_up) + up_bias[:, at : at + D]
            square = upward * upward
            bend = jnp.tanh(upward * (root + cube * square))
            half = 0.5 + 0.5 * bend
            act = upward * half
            slope = half + act * (1.0 - bend) * (root + (3.0 * cube) * square)
            act_low = act.astype(BF)
            branch_two = branch_two + dot(act_low, w_down)
            acc_down[at : at + D, :] += dot_tn(act_low, g_two)
            g_up = (slope * dot_nt(g_two, w_down)).astype(BF)
            acc_up[:, at : at + D] += dot_tn(hidden, g_up)
            acc_bias[0:1, at : at + D] += jnp.sum(g_up.astype(F32), axis=0, keepdims=True)
            d_hidden = d_hidden + dot_nt(g_up, w_up)
        acc_bias[1:2, :D] += jnp.sum(g_two.astype(F32), axis=0, keepdims=True)
        g_one = []
        for i in range(PAIR):
            row, slot = rows[i], PAIR * step + i
            d_hid, br_two = d_hidden[span[i]], branch_two[span[i]]
            held = (slot < info[0]).astype(F32)
            out[i] = ((middle[i] + row[:, 3 * D :] * br_two) * held).astype(BF)
            grad_mod[pl.ds(slot, 1), 3 * D :] = jnp.sum(cot[i] * br_two, axis=0, keepdims=True)
            grad_mod[pl.ds(slot, 1), D : 2 * D] = jnp.sum(d_hid, axis=0, keepdims=True)
            grad_mod[pl.ds(slot, 1), 2 * D : 3 * D] = jnp.sum(
                d_hid * normed[i], axis=0, keepdims=True
            )
            grad_mid = cot[i] + norm_back(
                d_hid * (1.0 + row[:, 2 * D : 3 * D]), normed[i], inverse[i]
            )
            grad_mid_out[slot] = grad_mid
            grad_mod[pl.ds(slot, 1), :D] = jnp.sum(
                grad_mid * branch_all[span[i]], axis=0, keepdims=True
            )
            g_one.append((grad_mid * row[:, :D]).astype(BF))
        g_one = jnp.concatenate(g_one, axis=0)
        acc_bias[2:3, :D] += jnp.sum(g_one.astype(F32), axis=0, keepdims=True)
        acc_proj[...] += dot_tn(mixed, g_one)
        grad_mixed_out[pl.ds(PAIR * step, PAIR)] = (
            dot_nt(g_one, w_proj).astype(BF).reshape(PAIR, TOK, D)
        )

    @pl.when(step == STEPS - 1)
    def _():
        cond_low = silu(conditions[...].astype(F32)).astype(BF)
        g_mod = grad_mod[...].astype(BF)
        mod_grad = dot_tn(cond_low.astype(F32), g_mod.astype(F32)).astype(BF)
        z_high, core, column = info[2], info[3], info[1]
        sums = jnp.sum(g_mod.astype(F32), axis=0, keepdims=True)
        rows = [jnp.zeros((ROW_MOD + 6, 128), F32)]
        rows += [sums[:, 128 * i : 128 * i + 128] for i in range(12)]
        rows += [acc_bias[2:3, 128 * i : 128 * i + 128] for i in range(3)]
        rows += [acc_bias[0:1, 128 * i : 128 * i + 128] for i in range(12)]
        rows += [acc_bias[1:2, 128 * i : 128 * i + 128] for i in range(3)]
        rows += [jnp.zeros((3, 128), F32)]
        bias_block = jnp.concatenate(rows, axis=0).astype(BF)
        for owner in range(8):
            zh, xx = owner // 4, owner % 4
            spot = lax.rem(xx - column + 4, 4) * 48
            spot = pl.multiple_of(spot, 16)
            is_mine = (z_high ^ core) == zh
            lo = 48 * owner

            def put(ref, spot=spot, lo=lo, owner=owner):
                ref[pl.ds(spot, 48), :FF] = acc_up[lo : lo + 48, :].astype(BF)
                ref[pl.ds(spot, 48), AT_MOD : AT_MOD + MOD_TWO] = mod_grad[lo : lo + 48, :]
                ref[pl.ds(spot, 48), AT_PROJ : AT_PROJ + D] = acc_proj[lo : lo + 48, :].astype(BF)
                for q in range(4):
                    at = 192 * owner + 48 * q
                    ref[pl.ds(spot, 48), AT_DOWN + D * q : AT_DOWN + D * q + D] = acc_down[
                        at : at + 48, :
                    ].astype(BF)
                ref[pl.ds(spot, 48), BIAS_TWO : BIAS_TWO + 128] = bias_block

            pl.when(is_mine)(functools.partial(put, keep))
            pl.when(jnp.logical_not(is_mine))(functools.partial(put, send))


def backward_kernel(
    first, last,
    info, latents, conditions, qkv_in, expo_in, mixed_in, rinv_in, hidden_in, grad_mid_in,
    grad_mixed_in, mod_in, weights, *refs,
):
    if last:
        weights_two, grad_mod_two, acc_in, bias_in, grad_mod_in, _, out, grad_cond, keep, send = refs[:10]
        acc_qkv, acc_bias, grad_mod = refs[10:]
    else:
        out, acc_qkv, acc_bias, grad_mod = refs
    step = pl.program_id(0)
    slot = PAIR * (step + first)

    @pl.when(step == 0)
    def _():
        if last:
            acc_qkv[...] = acc_in[...]
            acc_bias[...] = bias_in[...]
            grad_mod[...] = grad_mod_in[...]
        else:
            acc_qkv[...] = jnp.zeros_like(acc_qkv)
            acc_bias[...] = jnp.zeros_like(acc_bias)
            grad_mod[...] = jnp.zeros_like(grad_mod)

    @pl.when(slot >= info[0])
    def _():
        out[...] = jnp.zeros((PAIR, TOK, D), BF)

    @pl.when(slot < info[0])
    def _():
        low = lax.broadcasted_iota(jnp.int32, (TOK, 128), 1) < HEAD_DIM
        factor = HEAD_DIM**-0.5
        g_all = []
        for i in range(PAIR):
            qkv = qkv_in[slot + i]
            scaled = (grad_mixed_in[slot + i].astype(F32) * rinv_in[slot + i]).astype(BF)
            product = scaled.astype(F32) * mixed_in[slot + i].astype(F32)
            g_query, g_key, g_value = [], [], []
            for pair in range(HEADS // 2):
                at = 128 * pair
                query = qkv[:, at : at + 128]
                key = qkv[:, D + at : D + at + 128]
                value = qkv[:, 2 * D + at : 2 * D + at + 128]
                grad = scaled[:, at : at + 128]
                weighed = product[:, at : at + 128]
                parts = []
                for half in range(2):
                    mask = low if half == 0 else ~low
                    chosen = jnp.where(mask, grad, jnp.zeros_like(grad))
                    delta = jnp.sum(jnp.where(mask, weighed, 0.0), axis=-1, keepdims=True)
                    expo = expo_in[slot + i, 2 * pair + half]
                    g_probs = dot_nt(chosen, value)
                    g_scores = (expo.astype(F32) * (g_probs - delta)).astype(BF)
                    parts.append(
                        (dot(g_scores, key), dot_tn(g_scores, query), dot_tn(expo, grad))
                    )
                g_query.append((jnp.where(low, parts[0][0], parts[1][0]) * factor).astype(BF))
                g_key.append((jnp.where(low, parts[0][1], parts[1][1]) * factor).astype(BF))
                g_value.append(jnp.where(low, parts[0][2], parts[1][2]).astype(BF))
            g_all.append(jnp.concatenate(g_query + g_key + g_value, axis=1))
        g_qkv = jnp.concatenate(g_all, axis=0)
        hidden = hidden_in[pl.ds(slot, PAIR)].reshape(PAIR * TOK, D)
        acc_qkv[...] += dot_tn(hidden, g_qkv)
        acc_bias[0:1, :] += jnp.sum(g_qkv.astype(F32), axis=0, keepdims=True)
        d_all = dot_nt(g_qkv, weights[:, :QKV_W])
        for i in range(PAIR):
            row = mod_in[pl.ds(slot + i, 1), :]
            normed, inverse = normalize(latents[i].astype(F32))
            d_hidden = d_all[TOK * i : TOK * i + TOK]
            grad_mod[pl.ds(slot + i, 1), :D] = jnp.sum(d_hidden, axis=0, keepdims=True)
            grad_mod[pl.ds(slot + i, 1), D:] = jnp.sum(d_hidden * normed, axis=0, keepdims=True)
            back = norm_back(d_hidden * (1.0 + row[:, D : 2 * D]), normed, inverse)
            out[i] = (grad_mid_in[slot + i] + back).astype(BF)

    if not last:
        return

    @pl.when(step == STEPS - 1 - first)
    def _():
        cond = conditions[...].astype(F32)
        sig = 1.0 / (1.0 + jnp.exp(-cond))
        cond_low = (cond * sig).astype(BF)
        g_mod = grad_mod[...].astype(BF)
        g_mod_two = grad_mod_two[...].astype(BF)
        g_cond = dot_nt(g_mod, weights[:, QKV_W : QKV_W + MOD_ONE])
        g_cond += dot_nt(g_mod_two, weights_two[:, AT_MOD : AT_MOD + MOD_TWO])
        grad_cond[...] = (g_cond * (sig * (1.0 + cond * (1.0 - sig)))).astype(BF)
        mod_grad = dot_tn(cond_low.astype(F32), g_mod.astype(F32)).astype(BF)
        sums = jnp.sum(g_mod.astype(F32), axis=0, keepdims=True)
        rows = [acc_bias[0:1, 128 * i : 128 * i + 128] for i in range(9)]
        rows += [sums[:, 128 * i : 128 * i + 128] for i in range(6)]
        rows += [jnp.zeros((33, 128), F32)]
        bias_block = jnp.concatenate(rows, axis=0).astype(BF)
        z_high, core, column = info[2], info[3], info[1]
        for owner in range(8):
            zh, xx = owner // 4, owner % 4
            spot = pl.multiple_of(lax.rem(xx - column + 4, 4) * 48, 16)
            is_mine = (z_high ^ core) == zh
            lo = 48 * owner

            def put(ref, spot=spot, lo=lo):
                ref[pl.ds(spot, 48), :QKV_W] = acc_qkv[lo : lo + 48, :].astype(BF)
                ref[pl.ds(spot, 48), QKV_W : QKV_W + MOD_ONE] = mod_grad[lo : lo + 48, :]
                ref[pl.ds(spot, 48), BIAS_ONE : BIAS_ONE + 128] = bias_block

            pl.when(is_mine)(functools.partial(put, keep))
            pl.when(jnp.logical_not(is_mine))(functools.partial(put, send))


def slot_spec(first=0):
    def index(j, info):
        return (jnp.minimum(j + first, jnp.maximum((info[0] + 1) // 2 - 1, 0)), 0, 0)

    return pl.BlockSpec((PAIR, TOK, D), index)


def slot_out(first=0):
    return pl.BlockSpec((PAIR, TOK, D), lambda j, info: (j + first, 0, 0))


def held():
    return pl.BlockSpec(memory_space=pltpu.VMEM)


def whole(*shape):
    zeros = (0,) * len(shape)
    return pl.BlockSpec(shape, lambda j, info: zeros)


def params(mib):
    return pltpu.CompilerParams(
        dimension_semantics=("arbitrary",), vmem_limit_bytes=mib * MIB
    )


def far(value):
    return pltpu.with_memory_space_constraint(value, pltpu.HBM)


def stay(value):
    return pltpu.with_memory_space_constraint(value, pltpu.VMEM)


def run_forward(info, latents, conditions, pieces):
    return pl.pallas_call(
        forward_kernel,
        grid_spec=pltpu.PrefetchScalarGridSpec(
            num_scalar_prefetch=1,
            grid=(STEPS,),
            in_specs=[slot_spec(), whole(CAP, D)] + [held()] * 8,
            out_specs=[held()] * 8,
        ),
        out_shape=[
            pltpu.VMEM((D, LANES_ONE), BF),
            pltpu.VMEM((48, 128), F32),
            pltpu.VMEM((CAP, MOD_ONE), F32),
            pltpu.VMEM((CAP, TOK, QKV_W), BF),
            pltpu.VMEM((CAP, HEADS, TOK, TOK), BF),
            pltpu.VMEM((CAP, TOK, D), BF),
            pltpu.VMEM((CAP, TOK, D), F32),
            pltpu.VMEM((CAP, TOK, D), BF),
        ],
        compiler_params=params(13),
        name="attention_forward",
        cost_estimate=pl.CostEstimate(
            flops=3_000_000_000, bytes_accessed=20_000_000, transcendentals=3_000_000
        ),
    )(info, far(latents), far(conditions), *pieces)


def run_middle(info, latents, conditions, mixed, grad_out, bias, pieces):
    return pl.pallas_call(
        middle_kernel,
        grid_spec=pltpu.PrefetchScalarGridSpec(
            num_scalar_prefetch=1,
            grid=(STEPS,),
            in_specs=[
                slot_spec(),
                whole(CAP, D),
                held(),
                slot_spec(),
                held(),
            ]
            + [held()] * 8,
            out_specs=[held(), slot_out()] + [held()] * 5,
            scratch_shapes=[
                pltpu.VMEM((CAP, MOD_TWO), F32),
                pltpu.VMEM((D, FF), F32),
                pltpu.VMEM((FF, D), F32),
                pltpu.VMEM((D, D), F32),
                pltpu.VMEM((8, FF), F32),
            ],
        ),
        out_shape=[
            pltpu.VMEM((D, LANES_TWO), BF),
            jax.ShapeDtypeStruct((CAP, TOK, D), BF),
            pltpu.VMEM((CAP, TOK, D), F32),
            pltpu.VMEM((CAP, TOK, D), BF),
            pltpu.VMEM((CAP, MOD_TWO), F32),
            pltpu.VMEM((192, LANES_TWO), BF),
            pltpu.VMEM((192, LANES_TWO), BF),
        ],
        compiler_params=params(22),
        name="feed_forward_both_ways",
        cost_estimate=pl.CostEstimate(
            flops=16_000_000_000, bytes_accessed=30_000_000, transcendentals=3_000_000
        ),
    )(info, far(latents), far(conditions), stay(mixed), far(grad_out), stay(bias), *pieces)


def run_backward(first, count, info, latents, shared, carried=None):
    last = carried is not None

    in_specs = [slot_spec(first), whole(CAP, D)] + [held()] * 9
    out_specs = [slot_out(first)]
    out_shape = [jax.ShapeDtypeStruct((CAP, TOK, D), BF)]
    state = [(D, QKV_W), (8, QKV_W), (CAP, MOD_ONE)]
    if last:
        in_specs += [held()] * 5 + [pl.BlockSpec(memory_space=pl.ANY)]
        out_specs += [whole(CAP, D), held(), held()]
        out_shape += [jax.ShapeDtypeStruct((CAP, D), BF)]
        out_shape += [pltpu.VMEM((192, LANES_ONE), BF)] * 2
    else:
        out_specs += [held()] * 3
        out_shape += [pltpu.VMEM(shape, F32) for shape in state]
    return pl.pallas_call(
        functools.partial(backward_kernel, first, last),
        grid_spec=pltpu.PrefetchScalarGridSpec(
            num_scalar_prefetch=1,
            grid=(count,),
            in_specs=in_specs,
            out_specs=out_specs,
            scratch_shapes=[pltpu.VMEM(shape, F32) for shape in state] if last else [],
        ),
        out_shape=out_shape,
        input_output_aliases={17: 0} if last else {},
        compiler_params=params(15),
        name="attention_backward_rest" if last else "attention_backward_start",
        cost_estimate=pl.CostEstimate(
            flops=2_200_000_000 * count, bytes_accessed=8_000_000 * count, transcendentals=1_000
        ),
    )(info, far(latents), far(shared[0]), *map(stay, shared[1:]), *map(stay, (carried or ())[:-1]), *(carried or ())[-1:])


def place(index):
    shard, rep = divmod(index, 16)
    return shard // 4, shard % 4, rep // 4, (rep // 2) % 2, rep % 2


def index_of(z_high, x, y, z_low, core):
    return (z_high * 4 + x) * 16 + y * 4 + z_low * 2 + core


def routes(target_of):
    return [(i, target_of(*place(i))) for i in range(TWIN)]


def fetch(k):
    def source(zh, x, y, zl, c):
        if c == 0:
            return index_of(zh, (x + k) % 4, y, zl, c)
        return index_of(1 - zh, (x + k) % 4, y, 1 - zl, c)

    return [(source(*place(i)), i) for i in range(TWIN)]


CORE_SWAP = routes(lambda zh, x, y, zl, c: index_of(zh, x, y, zl, 1 - c))
ZLOW_SWAP = routes(lambda zh, x, y, zl, c: index_of(zh, x, y, 1 - zl, c))
BOTH = ("shard", "rep")


def move(value, pairs):
    return lax.ppermute(value, BOTH, pairs)


def y_route(k):
    return routes(lambda zh, x, y, zl, c: index_of(zh, x, (y + k) % 4, zl, c))


def after(value, *earlier):
    return lax.optimization_barrier((value, *earlier))[0]


def fetch_all(block):
    return [move(block, fetch(k)) for k in range(4)]


def swap_all(pieces):
    return [move(piece, CORE_SWAP) for piece in pieces]


def small_call(kernel, name, shapes, *values, scalars=False):
    return pl.pallas_call(
        kernel,
        in_specs=[pl.BlockSpec(memory_space=pltpu.SMEM)] * scalars
        + [held()] * (len(values) - scalars),
        out_shape=[jax.ShapeDtypeStruct(shape, BF) for shape in shapes],
        compiler_params=pltpu.CompilerParams(vmem_limit_bytes=14 * MIB),
        name=name,
    )(*values)


def add_kernel(*refs):
    refs[-1][...] = sum(ref[...].astype(F32) for ref in refs[:-1]).astype(BF)


def add(*values):
    return small_call(add_kernel, "add", [values[0].shape], *values)[0]


def add_blocks_kernel(left, right, *outs):
    for k, out in enumerate(outs):
        rows = slice(48 * k, 48 * k + 48)
        out[...] = (left[rows, :].astype(F32) + right[rows, :].astype(F32)).astype(BF)


def add_blocks(left, right):
    shape = (48, left.shape[1])
    return small_call(add_blocks_kernel, "add_blocks", [shape] * 4, left, right)


def add_halves_kernel(info, *refs):
    lanes = refs[-1].shape[1]
    for out, core in ((refs[-2], info[3]), (refs[-1], 1 - info[3])):
        at = pl.ds(pl.multiple_of(core * lanes, 128), lanes)
        out[...] = sum(ref[:, at].astype(F32) for ref in refs[:-2]).astype(BF)


def add_halves(info, pieces):
    shape = (48, pieces[0].shape[1] // 2)
    return small_call(
        add_halves_kernel, "add_halves", [shape] * 2, info, *pieces, scalars=True
    )


def scatter(blocks):
    back = [[(target, source) for source, target in fetch(k)] for k in range(4)]
    return [move(block, pairs) for block, pairs in zip(blocks, back)]


def sum_replicas(arrived, info):
    mine, other = add_halves(info, arrived)
    total = add(mine, move(other, CORE_SWAP))
    total = add(total, move(total, ZLOW_SWAP))
    total = add(total, *(move(total, y_route(k)) for k in (1, 2, 3)))
    return [total, move(total, CORE_SWAP)]


def row_of(ref):
    size = ref.shape[0]
    row = ref[...].astype(F32).reshape(1, size)
    if size % 128:
        row = jnp.concatenate([row, jnp.zeros((1, -size % 128), F32)], axis=1)
    return row


def pack_one_kernel(qkv, mod, qv_bias, mod_bias, proj_bias, up_bias, down_bias, out):
    out[:, :QKV_W] = qkv[...]
    out[:, QKV_W:BIAS_ONE] = mod[:, :MOD_ONE]
    flat = [row_of(ref) for ref in (qv_bias, mod_bias, proj_bias, up_bias, down_bias)]
    flat = jnp.concatenate(flat, axis=1)
    rows = [flat[:, 128 * i : 128 * i + 128] for i in range(8)] + [jnp.zeros((40, 128), F32)]
    out[:, BIAS_ONE:] = jnp.concatenate(rows, axis=0).astype(BF)


def pack_two_kernel(up, mod, proj, down, out):
    out[:, :FF] = up[...]
    out[:, AT_MOD:AT_PROJ] = mod[:, MOD_ONE:]
    out[:, AT_PROJ:AT_DOWN] = proj[...]
    for q in range(4):
        out[:, AT_DOWN + D * q : AT_DOWN + D * q + D] = down[48 * q : 48 * q + 48, :]
    out[:, BIAS_TWO:] = jnp.zeros((48, 128), BF)


def pack(kernel, name, lanes, *values):
    def once(shape):
        return pl.BlockSpec(shape, lambda j: (0,) * len(shape))

    return pl.pallas_call(
        kernel,
        grid=(1,),
        in_specs=[once(value.shape) for value in values],
        out_specs=once((48, lanes)),
        out_shape=pltpu.VMEM((48, lanes), BF),
        compiler_params=pltpu.CompilerParams(vmem_limit_bytes=8 * MIB),
        name=name,
    )(*map(far, values))


def finish_kernel(
    info, one_a, one_b, two_a, two_b, g_mod, g_mod_bias, g_qkv, g_qv_bias, g_proj, g_proj_bias,
    g_up, g_up_bias, g_down, g_down_bias,
):
    shard, first = info[1] + 4 * info[2], info[3] == 0

    def joined(mine, other):
        mine, other = mine[...].astype(F32), other[...].astype(F32)
        return jnp.concatenate(
            [jnp.where(first, mine, other), jnp.where(first, other, mine)], axis=1
        )

    one, two = joined(one_a, one_b), joined(two_a, two_b)
    g_mod[:, :MOD_ONE] = one[:, QKV_W:BIAS_ONE]
    g_mod[:, MOD_ONE:] = two[:, AT_MOD:AT_PROJ]
    g_qkv[...] = one[:, :QKV_W]
    g_proj[...] = two[:, AT_PROJ:AT_DOWN]
    g_up[...] = two[:, :FF]
    for q in range(4):
        g_down[48 * q : 48 * q + 48, :] = two[:, AT_DOWN + D * q : AT_DOWN + D * q + D]
    bias = one[:, BIAS_ONE:] + two[:, BIAS_TWO:]

    def own(first_row, count, size, out):
        row = bias_row(bias, first_row, count)
        row = jnp.broadcast_to(row, (8, 128 * count))
        turn = lax.rem(8 * size - shard * size, 8 * size)
        out[...] = pltpu.roll(row, turn, 1)[0:1, :size].reshape(size)

    own(ROW_MOD, 18, 288, g_mod_bias)
    query, value = bias_row(bias, 0, 3), bias_row(bias, 6, 3)
    row = jnp.broadcast_to(jnp.concatenate([query, value], axis=1), (8, 2 * D))
    turn = lax.rem(2 * D - shard * 96, 2 * D)
    g_qv_bias[...] = pltpu.roll(row, turn, 1)[0:1, :96].reshape(96)
    own(ROW_PROJ, 3, 48, g_proj_bias)
    own(ROW_UP, 12, 192, g_up_bias)
    own(ROW_DOWN, 3, 48, g_down_bias)


def finish(info, parts):
    shapes = [
        (48, 6 * D), (288,), (48, QKV_W), (96,), (48, D), (48,), (48, FF), (192,), (192, D), (48,),
    ]
    return pl.pallas_call(
        finish_kernel,
        in_specs=[pl.BlockSpec(memory_space=pltpu.SMEM)] + [held()] * 4,
        out_shape=[jax.ShapeDtypeStruct(shape, F32) for shape in shapes],
        compiler_params=pltpu.CompilerParams(vmem_limit_bytes=12 * MIB),
        name="unpack_gradients",
    )(info, *parts)


def on_device(
    latents, conditions, counts, mod_weight, mod_bias, qkv_weight, qv_bias, proj_weight,
    proj_bias, up_weight, up_bias, down_weight, down_bias, grad_out,
):
    shard = lax.axis_index("shard")
    rep = lax.axis_index("rep")
    info = jnp.stack([counts[0], shard % 4, shard // 4, rep % 2]).astype(jnp.int32)
    block_one = pack(
        pack_one_kernel, "pack_attention_weights", LANES_ONE,
        after(qkv_weight, info), mod_weight, qv_bias, mod_bias, proj_bias, up_bias, down_bias,
    )
    block_two = pack(
        pack_two_kernel, "pack_feed_forward_weights", LANES_TWO,
        up_weight, mod_weight, proj_weight, down_weight,
    )
    mine_one = fetch_all(block_one)
    other_one = swap_all(mine_one)
    mine_two = [move(block_two, fetch(0))]
    block_two = after(block_two, *other_one)
    mine_two += [move(block_two, fetch(k)) for k in (1, 2, 3)]
    weights, bias, mod, qkv, expo, mixed, rinv, hidden = run_forward(
        info, latents, conditions, mine_one + other_one
    )
    mine_two = [after(piece, mod) for piece in mine_two]
    other_two = swap_all(mine_two)
    weights_two, out, grad_mid, grad_mixed, grad_mod_two, keep_two, send_two = run_middle(
        info, latents, conditions, mixed, grad_out, bias, mine_two + other_two
    )
    swapped_two = move(send_two, CORE_SWAP)
    shared = (
        conditions, qkv, expo, mixed, rinv, hidden, grad_mid, grad_mixed, mod, weights,
    )
    grad_latents, acc_qkv, acc_bias, grad_mod = run_backward(0, 1, info, latents, shared)
    held_two = add_blocks(keep_two, after(swapped_two, acc_bias))
    arrived_two = scatter(held_two)
    grad_latents, grad_cond, keep_one, send_one = run_backward(
        1, 3, info, latents, shared,
        (weights_two, grad_mod_two, acc_qkv, acc_bias, after(grad_mod, held_two[0]), grad_latents),
    )
    held_one = add_blocks(keep_one, move(after(send_one, *arrived_two), CORE_SWAP))
    arrived_one = scatter(held_one)
    two = sum_replicas(arrived_two, info)
    one = sum_replicas(arrived_one, info)
    return (out, grad_latents, grad_cond, *finish(info, one + two))


def solution(mesh):
    slots = P(("shard", "rep"), None, None)
    rows = P(("shard", "rep"), None)
    matrix, vector = P("shard", None), P("shard")
    in_specs = (slots, rows, P(("shard", "rep"))) + (matrix, vector) * 5 + (slots,)
    out_specs = (slots, slots, rows) + (matrix, vector) * 5
    return jax.shard_map(
        on_device, mesh=mesh, in_specs=in_specs, out_specs=out_specs, check_vma=False
    )
```

profile of v0, /device:TPU:1, one launch (start us, length us, event | category | flops | bytes accessed | tf_op | source)
XLA Modules:
  0.0 177.5 jit_solution(7551697462546860557)
XLA Ops:
  2.5 5.6 %collective-permute-start.3 = (bf16[48,2048]{1,0:T(8,128)(2,1)S(1)}, bf16[48,2048]{1,0:T(8,128)(2,1)S(1)}, u32[]{:S(2)}, u32[]{:S(2)}) collective-permute-start(bf16[48,2048]{1,0:T(8,128)(2,1)S(1)} %pack_attention_weights.1), channel_id=1, source_target_pairs={{48,0},{115,1},{50,2},{113,3},{52,4},{119,5},{54,6},{117,7},{56,8}... | collective-permute-start | bytes 589832 | tf_op jit(solution)/shard_map/ppermute | solution.py:574
  9.7 4.1 %collective-permute-start.1 = (bf16[48,2048]{1,0:T(8,128)(2,1)S(1)}, bf16[48,2048]{1,0:T(8,128)(2,1)S(1)}, u32[]{:S(2)}, u32[]{:S(2)}) collective-permute-start(bf16[48,2048]{1,0:T(8,128)(2,1)S(1)} %pack_attention_weights.1), channel_id=1, source_target_pairs={{16,0},{83,1},{18,2},{81,3},{20,4},{87,5},{22,6},{85,7},{24,8},{91... | collective-permute-start | bytes 589832 | tf_op jit(solution)/shard_map/ppermute | solution.py:574
  13.8 1.9 %collective-permute-start = (bf16[48,2048]{1,0:T(8,128)(2,1)S(1)}, bf16[48,2048]{1,0:T(8,128)(2,1)S(1)}, u32[]{:S(2)}, u32[]{:S(2)}) collective-permute-start(bf16[48,2048]{1,0:T(8,128)(2,1)S(1)} %pack_attention_weights.1), channel_id=1, source_target_pairs={{0,0},{67,1},{2,2},{65,3},{4,4},{71,5},{6,6},{69,7},{8,8},{75,9},{... | collective-permute-start | bytes 589832 | tf_op jit(solution)/shard_map/ppermute | solution.py:574
  15.8 2.6 %collective-permute-done.2.p2 = bf16[48,2048]{1,0:T(8,128)(2,1)S(1)} collective-permute-done((bf16[48,2048]{1,0:T(8,128)(2,1)S(1)}, bf16[48,2048]{1,0:T(8,128)(2,1)S(1)}, u32[]{:S(2)}, u32[]{:S(2)}) %collective-permute-start.2) | collective-permute-done | bytes 196640 | tf_op jit(solution)/shard_map/ppermute | solution.py:574
  18.4 2.7 %collective-permute-done.1.p1 = bf16[48,2048]{1,0:T(8,128)(2,1)S(1)} collective-permute-done((bf16[48,2048]{1,0:T(8,128)(2,1)S(1)}, bf16[48,2048]{1,0:T(8,128)(2,1)S(1)}, u32[]{:S(2)}, u32[]{:S(2)}) %collective-permute-start.1) | collective-permute-done | bytes 196640 | tf_op jit(solution)/shard_map/ppermute | solution.py:574
  23.7 3.3 %collective-permute-start.8 = (bf16[48,5120]{1,0:T(8,128)(2,1)S(1)}, bf16[48,5120]{1,0:T(8,128)(2,1)S(1)}, u32[]{:S(2)}, u32[]{:S(2)}) collective-permute-start(bf16[48,5120]{1,0:T(8,128)(2,1)S(1)} %pack_feed_forward_weights.1), channel_id=1, source_target_pairs={{0,0},{67,1},{2,2},{65,3},{4,4},{71,5},{6,6},{69,7},{8,8},{75,9},{... | collective-permute-start | bytes 1474568 | tf_op jit(solution)/shard_map/ppermute | solution.py:574
  30.7 3.3 %collective-permute-start.9 = (bf16[48,5120]{1,0:T(8,128)(2,1)S(1)}, bf16[48,5120]{1,0:T(8,128)(2,1)S(1)}, u32[]{:S(2)}, u32[]{:S(2)}) collective-permute-start(bf16[48,5120]{1,0:T(8,128)(2,1)S(1)} %pack_feed_forward_weights.1), channel_id=1, source_target_pairs={{16,0},{83,1},{18,2},{81,3},{20,4},{87,5},{22,6},{85,7},{24,8},{91... | collective-permute-start | bytes 1474568 | tf_op jit(solution)/shard_map/ppermute | solution.py:574
  34.0 4.1 %attention_forward.1 = (bf16[384,2048]{1,0:T(8,128)(2,1)S(1)}, f32[48,128]{1,0:T(8,128)S(1)}, f32[8,768]{1,0:T(8,128)S(1)}, bf16[8,256,1152]{2,1,0:T(8,128)(2,1)...) custom-call(s32[4]{0:T(128)S(1)} %pad_add_fusion.info, ...), custom_call_target="tpu_custom_call" | custom-call | flops 3000000000 | bytes 20000000 | tf_op jit(solution)/shard_map/attention_forward/pallas_call | solution.py:446
  38.3 15.4 %collective-permute-done.11.p3 = bf16[48,5120]{1,0:T(8,128)(2,1)S(1)} collective-permute-done((bf16[48,5120]{1,0:T(8,128)(2,1)S(1)}, bf16[48,5120]{1,0:T(8,128)(2,1)S(1)}, u32[]{:S(2)}, u32[]{:S(2)}) %collective-permute-start.11) | collective-permute-done | bytes 491552 | tf_op jit(solution)/shard_map/ppermute | solution.py:574
  58.6 13.6 %feed_forward_both_ways.1 = (bf16[384,5120]{1,0:T(8,128)(2,1)S(1)}, bf16[8,256,384]{2,1,0:T(8,128)(2,1)}, f32[8,256,384]{2,1,0:T(8,128)S(1)}, bf16[8,256,384]{2,...) custom-call(s32[4]{0:T(128)S(1)} %pad_add_fusion.info, ...), custom_call_target="tpu_custom_call" | custom-call | flops 16000000000 | bytes 30000000 | tf_op jit(solution)/shard_map/feed_forward_both_ways/pallas_call | solution.py:473
  72.3 8.0 %attention_backward_start.1 = (bf16[8,256,384]{2,1,0:T(8,128)(2,1)}, f32[384,1152]{1,0:T(8,128)S(1)}, f32[8,1152]{1,0:T(8,128)S(1)}, f32[8,768]{1,0:T(8,128)S(1)}) custom-call(s32[4]{0:T(128)S(1)} %pad_add_fusion.info, bf16[8,256,384]{2,1,0:T(8,128)(2,1)} %latents.7, bf16[8,384]{1,0:T(8,128)(2,1)} %conditions.7, ...), custom_call_target="tpu_custom_call" | custom-call | flops 2200000000 | bytes 8000000 | tf_op jit(solution)/shard_map/attention_backward_start/pallas_call | solution.py:527
  80.8 28.1 %collective-permute-start.17 = (bf16[48,5120]{1,0:T(8,128)(2,1)S(1)}, bf16[48,5120]{1,0:T(8,128)(2,1)S(1)}, u32[]{:S(2)}, u32[]{:S(2)}) collective-permute-start(bf16[48,5120]{1,0:T(8,128)(2,1)S(1)} %get-tuple-element.92), channel_id=1, source_target_pairs={{0,0},{1,67},{2,2},{3,65},{4,4},{5,71},{6,6},{7,69},{8,8},{9,75},{... | collective-permute-start | bytes 1474568 | tf_op jit(solution)/shard_map/ppermute | solution.py:574
  110.3 3.4 %collective-permute-start.20 = (bf16[48,5120]{1,0:T(8,128)(2,1)S(1)}, bf16[48,5120]{1,0:T(8,128)(2,1)S(1)}, u32[]{:S(2)}, u32[]{:S(2)}) collective-permute-start(bf16[48,5120]{1,0:T(8,128)(2,1)S(1)} %get-tuple-element.101), channel_id=1, source_target_pairs={{0,48},{1,115},{2,50},{3,113},{4,52},{5,119},{6,54},{7,117},{8,56}... | collective-permute-start | bytes 1474568 | tf_op jit(solution)/shard_map/ppermute | solution.py:574
  113.7 4.2 %attention_backward_rest.1 = (bf16[8,256,384]{2,1,0:T(8,128)(2,1)}, bf16[8,384]{1,0:T(8,128)(2,1)}, bf16[192,2048]{1,0:T(8,128)(2,1)S(1)}, bf16[192,2048]{1,0:T(8,128)(2,1)S(1)}) custom-call(s32[4]{0:T(128)S(1)} %pad_add_fusion.info, bf16[8,256,384]{2,1,0:T(8,128)(2,1)} %latents.7, bf16[8,384]{1,0:T(8,128)(2,1)} %conditions.7, ...), custom_call_target="tpu_custom_call", output_to_operand_aliasing={{0}: (17, {})} | custom-call | flops 6600000000 | bytes 24000000 | tf_op jit(solution)/shard_map/attention_backward_rest/pallas_call | solution.py:527
  117.9 17.8 %collective-permute-done.18.refs_1_ = bf16[48,5120]{1,0:T(8,128)(2,1)S(1)} collective-permute-done((bf16[48,5120]{1,0:T(8,128)(2,1)S(1)}, bf16[48,5120]{1,0:T(8,128)(2,1)S(1)}, u32[]{:S(2)}, u32[]{:S(2)}) %collective-permute-start.18) | collective-permute-done | bytes 491552 | tf_op jit(solution)/shard_map/ppermute | solution.py:574
  139.8 1.9 %collective-permute-start.22 = (bf16[48,2048]{1,0:T(8,128)(2,1)S(1)}, bf16[48,2048]{1,0:T(8,128)(2,1)S(1)}, u32[]{:S(2)}, u32[]{:S(2)}) collective-permute-start(bf16[48,2048]{1,0:T(8,128)(2,1)S(1)} %get-tuple-element.103), channel_id=1, source_target_pairs={{0,0},{1,67},{2,2},{3,65},{4,4},{5,71},{6,6},{7,69},{8,8},{9,75},{... | collective-permute-start | bytes 589832 | tf_op jit(solution)/shard_map/ppermute | solution.py:574
  141.8 2.8 %collective-permute-start.24 = (bf16[48,2048]{1,0:T(8,128)(2,1)S(1)}, bf16[48,2048]{1,0:T(8,128)(2,1)S(1)}, u32[]{:S(2)}, u32[]{:S(2)}) collective-permute-start(bf16[48,2048]{1,0:T(8,128)(2,1)S(1)} %get-tuple-element.105), channel_id=1, source_target_pairs={{0,32},{1,99},{2,34},{3,97},{4,36},{5,103},{6,38},{7,101},{8,40},{... | collective-permute-start | bytes 589832 | tf_op jit(solution)/shard_map/ppermute | solution.py:574
  144.6 2.3 %collective-permute-start.25 = (bf16[48,2048]{1,0:T(8,128)(2,1)S(1)}, bf16[48,2048]{1,0:T(8,128)(2,1)S(1)}, u32[]{:S(2)}, u32[]{:S(2)}) collective-permute-start(bf16[48,2048]{1,0:T(8,128)(2,1)S(1)} %get-tuple-element.106), channel_id=1, source_target_pairs={{0,48},{1,115},{2,50},{3,113},{4,52},{5,119},{6,54},{7,117},{8,56}... | collective-permute-start | bytes 589832 | tf_op jit(solution)/shard_map/ppermute | solution.py:574
  148.2 3.8 %collective-permute-start.35 = (bf16[48,2560]{1,0:T(8,128)(2,1)S(1)}, bf16[48,2560]{1,0:T(8,128)(2,1)S(1)}, u32[]{:S(2)}, u32[]{:S(2)}) collective-permute-start(bf16[48,2560]{1,0:T(8,128)(2,1)S(1)} %add.26.refs_0_), channel_id=1, source_target_pairs={{0,8},{1,9},{2,10},{3,11},{4,12},{5,13},{6,14},{7,15},{8,0},{9,1},... | collective-permute-start | bytes 737288 | tf_op jit(solution)/shard_map/ppermute | solution.py:574
  152.8 2.2 %collective-permute-done.25.refs_3_ = bf16[48,2048]{1,0:T(8,128)(2,1)S(1)} collective-permute-done((bf16[48,2048]{1,0:T(8,128)(2,1)S(1)}, bf16[48,2048]{1,0:T(8,128)(2,1)S(1)}, u32[]{:S(2)}, u32[]{:S(2)}) %collective-permute-start.25) | collective-permute-done | bytes 196640 | tf_op jit(solution)/shard_map/ppermute | solution.py:574
  158.2 5.1 %collective-permute-done.34.refs_1_ = bf16[48,2560]{1,0:T(8,128)(2,1)S(1)} collective-permute-done((bf16[48,2560]{1,0:T(8,128)(2,1)S(1)}, bf16[48,2560]{1,0:T(8,128)(2,1)S(1)}, u32[]{:S(2)}, u32[]{:S(2)}) %collective-permute-start.34) | collective-permute-done | bytes 245792 | tf_op jit(solution)/shard_map/ppermute | solution.py:574
  164.1 3.2 %collective-permute-start.29 = (bf16[48,1024]{1,0:T(8,128)(2,1)S(1)}, bf16[48,1024]{1,0:T(8,128)(2,1)S(1)}, u32[]{:S(2)}, u32[]{:S(2)}) collective-permute-start(bf16[48,1024]{1,0:T(8,128)(2,1)S(1)} %add.23.refs_0_), channel_id=1, source_target_pairs={{0,8},{1,9},{2,10},{3,11},{4,12},{5,13},{6,14},{7,15},{8,0},{9,1},... | collective-permute-start | bytes 294920 | tf_op jit(solution)/shard_map/ppermute | solution.py:574
  169.3 2.9 %collective-permute-done.28.refs_1_ = bf16[48,1024]{1,0:T(8,128)(2,1)S(1)} collective-permute-done((bf16[48,1024]{1,0:T(8,128)(2,1)S(1)}, bf16[48,1024]{1,0:T(8,128)(2,1)S(1)}, u32[]{:S(2)}, u32[]{:S(2)}) %collective-permute-start.28) | collective-permute-done | bytes 98336 | tf_op jit(solution)/shard_map/ppermute | solution.py:574
  172.3 2.5 %collective-permute-start.31 = (bf16[48,1024]{1,0:T(8,128)(2,1)S(1)}, bf16[48,1024]{1,0:T(8,128)(2,1)S(1)}, u32[]{:S(2)}, u32[]{:S(2)}) collective-permute-start(bf16[48,1024]{1,0:T(8,128)(2,1)S(1)} %add.24.one_a), channel_id=1, source_target_pairs={{0,1},{1,0},{2,3},{3,2},{4,5},{5,4},{6,7},{7,6},{8,9},{9,8},{10,11... | collective-permute-start | bytes 294920 | tf_op jit(solution)/shard_map/ppermute | solution.py:574
  (74 shorter events, 31.2 us)
Async XLA Ops:
  2.5 13.2 %collective-permute-start.3 = (bf16[48,2048]{1,0:T(8,128)(2,1)S(1)}, bf16[48,2048]{1,0:T(8,128)(2,1)S(1)}, u32[]{:S(2)}, u32[]{:S(2)}) collective-permute-start(bf16[48,2048]{1,0:T(8,128)(2,1)S(1)} %pack_attention_weights.1), channel_id=1, source_target_pairs={{48,0},{115,1},{50,2},{113,3},{52,4},{119,5},{54,6},{117,7},{56,8}... | collective-permute-start | bytes 589832 | tf_op jit(solution)/shard_map/ppermute | solution.py:574
  8.1 10.3 %collective-permute-start.2 = (bf16[48,2048]{1,0:T(8,128)(2,1)S(1)}, bf16[48,2048]{1,0:T(8,128)(2,1)S(1)}, u32[]{:S(2)}, u32[]{:S(2)}) collective-permute-start(bf16[48,2048]{1,0:T(8,128)(2,1)S(1)} %pack_attention_weights.1), channel_id=1, source_target_pairs={{32,0},{99,1},{34,2},{97,3},{36,4},{103,5},{38,6},{101,7},{40,8},{... | collective-permute-start | bytes 589832 | tf_op jit(solution)/shard_map/ppermute | solution.py:574
  9.7 11.4 %collective-permute-start.1 = (bf16[48,2048]{1,0:T(8,128)(2,1)S(1)}, bf16[48,2048]{1,0:T(8,128)(2,1)S(1)}, u32[]{:S(2)}, u32[]{:S(2)}) collective-permute-start(bf16[48,2048]{1,0:T(8,128)(2,1)S(1)} %pack_attention_weights.1), channel_id=1, source_target_pairs={{16,0},{83,1},{18,2},{81,3},{20,4},{87,5},{22,6},{85,7},{24,8},{91... | collective-permute-start | bytes 589832 | tf_op jit(solution)/shard_map/ppermute | solution.py:574
  13.8 8.8 %collective-permute-start = (bf16[48,2048]{1,0:T(8,128)(2,1)S(1)}, bf16[48,2048]{1,0:T(8,128)(2,1)S(1)}, u32[]{:S(2)}, u32[]{:S(2)}) collective-permute-start(bf16[48,2048]{1,0:T(8,128)(2,1)S(1)} %pack_attention_weights.1), channel_id=1, source_target_pairs={{0,0},{67,1},{2,2},{65,3},{4,4},{71,5},{6,6},{69,7},{8,8},{75,9},{... | collective-permute-start | bytes 589832 | tf_op jit(solution)/shard_map/ppermute | solution.py:574
  15.7 11.3 %collective-permute-start.7 = (bf16[48,2048]{1,0:T(8,128)(2,1)S(1)}, bf16[48,2048]{1,0:T(8,128)(2,1)S(1)}, u32[]{:S(2)}, u32[]{:S(2)}) collective-permute-start(bf16[48,2048]{1,0:T(8,128)(2,1)S(1)} %collective-permute-done.3.p3), channel_id=1, source_target_pairs={{0,1},{1,0},{2,3},{3,2},{4,5},{5,4},{6,7},{7,6},{8,9},{9,8},{10,11... | collective-permute-start | bytes 589832 | tf_op jit(solution)/shard_map/ppermute | solution.py:574
  18.4 8.7 %collective-permute-start.6 = (bf16[48,2048]{1,0:T(8,128)(2,1)S(1)}, bf16[48,2048]{1,0:T(8,128)(2,1)S(1)}, u32[]{:S(2)}, u32[]{:S(2)}) collective-permute-start(bf16[48,2048]{1,0:T(8,128)(2,1)S(1)} %collective-permute-done.2.p2), channel_id=1, source_target_pairs={{0,1},{1,0},{2,3},{3,2},{4,5},{5,4},{6,7},{7,6},{8,9},{9,8},{10,11... | collective-permute-start | bytes 589832 | tf_op jit(solution)/shard_map/ppermute | solution.py:574
  23.7 14.5 %collective-permute-start.8 = (bf16[48,5120]{1,0:T(8,128)(2,1)S(1)}, bf16[48,5120]{1,0:T(8,128)(2,1)S(1)}, u32[]{:S(2)}, u32[]{:S(2)}) collective-permute-start(bf16[48,5120]{1,0:T(8,128)(2,1)S(1)} %pack_feed_forward_weights.1), channel_id=1, source_target_pairs={{0,0},{67,1},{2,2},{65,3},{4,4},{71,5},{6,6},{69,7},{8,8},{75,9},{... | collective-permute-start | bytes 1474568 | tf_op jit(solution)/shard_map/ppermute | solution.py:574
  27.0 26.6 %collective-permute-start.11 = (bf16[48,5120]{1,0:T(8,128)(2,1)S(1)}, bf16[48,5120]{1,0:T(8,128)(2,1)S(1)}, u32[]{:S(2)}, u32[]{:S(2)}) collective-permute-start(bf16[48,5120]{1,0:T(8,128)(2,1)S(1)} %pack_feed_forward_weights.1), channel_id=1, source_target_pairs={{48,0},{115,1},{50,2},{113,3},{52,4},{119,5},{54,6},{117,7},{56,8}... | collective-permute-start | bytes 1474568 | tf_op jit(solution)/shard_map/ppermute | solution.py:574
  28.9 24.7 %collective-permute-start.10 = (bf16[48,5120]{1,0:T(8,128)(2,1)S(1)}, bf16[48,5120]{1,0:T(8,128)(2,1)S(1)}, u32[]{:S(2)}, u32[]{:S(2)}) collective-permute-start(bf16[48,5120]{1,0:T(8,128)(2,1)S(1)} %pack_feed_forward_weights.1), channel_id=1, source_target_pairs={{32,0},{99,1},{34,2},{97,3},{36,4},{103,5},{38,6},{101,7},{40,8},{... | collective-permute-start | bytes 1474568 | tf_op jit(solution)/shard_map/ppermute | solution.py:574
  30.7 24.6 %collective-permute-start.9 = (bf16[48,5120]{1,0:T(8,128)(2,1)S(1)}, bf16[48,5120]{1,0:T(8,128)(2,1)S(1)}, u32[]{:S(2)}, u32[]{:S(2)}) collective-permute-start(bf16[48,5120]{1,0:T(8,128)(2,1)S(1)} %pack_feed_forward_weights.1), channel_id=1, source_target_pairs={{16,0},{83,1},{18,2},{81,3},{20,4},{87,5},{22,6},{85,7},{24,8},{91... | collective-permute-start | bytes 1474568 | tf_op jit(solution)/shard_map/ppermute | solution.py:574
  38.2 17.7 %collective-permute-start.12 = (bf16[48,5120]{1,0:T(8,128)(2,1)S(1)}, bf16[48,5120]{1,0:T(8,128)(2,1)S(1)}, u32[]{:S(2)}, u32[]{:S(2)}) collective-permute-start(bf16[48,5120]{1,0:T(8,128)(2,1)S(1)} %collective-permute-done.8.p0), channel_id=1, source_target_pairs={{0,1},{1,0},{2,3},{3,2},{4,5},{5,4},{6,7},{7,6},{8,9},{9,8},{10,11... | collective-permute-start | bytes 1474568 | tf_op jit(solution)/shard_map/ppermute | solution.py:574
  72.2 8.1 %collective-permute-start.16 = (bf16[192,5120]{1,0:T(8,128)(2,1)S(1)}, bf16[192,5120]{1,0:T(8,128)(2,1)S(1)}, u32[]{:S(2)}, u32[]{:S(2)}) collective-permute-start(bf16[192,5120]{1,0:T(8,128)(2,1)S(1)} %get-tuple-element.90), channel_id=1, source_target_pairs={{0,1},{1,0},{2,3},{3,2},{4,5},{5,4},{6,7},{7,6},{8,9},{9,8},{10,11... | collective-permute-start | bytes 5898248 | tf_op jit(solution)/shard_map/ppermute | solution.py:574
  80.8 56.0 %collective-permute-start.17 = (bf16[48,5120]{1,0:T(8,128)(2,1)S(1)}, bf16[48,5120]{1,0:T(8,128)(2,1)S(1)}, u32[]{:S(2)}, u32[]{:S(2)}) collective-permute-start(bf16[48,5120]{1,0:T(8,128)(2,1)S(1)} %get-tuple-element.92), channel_id=1, source_target_pairs={{0,0},{1,67},{2,2},{3,65},{4,4},{5,71},{6,6},{7,69},{8,8},{9,75},{... | collective-permute-start | bytes 1474568 | tf_op jit(solution)/shard_map/ppermute | solution.py:574
  108.8 26.8 %collective-permute-start.18 = (bf16[48,5120]{1,0:T(8,128)(2,1)S(1)}, bf16[48,5120]{1,0:T(8,128)(2,1)S(1)}, u32[]{:S(2)}, u32[]{:S(2)}) collective-permute-start(bf16[48,5120]{1,0:T(8,128)(2,1)S(1)} %get-tuple-element.99), channel_id=1, source_target_pairs={{0,16},{1,83},{2,18},{3,81},{4,20},{5,87},{6,22},{7,85},{8,24},{9,... | collective-permute-start | bytes 1474568 | tf_op jit(solution)/shard_map/ppermute | solution.py:574
  108.9 26.8 %collective-permute-start.19 = (bf16[48,5120]{1,0:T(8,128)(2,1)S(1)}, bf16[48,5120]{1,0:T(8,128)(2,1)S(1)}, u32[]{:S(2)}, u32[]{:S(2)}) collective-permute-start(bf16[48,5120]{1,0:T(8,128)(2,1)S(1)} %get-tuple-element.100), channel_id=1, source_target_pairs={{0,32},{1,99},{2,34},{3,97},{4,36},{5,103},{6,38},{7,101},{8,40},{... | collective-permute-start | bytes 1474568 | tf_op jit(solution)/shard_map/ppermute | solution.py:574
  110.3 26.5 %collective-permute-start.20 = (bf16[48,5120]{1,0:T(8,128)(2,1)S(1)}, bf16[48,5120]{1,0:T(8,128)(2,1)S(1)}, u32[]{:S(2)}, u32[]{:S(2)}) collective-permute-start(bf16[48,5120]{1,0:T(8,128)(2,1)S(1)} %get-tuple-element.101), channel_id=1, source_target_pairs={{0,48},{1,115},{2,50},{3,113},{4,52},{5,119},{6,54},{7,117},{8,56}... | collective-permute-start | bytes 1474568 | tf_op jit(solution)/shard_map/ppermute | solution.py:574
  139.8 8.5 %collective-permute-start.22 = (bf16[48,2048]{1,0:T(8,128)(2,1)S(1)}, bf16[48,2048]{1,0:T(8,128)(2,1)S(1)}, u32[]{:S(2)}, u32[]{:S(2)}) collective-permute-start(bf16[48,2048]{1,0:T(8,128)(2,1)S(1)} %get-tuple-element.103), channel_id=1, source_target_pairs={{0,0},{1,67},{2,2},{3,65},{4,4},{5,71},{6,6},{7,69},{8,8},{9,75},{... | collective-permute-start | bytes 589832 | tf_op jit(solution)/shard_map/ppermute | solution.py:574
  141.7 10.7 %collective-permute-start.23 = (bf16[48,2048]{1,0:T(8,128)(2,1)S(1)}, bf16[48,2048]{1,0:T(8,128)(2,1)S(1)}, u32[]{:S(2)}, u32[]{:S(2)}) collective-permute-start(bf16[48,2048]{1,0:T(8,128)(2,1)S(1)} %get-tuple-element.104), channel_id=1, source_target_pairs={{0,16},{1,83},{2,18},{3,81},{4,20},{5,87},{6,22},{7,85},{8,24},{9,... | collective-permute-start | bytes 589832 | tf_op jit(solution)/shard_map/ppermute | solution.py:574
  141.8 11.0 %collective-permute-start.24 = (bf16[48,2048]{1,0:T(8,128)(2,1)S(1)}, bf16[48,2048]{1,0:T(8,128)(2,1)S(1)}, u32[]{:S(2)}, u32[]{:S(2)}) collective-permute-start(bf16[48,2048]{1,0:T(8,128)(2,1)S(1)} %get-tuple-element.105), channel_id=1, source_target_pairs={{0,32},{1,99},{2,34},{3,97},{4,36},{5,103},{6,38},{7,101},{8,40},{... | collective-permute-start | bytes 589832 | tf_op jit(solution)/shard_map/ppermute | solution.py:574
  144.6 10.5 %collective-permute-start.25 = (bf16[48,2048]{1,0:T(8,128)(2,1)S(1)}, bf16[48,2048]{1,0:T(8,128)(2,1)S(1)}, u32[]{:S(2)}, u32[]{:S(2)}) collective-permute-start(bf16[48,2048]{1,0:T(8,128)(2,1)S(1)} %get-tuple-element.106), channel_id=1, source_target_pairs={{0,48},{1,115},{2,50},{3,113},{4,52},{5,119},{6,54},{7,117},{8,56}... | collective-permute-start | bytes 589832 | tf_op jit(solution)/shard_map/ppermute | solution.py:574
  146.9 11.1 %collective-permute-start.36 = (bf16[48,2560]{1,0:T(8,128)(2,1)S(1)}, bf16[48,2560]{1,0:T(8,128)(2,1)S(1)}, u32[]{:S(2)}, u32[]{:S(2)}) collective-permute-start(bf16[48,2560]{1,0:T(8,128)(2,1)S(1)} %add.26.refs_0_), channel_id=1, source_target_pairs={{0,12},{1,13},{2,14},{3,15},{4,0},{5,1},{6,2},{7,3},{8,4},{9,5},{1... | collective-permute-start | bytes 737288 | tf_op jit(solution)/shard_map/ppermute | solution.py:574
  148.2 9.9 %collective-permute-start.35 = (bf16[48,2560]{1,0:T(8,128)(2,1)S(1)}, bf16[48,2560]{1,0:T(8,128)(2,1)S(1)}, u32[]{:S(2)}, u32[]{:S(2)}) collective-permute-start(bf16[48,2560]{1,0:T(8,128)(2,1)S(1)} %add.26.refs_0_), channel_id=1, source_target_pairs={{0,8},{1,9},{2,10},{3,11},{4,12},{5,13},{6,14},{7,15},{8,0},{9,1},... | collective-permute-start | bytes 737288 | tf_op jit(solution)/shard_map/ppermute | solution.py:574
  152.4 10.9 %collective-permute-start.34 = (bf16[48,2560]{1,0:T(8,128)(2,1)S(1)}, bf16[48,2560]{1,0:T(8,128)(2,1)S(1)}, u32[]{:S(2)}, u32[]{:S(2)}) collective-permute-start(bf16[48,2560]{1,0:T(8,128)(2,1)S(1)} %add.26.refs_0_), channel_id=1, source_target_pairs={{0,4},{1,5},{2,6},{3,7},{4,8},{5,9},{6,10},{7,11},{8,12},{9,13},{1... | collective-permute-start | bytes 737288 | tf_op jit(solution)/shard_map/ppermute | solution.py:574
  163.5 11.4 %collective-permute-start.37 = (bf16[48,2560]{1,0:T(8,128)(2,1)S(1)}, bf16[48,2560]{1,0:T(8,128)(2,1)S(1)}, u32[]{:S(2)}, u32[]{:S(2)}) collective-permute-start(bf16[48,2560]{1,0:T(8,128)(2,1)S(1)} %add.27.two_a), channel_id=1, source_target_pairs={{0,1},{1,0},{2,3},{3,2},{4,5},{5,4},{6,7},{7,6},{8,9},{9,8},{10,11... | collective-permute-start | bytes 737288 | tf_op jit(solution)/shard_map/ppermute | solution.py:574
  (16 other events, 96.8 us)
where the time goes:
time: 178 us
  starting transfers between devices  78.2 us (44%)
  waiting for transfers between devices  61.4 us (34%)
  Pallas kernels  36.3 us (20%)
    ppermute x38, starting transfers between devices, move(): return lax.ppermute(value, BOTH, pairs)  78.2 us
    ppermute x38, waiting for transfers between devices, move(): return lax.ppermute(value, BOTH, pairs)  61.4 us
    pallas_call x1, Pallas kernels, run_middle(): pl.pallas_call(middle_kernel, grid_spec=pltpu.PrefetchScalarGridSpec(num_...  13.6 us
    pallas_call x2, Pallas kernels, run_backward(): pl.pallas_call(functools.partial(backward_kernel, first, last), grid_spec...  12.2 us
    pallas_call x1, Pallas kernels, run_forward(): pl.pallas_call(forward_kernel, grid_spec=pltpu.PrefetchScalarGridSpec(num...  4.12 us
  transfers between devices with their start and end apart: 38, of which 19 were waited for; matrix products, arithmetic and copies ran while one was open for 0% of the time, Pallas kernels for 11%

commit v1 on v0

--- a/solution.py
+++ b/solution.py
@@ -14,6 +14,7 @@
 TOK = 256
 CAP = 8
 PAIR = 2
+CHUNK = 768
 STEPS = CAP // PAIR
 TWIN = 128
 BF = jnp.bfloat16
@@ -84,6 +85,11 @@
     full = jnp.concatenate(full, axis=1)
     cut = [full[:, 128 * i : 128 * i + 128] for i in range(45)]
     return jnp.concatenate(cut + [jnp.zeros((3, 128), F32)], axis=0)
+
+
+def by_head(value, low):
+    zero = jnp.zeros_like(value)
+    return jnp.concatenate([jnp.where(low, value, zero), jnp.where(low, zero, value)], axis=0)
 
 
 def bias_row(bias, first, count):
@@ -137,7 +143,6 @@
         qkv_all = dot(jnp.concatenate(hidden, axis=0), weights[:, :QKV_W])
         qkv_all = (qkv_all + full_bias).astype(BF)
         low = lax.broadcasted_iota(jnp.int32, (TOK, 128), 1) < HEAD_DIM
-        ones = jnp.ones((TOK, 128), BF)
         for i in range(PAIR):
             slot = PAIR * step + i
             qkv = qkv_all[TOK * i : TOK * i + TOK]
@@ -145,27 +150,27 @@
             for pair in range(HEADS // 2):
                 at = 128 * pair
                 query = qkv[:, at : at + 128] * jnp.asarray(HEAD_DIM**-0.5, BF)
-                key = qkv[:, D + at : D + at + 128]
-                value = jnp.concatenate([qkv[:, 2 * D + at : 2 * D + at + 128], ones], axis=1)
-                parts = []
-                for half in range(2):
-                    chosen = jnp.where(low if half == 0 else ~low, query, jnp.zeros_like(query))
-                    scores = dot_nt(chosen, key)
-                    expo = jnp.exp(scores - jnp.max(scores, axis=-1, keepdims=True)).astype(BF)
-                    expo_out[slot, 2 * pair + half] = expo
-                    parts.append(dot(expo, value))
-                total = jnp.where(low, parts[0][:, 128:], parts[1][:, 128:])
-                inverse = 1.0 / total
+                value = qkv[:, 2 * D + at : 2 * D + at + 128]
+                scores = dot_nt(query, by_head(qkv[:, D + at : D + at + 128], low))
+                expo = jnp.concatenate(
+                    [
+                        jnp.exp(part - jnp.max(part, axis=-1, keepdims=True)).astype(BF)
+                        for part in (scores[:, :TOK], scores[:, TOK:])
+                    ],
+                    axis=1,
+                )
+                expo_out[slot, pair] = expo
+                sums = by_head(jnp.ones((TOK, 128), BF), low)
+                both = dot(expo, jnp.concatenate([by_head(value, low), sums], axis=1))
+                inverse = 1.0 / both[:, 128:]
                 rinv_out[slot, :, at : at + 128] = inverse
-                mixed_out[slot, :, at : at + 128] = (
-                    jnp.where(low, parts[0][:, :128], parts[1][:, :128]) * inverse
-                ).astype(BF)
+                mixed_out[slot, :, at : at + 128] = (both[:, :128] * inverse).astype(BF)
 
 
 def middle_kernel(
     info, latents, conditions, mixed_in, grad_out, bias_in, p0, p1, p2, p3, p4, p5, p6, p7,
     weights, out, grad_mid_out, grad_mixed_out, grad_mod, keep, send,
-    mod, acc_up, acc_down, acc_proj, acc_bias,
+    mod, acc_up, acc_down, acc_proj, acc_bias, down,
 ):
     step = pl.program_id(0)
 
@@ -176,6 +181,12 @@
         mod[...] = dot(cond_low, weights[:, AT_MOD : AT_MOD + MOD_TWO]) + bias_row(
             bias_in[...], ROW_MOD + 6, 12
         )
+        for owner in range(8):
+            for q in range(4):
+                at = 192 * owner + 48 * q
+                down[at : at + 48, :] = weights[
+                    48 * owner : 48 * owner + 48, AT_DOWN + D * q : AT_DOWN + D * q + D
+                ]
         acc_up[...] = jnp.zeros_like(acc_up)
         acc_down[...] = jnp.zeros_like(acc_down)
         acc_proj[...] = jnp.zeros_like(acc_proj)
@@ -212,18 +223,11 @@
         d_hidden = jnp.zeros((PAIR * TOK, D), F32)
         root = 0.7978845608028654
         cube = root * 0.044715
-        for chunk in range(4):
-            at = D * chunk
-            w_up = weights[:, at : at + D]
-            w_down = jnp.concatenate(
-                [
-                    weights[48 * s : 48 * s + 48, AT_DOWN + D * q : AT_DOWN + D * q + D]
-                    for s in (2 * chunk, 2 * chunk + 1)
-                    for q in range(4)
-                ],
-                axis=0,
-            )
-            upward = dot(hidden, w_up) + up_bias[:, at : at + D]
+        for chunk in range(FF // CHUNK):
+            at = CHUNK * chunk
+            w_up = weights[:, at : at + CHUNK]
+            w_down = down[at : at + CHUNK, :]
+            upward = dot(hidden, w_up) + up_bias[:, at : at + CHUNK]
             square = upward * upward
             bend = jnp.tanh(upward * (root + cube * square))
             half = 0.5 + 0.5 * bend
@@ -231,10 +235,10 @@
             slope = half + act * (1.0 - bend) * (root + (3.0 * cube) * square)
             act_low = act.astype(BF)
             branch_two = branch_two + dot(act_low, w_down)
-            acc_down[at : at + D, :] += dot_tn(act_low, g_two)
+            acc_down[at : at + CHUNK, :] += dot_tn(act_low, g_two)
             g_up = (slope * dot_nt(g_two, w_down)).astype(BF)
-            acc_up[:, at : at + D] += dot_tn(hidden, g_up)
-            acc_bias[0:1, at : at + D] += jnp.sum(g_up.astype(F32), axis=0, keepdims=True)
+            acc_up[:, at : at + CHUNK] += dot_tn(hidden, g_up)
+            acc_bias[0:1, at : at + CHUNK] += jnp.sum(g_up.astype(F32), axis=0, keepdims=True)
             d_hidden = d_hidden + dot_nt(g_up, w_up)
         acc_bias[1:2, :D] += jnp.sum(g_two.astype(F32), axis=0, keepdims=True)
         g_one = []
@@ -340,24 +344,25 @@
             for pair in range(HEADS // 2):
                 at = 128 * pair
                 query = qkv[:, at : at + 128]
-                key = qkv[:, D + at : D + at + 128]
-                value = qkv[:, 2 * D + at : 2 * D + at + 128]
+                key = by_head(qkv[:, D + at : D + at + 128], low)
+                value = by_head(qkv[:, 2 * D + at : 2 * D + at + 128], low)
                 grad = scaled[:, at : at + 128]
                 weighed = product[:, at : at + 128]
-                parts = []
+                expo = expo_in[slot + i, pair]
+                g_probs = dot_nt(grad, value)
+                g_scores = []
                 for half in range(2):
                     mask = low if half == 0 else ~low
-                    chosen = jnp.where(mask, grad, jnp.zeros_like(grad))
                     delta = jnp.sum(jnp.where(mask, weighed, 0.0), axis=-1, keepdims=True)
-                    expo = expo_in[slot + i, 2 * pair + half]
-                    g_probs = dot_nt(chosen, value)
-                    g_scores = (expo.astype(F32) * (g_probs - delta)).astype(BF)
-                    parts.append(
-                        (dot(g_scores, key), dot_tn(g_scores, query), dot_tn(expo, grad))
+                    lanes = slice(TOK * half, TOK * half + TOK)
+                    g_scores.append(
+                        (expo[:, lanes].astype(F32) * (g_probs[:, lanes] - delta)).astype(BF)
                     )
-                g_query.append((jnp.where(low, parts[0][0], parts[1][0]) * factor).astype(BF))
-                g_key.append((jnp.where(low, parts[0][1], parts[1][1]) * factor).astype(BF))
-                g_value.append(jnp.where(low, parts[0][2], parts[1][2]).astype(BF))
+                g_scores = jnp.concatenate(g_scores, axis=1)
+                d_key, d_value = dot_tn(g_scores, query), dot_tn(expo, grad)
+                g_query.append((dot(g_scores, key) * factor).astype(BF))
+                g_key.append((jnp.where(low, d_key[:TOK], d_key[TOK:]) * factor).astype(BF))
+                g_value.append(jnp.where(low, d_value[:TOK], d_value[TOK:]).astype(BF))
             g_all.append(jnp.concatenate(g_query + g_key + g_value, axis=1))
         g_qkv = jnp.concatenate(g_all, axis=0)
         hidden = hidden_in[pl.ds(slot, PAIR)].reshape(PAIR * TOK, D)
@@ -456,12 +461,12 @@
             pltpu.VMEM((48, 128), F32),
             pltpu.VMEM((CAP, MOD_ONE), F32),
             pltpu.VMEM((CAP, TOK, QKV_W), BF),
-            pltpu.VMEM((CAP, HEADS, TOK, TOK), BF),
+            pltpu.VMEM((CAP, HEADS // 2, TOK, 2 * TOK), BF),
             pltpu.VMEM((CAP, TOK, D), BF),
             pltpu.VMEM((CAP, TOK, D), F32),
             pltpu.VMEM((CAP, TOK, D), BF),
         ],
-        compiler_params=params(13),
+        compiler_params=params(10),
         name="attention_forward",
         cost_estimate=pl.CostEstimate(
             flops=3_000_000_000, bytes_accessed=20_000_000, transcendentals=3_000_000
@@ -490,6 +495,7 @@
                 pltpu.VMEM((FF, D), F32),
                 pltpu.VMEM((D, D), F32),
                 pltpu.VMEM((8, FF), F32),
+                pltpu.VMEM((FF, D), BF),
             ],
         ),
         out_shape=[
@@ -501,7 +507,7 @@
             pltpu.VMEM((192, LANES_TWO), BF),
             pltpu.VMEM((192, LANES_TWO), BF),
         ],
-        compiler_params=params(22),
+        compiler_params=params(23),
         name="feed_forward_both_ways",
         cost_estimate=pl.CostEstimate(
             flops=16_000_000_000, bytes_accessed=30_000_000, transcendentals=3_000_000
@@ -535,7 +541,7 @@
         ),
         out_shape=out_shape,
         input_output_aliases={17: 0} if last else {},
-        compiler_params=params(15),
+        compiler_params=params(10),
         name="attention_backward_rest" if last else "attention_backward_start",
         cost_estimate=pl.CostEstimate(
             flops=2_200_000_000 * count, bytes_accessed=8_000_000 * count, transcendentals=1_000
@@ -755,9 +761,9 @@
         up_weight, mod_weight, proj_weight, down_weight,
     )
     mine_one = fetch_all(block_one)
-    other_one = swap_all(mine_one)
     mine_two = [move(block_two, fetch(0))]
-    block_two = after(block_two, *other_one)
+    other_one = swap_all([mine_one[0]] + [after(piece, block_two) for piece in mine_one[1:]])
+    block_two = after(block_two, *mine_one)
     mine_two += [move(block_two, fetch(k)) for k in (1, 2, 3)]
     weights, bias, mod, qkv, expo, mixed, rinv, hidden = run_forward(
         info, latents, conditions, mine_one + other_one

time: 178 us -> 169 us (0.949)
  Pallas kernels: 36.3 us -> 73 us
  starting transfers between devices: 78.2 us -> 48 us
  waiting for transfers between devices: 61.4 us -> 46.4 us
    ppermute x38, starting transfers between devices: 78.2 us -> 48 us  [move(): return lax.ppermute(value, BOTH, pairs)]
    pallas_call x1, Pallas kernels: 13.6 us -> 32.3 us  [run_middle(): pl.pallas_call(middle_kernel, grid_spec=pltpu.PrefetchScalarGridSpec(num_...]
    ppermute x38, waiting for transfers between devices: 61.4 us -> 46.4 us  [move(): return lax.ppermute(value, BOTH, pairs)]
    pallas_call x2, Pallas kernels: 12.2 us -> 23.8 us  [run_backward(): pl.pallas_call(functools.partial(backward_kernel, first, last), grid_spec...]
    pallas_call x1, Pallas kernels: 4.12 us -> 10.5 us  [run_forward(): pl.pallas_call(forward_kernel, grid_spec=pltpu.PrefetchScalarGridSpec(num...]
  transfers between devices with their start and end apart: 38 -> 38, of which waited for: 19 -> 20; matrix products, arithmetic and copies ran while one was open for 0% -> 0% of each run, Pallas kernels for 11% -> 22%
where the time goes in v1:
time: 169 us
  Pallas kernels  73 us (43%)
  starting transfers between devices  48 us (28%)
  waiting for transfers between devices  46.4 us (27%)
    ppermute x38, starting transfers between devices, move(): return lax.ppermute(value, BOTH, pairs)  48 us
    ppermute x38, waiting for transfers between devices, move(): return lax.ppermute(value, BOTH, pairs)  46.4 us
    pallas_call x1, Pallas kernels, run_middle(): pl.pallas_call(middle_kernel, grid_spec=pltpu.PrefetchScalarGridSpec(num_...  32.3 us
    pallas_call x2, Pallas kernels, run_backward(): pl.pallas_call(functools.partial(backward_kernel, first, last), grid_spec...  23.8 us
    pallas_call x1, Pallas kernels, run_forward(): pl.pallas_call(forward_kernel, grid_spec=pltpu.PrefetchScalarGridSpec(num...  10.5 us
  transfers between devices with their start and end apart: 38, of which 20 were waited for; matrix products, arithmetic and copies ran while one was open for 0% of the time, Pallas kernels for 22%

profile of v1, /device:TPU:1, one launch (start us, length us, event | category | flops | bytes accessed | tf_op | source)
XLA Modules:
  0.0 169.0 jit_solution(6483142633401585473)
XLA Ops:
  2.5 6.5 %collective-permute-start = (bf16[48,2048]{1,0:T(8,128)(2,1)S(1)}, bf16[48,2048]{1,0:T(8,128)(2,1)S(1)}, u32[]{:S(2)}, u32[]{:S(2)}) collective-permute-start(bf16[48,2048]{1,0:T(8,128)(2,1)S(1)} %pack_attention_weights.1), channel_id=1, source_target_pairs={{0,0},{67,1},{2,2},{65,3},{4,4},{71,5},{6,6},{69,7},{8,8},{75,9},{... | collective-permute-start | bytes 589832 | tf_op jit(solution)/shard_map/ppermute | solution.py:580
  9.0 2.3 %collective-permute-start.1 = (bf16[48,2048]{1,0:T(8,128)(2,1)S(1)}, bf16[48,2048]{1,0:T(8,128)(2,1)S(1)}, u32[]{:S(2)}, u32[]{:S(2)}) collective-permute-start(bf16[48,2048]{1,0:T(8,128)(2,1)S(1)} %pack_attention_weights.1), channel_id=1, source_target_pairs={{16,0},{83,1},{18,2},{81,3},{20,4},{87,5},{22,6},{85,7},{24,8},{91... | collective-permute-start | bytes 589832 | tf_op jit(solution)/shard_map/ppermute | solution.py:580
  11.2 2.9 %collective-permute-start.2 = (bf16[48,2048]{1,0:T(8,128)(2,1)S(1)}, bf16[48,2048]{1,0:T(8,128)(2,1)S(1)}, u32[]{:S(2)}, u32[]{:S(2)}) collective-permute-start(bf16[48,2048]{1,0:T(8,128)(2,1)S(1)} %pack_attention_weights.1), channel_id=1, source_target_pairs={{32,0},{99,1},{34,2},{97,3},{36,4},{103,5},{38,6},{101,7},{40,8},{... | collective-permute-start | bytes 589832 | tf_op jit(solution)/shard_map/ppermute | solution.py:580
  15.7 2.0 %collective-permute-done.1.p1 = bf16[48,2048]{1,0:T(8,128)(2,1)S(1)} collective-permute-done((bf16[48,2048]{1,0:T(8,128)(2,1)S(1)}, bf16[48,2048]{1,0:T(8,128)(2,1)S(1)}, u32[]{:S(2)}, u32[]{:S(2)}) %collective-permute-start.1) | collective-permute-done | bytes 196640 | tf_op jit(solution)/shard_map/ppermute | solution.py:580
  17.8 3.8 %collective-permute-done.2.p2 = bf16[48,2048]{1,0:T(8,128)(2,1)S(1)} collective-permute-done((bf16[48,2048]{1,0:T(8,128)(2,1)S(1)}, bf16[48,2048]{1,0:T(8,128)(2,1)S(1)}, u32[]{:S(2)}, u32[]{:S(2)}) %collective-permute-start.2) | collective-permute-done | bytes 196640 | tf_op jit(solution)/shard_map/ppermute | solution.py:580
  21.6 2.5 %collective-permute-start.8 = (bf16[48,5120]{1,0:T(8,128)(2,1)S(1)}, bf16[48,5120]{1,0:T(8,128)(2,1)S(1)}, u32[]{:S(2)}, u32[]{:S(2)}) collective-permute-start(bf16[48,5120]{1,0:T(8,128)(2,1)S(1)} %pack_feed_forward_weights.1), channel_id=1, source_target_pairs={{0,0},{67,1},{2,2},{65,3},{4,4},{71,5},{6,6},{69,7},{8,8},{75,9},{... | collective-permute-start | bytes 1474568 | tf_op jit(solution)/shard_map/ppermute | solution.py:580
  24.1 2.9 %collective-permute-start.11 = (bf16[48,5120]{1,0:T(8,128)(2,1)S(1)}, bf16[48,5120]{1,0:T(8,128)(2,1)S(1)}, u32[]{:S(2)}, u32[]{:S(2)}) collective-permute-start(bf16[48,5120]{1,0:T(8,128)(2,1)S(1)} %pack_feed_forward_weights.1), channel_id=1, source_target_pairs={{48,0},{115,1},{50,2},{113,3},{52,4},{119,5},{54,6},{117,7},{56,8}... | collective-permute-start | bytes 1474568 | tf_op jit(solution)/shard_map/ppermute | solution.py:580
  27.0 3.1 %collective-permute-start.10 = (bf16[48,5120]{1,0:T(8,128)(2,1)S(1)}, bf16[48,5120]{1,0:T(8,128)(2,1)S(1)}, u32[]{:S(2)}, u32[]{:S(2)}) collective-permute-start(bf16[48,5120]{1,0:T(8,128)(2,1)S(1)} %pack_feed_forward_weights.1), channel_id=1, source_target_pairs={{32,0},{99,1},{34,2},{97,3},{36,4},{103,5},{38,6},{101,7},{40,8},{... | collective-permute-start | bytes 1474568 | tf_op jit(solution)/shard_map/ppermute | solution.py:580
  32.2 10.5 %attention_forward.1 = (bf16[384,2048]{1,0:T(8,128)(2,1)S(1)}, f32[48,128]{1,0:T(8,128)S(1)}, f32[8,768]{1,0:T(8,128)S(1)}, bf16[8,256,1152]{2,1,0:T(8,128)(2,1)...) custom-call(s32[4]{0:T(128)S(1)} %pad_add_fusion.info, ...), custom_call_target="tpu_custom_call" | custom-call | flops 3000000000 | bytes 20000000 | tf_op jit(solution)/shard_map/attention_forward/pallas_call | solution.py:451
  42.9 8.7 %collective-permute-done.11.p3 = bf16[48,5120]{1,0:T(8,128)(2,1)S(1)} collective-permute-done((bf16[48,5120]{1,0:T(8,128)(2,1)S(1)}, bf16[48,5120]{1,0:T(8,128)(2,1)S(1)}, u32[]{:S(2)}, u32[]{:S(2)}) %collective-permute-start.11) | collective-permute-done | bytes 491552 | tf_op jit(solution)/shard_map/ppermute | solution.py:580
  56.9 32.3 %feed_forward_both_ways.1 = (bf16[384,5120]{1,0:T(8,128)(2,1)S(1)}, bf16[8,256,384]{2,1,0:T(8,128)(2,1)}, f32[8,256,384]{2,1,0:T(8,128)S(1)}, bf16[8,256,384]{2,...) custom-call(s32[4]{0:T(128)S(1)} %pad_add_fusion.info, ...), custom_call_target="tpu_custom_call" | custom-call | flops 16000000000 | bytes 30000000 | tf_op jit(solution)/shard_map/feed_forward_both_ways/pallas_call | solution.py:478
  89.3 7.1 %attention_backward_start.1 = (bf16[8,256,384]{2,1,0:T(8,128)(2,1)}, f32[384,1152]{1,0:T(8,128)S(1)}, f32[8,1152]{1,0:T(8,128)S(1)}, f32[8,768]{1,0:T(8,128)S(1)}) custom-call(s32[4]{0:T(128)S(1)} %pad_add_fusion.info, bf16[8,256,384]{2,1,0:T(8,128)(2,1)} %latents.7, bf16[8,384]{1,0:T(8,128)(2,1)} %conditions.7, ...), custom_call_target="tpu_custom_call" | custom-call | flops 2200000000 | bytes 8000000 | tf_op jit(solution)/shard_map/attention_backward_start/pallas_call | solution.py:533
  96.9 2.9 %collective-permute-start.17 = (bf16[48,5120]{1,0:T(8,128)(2,1)S(1)}, bf16[48,5120]{1,0:T(8,128)(2,1)S(1)}, u32[]{:S(2)}, u32[]{:S(2)}) collective-permute-start(bf16[48,5120]{1,0:T(8,128)(2,1)S(1)} %get-tuple-element.98), channel_id=1, source_target_pairs={{0,0},{1,67},{2,2},{3,65},{4,4},{5,71},{6,6},{7,69},{8,8},{9,75},{... | collective-permute-start | bytes 1474568 | tf_op jit(solution)/shard_map/ppermute | solution.py:580
  99.9 2.5 %collective-permute-start.19 = (bf16[48,5120]{1,0:T(8,128)(2,1)S(1)}, bf16[48,5120]{1,0:T(8,128)(2,1)S(1)}, u32[]{:S(2)}, u32[]{:S(2)}) collective-permute-start(bf16[48,5120]{1,0:T(8,128)(2,1)S(1)} %get-tuple-element.106), channel_id=1, source_target_pairs={{0,32},{1,99},{2,34},{3,97},{4,36},{5,103},{6,38},{7,101},{8,40},{... | collective-permute-start | bytes 1474568 | tf_op jit(solution)/shard_map/ppermute | solution.py:580
  102.3 2.3 %collective-permute-start.20 = (bf16[48,5120]{1,0:T(8,128)(2,1)S(1)}, bf16[48,5120]{1,0:T(8,128)(2,1)S(1)}, u32[]{:S(2)}, u32[]{:S(2)}) collective-permute-start(bf16[48,5120]{1,0:T(8,128)(2,1)S(1)} %get-tuple-element.107), channel_id=1, source_target_pairs={{0,48},{1,115},{2,50},{3,113},{4,52},{5,119},{6,54},{7,117},{8,56}... | collective-permute-start | bytes 1474568 | tf_op jit(solution)/shard_map/ppermute | solution.py:580
  104.6 16.8 %attention_backward_rest.1 = (bf16[8,256,384]{2,1,0:T(8,128)(2,1)}, bf16[8,384]{1,0:T(8,128)(2,1)}, bf16[192,2048]{1,0:T(8,128)(2,1)S(1)}, bf16[192,2048]{1,0:T(8,128)(2,1)S(1)}) custom-call(s32[4]{0:T(128)S(1)} %pad_add_fusion.info, bf16[8,256,384]{2,1,0:T(8,128)(2,1)} %latents.7, bf16[8,384]{1,0:T(8,128)(2,1)} %conditions.7, ...), custom_call_target="tpu_custom_call", output_to_operand_aliasing={{0}: (17, {})} | custom-call | flops 6600000000 | bytes 24000000 | tf_op jit(solution)/shard_map/attention_backward_rest/pallas_call | solution.py:533
  121.4 5.4 %collective-permute-done.18.refs_1_ = bf16[48,5120]{1,0:T(8,128)(2,1)S(1)} collective-permute-done((bf16[48,5120]{1,0:T(8,128)(2,1)S(1)}, bf16[48,5120]{1,0:T(8,128)(2,1)S(1)}, u32[]{:S(2)}, u32[]{:S(2)}) %collective-permute-start.18) | collective-permute-done | bytes 491552 | tf_op jit(solution)/shard_map/ppermute | solution.py:580
  134.0 3.0 %collective-permute-start.24 = (bf16[48,2048]{1,0:T(8,128)(2,1)S(1)}, bf16[48,2048]{1,0:T(8,128)(2,1)S(1)}, u32[]{:S(2)}, u32[]{:S(2)}) collective-permute-start(bf16[48,2048]{1,0:T(8,128)(2,1)S(1)} %get-tuple-element.111), channel_id=1, source_target_pairs={{0,32},{1,99},{2,34},{3,97},{4,36},{5,103},{6,38},{7,101},{8,40},{... | collective-permute-start | bytes 589832 | tf_op jit(solution)/shard_map/ppermute | solution.py:580
  139.2 2.6 %collective-permute-start.36 = (bf16[48,2560]{1,0:T(8,128)(2,1)S(1)}, bf16[48,2560]{1,0:T(8,128)(2,1)S(1)}, u32[]{:S(2)}, u32[]{:S(2)}) collective-permute-start(bf16[48,2560]{1,0:T(8,128)(2,1)S(1)} %add.26.refs_0_), channel_id=1, source_target_pairs={{0,12},{1,13},{2,14},{3,15},{4,0},{5,1},{6,2},{7,3},{8,4},{9,5},{1... | collective-permute-start | bytes 737288 | tf_op jit(solution)/shard_map/ppermute | solution.py:580
  143.0 2.2 %collective-permute-done.23.refs_1_ = bf16[48,2048]{1,0:T(8,128)(2,1)S(1)} collective-permute-done((bf16[48,2048]{1,0:T(8,128)(2,1)S(1)}, bf16[48,2048]{1,0:T(8,128)(2,1)S(1)}, u32[]{:S(2)}, u32[]{:S(2)}) %collective-permute-start.23) | collective-permute-done | bytes 196640 | tf_op jit(solution)/shard_map/ppermute | solution.py:580
  145.1 2.2 %collective-permute-start.34 = (bf16[48,2560]{1,0:T(8,128)(2,1)S(1)}, bf16[48,2560]{1,0:T(8,128)(2,1)S(1)}, u32[]{:S(2)}, u32[]{:S(2)}) collective-permute-start(bf16[48,2560]{1,0:T(8,128)(2,1)S(1)} %add.26.refs_0_), channel_id=1, source_target_pairs={{0,4},{1,5},{2,6},{3,7},{4,8},{5,9},{6,10},{7,11},{8,12},{9,13},{1... | collective-permute-start | bytes 737288 | tf_op jit(solution)/shard_map/ppermute | solution.py:580
  152.6 3.9 %collective-permute-done.34.refs_1_ = bf16[48,2560]{1,0:T(8,128)(2,1)S(1)} collective-permute-done((bf16[48,2560]{1,0:T(8,128)(2,1)S(1)}, bf16[48,2560]{1,0:T(8,128)(2,1)S(1)}, u32[]{:S(2)}, u32[]{:S(2)}) %collective-permute-start.34) | collective-permute-done | bytes 245792 | tf_op jit(solution)/shard_map/ppermute | solution.py:580
  158.7 2.8 %collective-permute-done.30.refs_3_ = bf16[48,1024]{1,0:T(8,128)(2,1)S(1)} collective-permute-done((bf16[48,1024]{1,0:T(8,128)(2,1)S(1)}, bf16[48,1024]{1,0:T(8,128)(2,1)S(1)}, u32[]{:S(2)}, u32[]{:S(2)}) %collective-permute-start.30) | collective-permute-done | bytes 98336 | tf_op jit(solution)/shard_map/ppermute | solution.py:580
  162.8 2.4 %collective-permute-done.28.refs_1_ = bf16[48,1024]{1,0:T(8,128)(2,1)S(1)} collective-permute-done((bf16[48,1024]{1,0:T(8,128)(2,1)S(1)}, bf16[48,1024]{1,0:T(8,128)(2,1)S(1)}, u32[]{:S(2)}, u32[]{:S(2)}) %collective-permute-start.28) | collective-permute-done | bytes 98336 | tf_op jit(solution)/shard_map/ppermute | solution.py:580
  (70 shorter events, 34.0 us)
Async XLA Ops:
  2.5 13.2 %collective-permute-start = (bf16[48,2048]{1,0:T(8,128)(2,1)S(1)}, bf16[48,2048]{1,0:T(8,128)(2,1)S(1)}, u32[]{:S(2)}, u32[]{:S(2)}) collective-permute-start(bf16[48,2048]{1,0:T(8,128)(2,1)S(1)} %pack_attention_weights.1), channel_id=1, source_target_pairs={{0,0},{67,1},{2,2},{65,3},{4,4},{71,5},{6,6},{69,7},{8,8},{75,9},{... | collective-permute-start | bytes 589832 | tf_op jit(solution)/shard_map/ppermute | solution.py:580
  9.0 8.8 %collective-permute-start.1 = (bf16[48,2048]{1,0:T(8,128)(2,1)S(1)}, bf16[48,2048]{1,0:T(8,128)(2,1)S(1)}, u32[]{:S(2)}, u32[]{:S(2)}) collective-permute-start(bf16[48,2048]{1,0:T(8,128)(2,1)S(1)} %pack_attention_weights.1), channel_id=1, source_target_pairs={{16,0},{83,1},{18,2},{81,3},{20,4},{87,5},{22,6},{85,7},{24,8},{91... | collective-permute-start | bytes 589832 | tf_op jit(solution)/shard_map/ppermute | solution.py:580
  11.2 10.3 %collective-permute-start.2 = (bf16[48,2048]{1,0:T(8,128)(2,1)S(1)}, bf16[48,2048]{1,0:T(8,128)(2,1)S(1)}, u32[]{:S(2)}, u32[]{:S(2)}) collective-permute-start(bf16[48,2048]{1,0:T(8,128)(2,1)S(1)} %pack_attention_weights.1), channel_id=1, source_target_pairs={{32,0},{99,1},{34,2},{97,3},{36,4},{103,5},{38,6},{101,7},{40,8},{... | collective-permute-start | bytes 589832 | tf_op jit(solution)/shard_map/ppermute | solution.py:580
  14.1 9.9 %collective-permute-start.3 = (bf16[48,2048]{1,0:T(8,128)(2,1)S(1)}, bf16[48,2048]{1,0:T(8,128)(2,1)S(1)}, u32[]{:S(2)}, u32[]{:S(2)}) collective-permute-start(bf16[48,2048]{1,0:T(8,128)(2,1)S(1)} %pack_attention_weights.1), channel_id=1, source_target_pairs={{48,0},{115,1},{50,2},{113,3},{52,4},{119,5},{54,6},{117,7},{56,8}... | collective-permute-start | bytes 589832 | tf_op jit(solution)/shard_map/ppermute | solution.py:580
  15.6 11.3 %collective-permute-start.4 = (bf16[48,2048]{1,0:T(8,128)(2,1)S(1)}, bf16[48,2048]{1,0:T(8,128)(2,1)S(1)}, u32[]{:S(2)}, u32[]{:S(2)}) collective-permute-start(bf16[48,2048]{1,0:T(8,128)(2,1)S(1)} %collective-permute-done.p0), channel_id=1, source_target_pairs={{0,1},{1,0},{2,3},{3,2},{4,5},{5,4},{6,7},{7,6},{8,9},{9,8},{10,11... | collective-permute-start | bytes 589832 | tf_op jit(solution)/shard_map/ppermute | solution.py:580
  17.8 12.3 %collective-permute-start.5 = (bf16[48,2048]{1,0:T(8,128)(2,1)S(1)}, bf16[48,2048]{1,0:T(8,128)(2,1)S(1)}, u32[]{:S(2)}, u32[]{:S(2)}) collective-permute-start(bf16[48,2048]{1,0:T(8,128)(2,1)S(1)} %collective-permute-done.1.p1), channel_id=1, source_target_pairs={{0,1},{1,0},{2,3},{3,2},{4,5},{5,4},{6,7},{7,6},{8,9},{9,8},{10,11... | collective-permute-start | bytes 589832 | tf_op jit(solution)/shard_map/ppermute | solution.py:580
  21.6 9.2 %collective-permute-start.6 = (bf16[48,2048]{1,0:T(8,128)(2,1)S(1)}, bf16[48,2048]{1,0:T(8,128)(2,1)S(1)}, u32[]{:S(2)}, u32[]{:S(2)}) collective-permute-start(bf16[48,2048]{1,0:T(8,128)(2,1)S(1)} %collective-permute-done.2.p2), channel_id=1, source_target_pairs={{0,1},{1,0},{2,3},{3,2},{4,5},{5,4},{6,7},{7,6},{8,9},{9,8},{10,11... | collective-permute-start | bytes 589832 | tf_op jit(solution)/shard_map/ppermute | solution.py:580
  21.6 21.1 %collective-permute-start.8 = (bf16[48,5120]{1,0:T(8,128)(2,1)S(1)}, bf16[48,5120]{1,0:T(8,128)(2,1)S(1)}, u32[]{:S(2)}, u32[]{:S(2)}) collective-permute-start(bf16[48,5120]{1,0:T(8,128)(2,1)S(1)} %pack_feed_forward_weights.1), channel_id=1, source_target_pairs={{0,0},{67,1},{2,2},{65,3},{4,4},{71,5},{6,6},{69,7},{8,8},{75,9},{... | collective-permute-start | bytes 1474568 | tf_op jit(solution)/shard_map/ppermute | solution.py:580
  24.1 27.5 %collective-permute-start.11 = (bf16[48,5120]{1,0:T(8,128)(2,1)S(1)}, bf16[48,5120]{1,0:T(8,128)(2,1)S(1)}, u32[]{:S(2)}, u32[]{:S(2)}) collective-permute-start(bf16[48,5120]{1,0:T(8,128)(2,1)S(1)} %pack_feed_forward_weights.1), channel_id=1, source_target_pairs={{48,0},{115,1},{50,2},{113,3},{52,4},{119,5},{54,6},{117,7},{56,8}... | collective-permute-start | bytes 1474568 | tf_op jit(solution)/shard_map/ppermute | solution.py:580
  27.0 24.6 %collective-permute-start.10 = (bf16[48,5120]{1,0:T(8,128)(2,1)S(1)}, bf16[48,5120]{1,0:T(8,128)(2,1)S(1)}, u32[]{:S(2)}, u32[]{:S(2)}) collective-permute-start(bf16[48,5120]{1,0:T(8,128)(2,1)S(1)} %pack_feed_forward_weights.1), channel_id=1, source_target_pairs={{32,0},{99,1},{34,2},{97,3},{36,4},{103,5},{38,6},{101,7},{40,8},{... | collective-permute-start | bytes 1474568 | tf_op jit(solution)/shard_map/ppermute | solution.py:580
  30.1 23.5 %collective-permute-start.9 = (bf16[48,5120]{1,0:T(8,128)(2,1)S(1)}, bf16[48,5120]{1,0:T(8,128)(2,1)S(1)}, u32[]{:S(2)}, u32[]{:S(2)}) collective-permute-start(bf16[48,5120]{1,0:T(8,128)(2,1)S(1)} %pack_feed_forward_weights.1), channel_id=1, source_target_pairs={{16,0},{83,1},{18,2},{81,3},{20,4},{87,5},{22,6},{85,7},{24,8},{91... | collective-permute-start | bytes 1474568 | tf_op jit(solution)/shard_map/ppermute | solution.py:580
  42.7 11.5 %collective-permute-start.12 = (bf16[48,5120]{1,0:T(8,128)(2,1)S(1)}, bf16[48,5120]{1,0:T(8,128)(2,1)S(1)}, u32[]{:S(2)}, u32[]{:S(2)}) collective-permute-start(bf16[48,5120]{1,0:T(8,128)(2,1)S(1)} %collective-permute-done.8.p0), channel_id=1, source_target_pairs={{0,1},{1,0},{2,3},{3,2},{4,5},{5,4},{6,7},{7,6},{8,9},{9,8},{10,11... | collective-permute-start | bytes 1474568 | tf_op jit(solution)/shard_map/ppermute | solution.py:580
  96.9 31.9 %collective-permute-start.17 = (bf16[48,5120]{1,0:T(8,128)(2,1)S(1)}, bf16[48,5120]{1,0:T(8,128)(2,1)S(1)}, u32[]{:S(2)}, u32[]{:S(2)}) collective-permute-start(bf16[48,5120]{1,0:T(8,128)(2,1)S(1)} %get-tuple-element.98), channel_id=1, source_target_pairs={{0,0},{1,67},{2,2},{3,65},{4,4},{5,71},{6,6},{7,69},{8,8},{9,75},{... | collective-permute-start | bytes 1474568 | tf_op jit(solution)/shard_map/ppermute | solution.py:580
  99.8 27.0 %collective-permute-start.18 = (bf16[48,5120]{1,0:T(8,128)(2,1)S(1)}, bf16[48,5120]{1,0:T(8,128)(2,1)S(1)}, u32[]{:S(2)}, u32[]{:S(2)}) collective-permute-start(bf16[48,5120]{1,0:T(8,128)(2,1)S(1)} %get-tuple-element.105), channel_id=1, source_target_pairs={{0,16},{1,83},{2,18},{3,81},{4,20},{5,87},{6,22},{7,85},{8,24},{9,... | collective-permute-start | bytes 1474568 | tf_op jit(solution)/shard_map/ppermute | solution.py:580
  99.9 27.0 %collective-permute-start.19 = (bf16[48,5120]{1,0:T(8,128)(2,1)S(1)}, bf16[48,5120]{1,0:T(8,128)(2,1)S(1)}, u32[]{:S(2)}, u32[]{:S(2)}) collective-permute-start(bf16[48,5120]{1,0:T(8,128)(2,1)S(1)} %get-tuple-element.106), channel_id=1, source_target_pairs={{0,32},{1,99},{2,34},{3,97},{4,36},{5,103},{6,38},{7,101},{8,40},{... | collective-permute-start | bytes 1474568 | tf_op jit(solution)/shard_map/ppermute | solution.py:580
  102.3 26.4 %collective-permute-start.20 = (bf16[48,5120]{1,0:T(8,128)(2,1)S(1)}, bf16[48,5120]{1,0:T(8,128)(2,1)S(1)}, u32[]{:S(2)}, u32[]{:S(2)}) collective-permute-start(bf16[48,5120]{1,0:T(8,128)(2,1)S(1)} %get-tuple-element.107), channel_id=1, source_target_pairs={{0,48},{1,115},{2,50},{3,113},{4,52},{5,119},{6,54},{7,117},{8,56}... | collective-permute-start | bytes 1474568 | tf_op jit(solution)/shard_map/ppermute | solution.py:580
  132.0 9.8 %collective-permute-start.22 = (bf16[48,2048]{1,0:T(8,128)(2,1)S(1)}, bf16[48,2048]{1,0:T(8,128)(2,1)S(1)}, u32[]{:S(2)}, u32[]{:S(2)}) collective-permute-start(bf16[48,2048]{1,0:T(8,128)(2,1)S(1)} %get-tuple-element.109), channel_id=1, source_target_pairs={{0,0},{1,67},{2,2},{3,65},{4,4},{5,71},{6,6},{7,69},{8,8},{9,75},{... | collective-permute-start | bytes 589832 | tf_op jit(solution)/shard_map/ppermute | solution.py:580
  134.0 11.2 %collective-permute-start.23 = (bf16[48,2048]{1,0:T(8,128)(2,1)S(1)}, bf16[48,2048]{1,0:T(8,128)(2,1)S(1)}, u32[]{:S(2)}, u32[]{:S(2)}) collective-permute-start(bf16[48,2048]{1,0:T(8,128)(2,1)S(1)} %get-tuple-element.110), channel_id=1, source_target_pairs={{0,16},{1,83},{2,18},{3,81},{4,20},{5,87},{6,22},{7,85},{8,24},{9,... | collective-permute-start | bytes 589832 | tf_op jit(solution)/shard_map/ppermute | solution.py:580
  134.0 13.3 %collective-permute-start.24 = (bf16[48,2048]{1,0:T(8,128)(2,1)S(1)}, bf16[48,2048]{1,0:T(8,128)(2,1)S(1)}, u32[]{:S(2)}, u32[]{:S(2)}) collective-permute-start(bf16[48,2048]{1,0:T(8,128)(2,1)S(1)} %get-tuple-element.111), channel_id=1, source_target_pairs={{0,32},{1,99},{2,34},{3,97},{4,36},{5,103},{6,38},{7,101},{8,40},{... | collective-permute-start | bytes 589832 | tf_op jit(solution)/shard_map/ppermute | solution.py:580
  137.1 10.3 %collective-permute-start.25 = (bf16[48,2048]{1,0:T(8,128)(2,1)S(1)}, bf16[48,2048]{1,0:T(8,128)(2,1)S(1)}, u32[]{:S(2)}, u32[]{:S(2)}) collective-permute-start(bf16[48,2048]{1,0:T(8,128)(2,1)S(1)} %get-tuple-element.112), channel_id=1, source_target_pairs={{0,48},{1,115},{2,50},{3,113},{4,52},{5,119},{6,54},{7,117},{8,56}... | collective-permute-start | bytes 589832 | tf_op jit(solution)/shard_map/ppermute | solution.py:580
  139.2 13.4 %collective-permute-start.36 = (bf16[48,2560]{1,0:T(8,128)(2,1)S(1)}, bf16[48,2560]{1,0:T(8,128)(2,1)S(1)}, u32[]{:S(2)}, u32[]{:S(2)}) collective-permute-start(bf16[48,2560]{1,0:T(8,128)(2,1)S(1)} %add.26.refs_0_), channel_id=1, source_target_pairs={{0,12},{1,13},{2,14},{3,15},{4,0},{5,1},{6,2},{7,3},{8,4},{9,5},{1... | collective-permute-start | bytes 737288 | tf_op jit(solution)/shard_map/ppermute | solution.py:580
  141.8 10.8 %collective-permute-start.35 = (bf16[48,2560]{1,0:T(8,128)(2,1)S(1)}, bf16[48,2560]{1,0:T(8,128)(2,1)S(1)}, u32[]{:S(2)}, u32[]{:S(2)}) collective-permute-start(bf16[48,2560]{1,0:T(8,128)(2,1)S(1)} %add.26.refs_0_), channel_id=1, source_target_pairs={{0,8},{1,9},{2,10},{3,11},{4,12},{5,13},{6,14},{7,15},{8,0},{9,1},... | collective-permute-start | bytes 737288 | tf_op jit(solution)/shard_map/ppermute | solution.py:580
  145.1 11.4 %collective-permute-start.34 = (bf16[48,2560]{1,0:T(8,128)(2,1)S(1)}, bf16[48,2560]{1,0:T(8,128)(2,1)S(1)}, u32[]{:S(2)}, u32[]{:S(2)}) collective-permute-start(bf16[48,2560]{1,0:T(8,128)(2,1)S(1)} %add.26.refs_0_), channel_id=1, source_target_pairs={{0,4},{1,5},{2,6},{3,7},{4,8},{5,9},{6,10},{7,11},{8,12},{9,13},{1... | collective-permute-start | bytes 737288 | tf_op jit(solution)/shard_map/ppermute | solution.py:580
  156.7 9.6 %collective-permute-start.37 = (bf16[48,2560]{1,0:T(8,128)(2,1)S(1)}, bf16[48,2560]{1,0:T(8,128)(2,1)S(1)}, u32[]{:S(2)}, u32[]{:S(2)}) collective-permute-start(bf16[48,2560]{1,0:T(8,128)(2,1)S(1)} %add.27.two_a), channel_id=1, source_target_pairs={{0,1},{1,0},{2,3},{3,2},{4,5},{5,4},{6,7},{7,6},{8,9},{9,8},{10,11... | collective-permute-start | bytes 737288 | tf_op jit(solution)/shard_map/ppermute | solution.py:580
  (14 other events, 56.2 us)

commit v2 on v1

--- a/solution.py
+++ b/solution.py
@@ -304,28 +304,19 @@
 
 
 def backward_kernel(
-    first, last,
     info, latents, conditions, qkv_in, expo_in, mixed_in, rinv_in, hidden_in, grad_mid_in,
-    grad_mixed_in, mod_in, weights, *refs,
+    grad_mixed_in, mod_in, weights, weights_two, grad_mod_two,
+    out, grad_cond, keep, send,
+    acc_qkv, acc_bias, grad_mod,
 ):
-    if last:
-        weights_two, grad_mod_two, acc_in, bias_in, grad_mod_in, _, out, grad_cond, keep, send = refs[:10]
-        acc_qkv, acc_bias, grad_mod = refs[10:]
-    else:
-        out, acc_qkv, acc_bias, grad_mod = refs
     step = pl.program_id(0)
-    slot = PAIR * (step + first)
+    slot = PAIR * step
 
     @pl.when(step == 0)
     def _():
-        if last:
-            acc_qkv[...] = acc_in[...]
-            acc_bias[...] = bias_in[...]
-            grad_mod[...] = grad_mod_in[...]
-        else:
-            acc_qkv[...] = jnp.zeros_like(acc_qkv)
-            acc_bias[...] = jnp.zeros_like(acc_bias)
-            grad_mod[...] = jnp.zeros_like(grad_mod)
+        acc_qkv[...] = jnp.zeros_like(acc_qkv)
+        acc_bias[...] = jnp.zeros_like(acc_bias)
+        grad_mod[...] = jnp.zeros_like(grad_mod)
 
     @pl.when(slot >= info[0])
     def _():
@@ -378,10 +369,7 @@
             back = norm_back(d_hidden * (1.0 + row[:, D : 2 * D]), normed, inverse)
             out[i] = (grad_mid_in[slot + i] + back).astype(BF)
 
-    if not last:
-        return
-
-    @pl.when(step == STEPS - 1 - first)
+    @pl.when(step == STEPS - 1)
     def _():
         cond = conditions[...].astype(F32)
         sig = 1.0 / (1.0 + jnp.exp(-cond))
@@ -413,15 +401,15 @@
             pl.when(jnp.logical_not(is_mine))(functools.partial(put, send))
 
 
-def slot_spec(first=0):
+def slot_spec():
     def index(j, info):
-        return (jnp.minimum(j + first, jnp.maximum((info[0] + 1) // 2 - 1, 0)), 0, 0)
+        return (jnp.minimum(j, jnp.maximum((info[0] + 1) // 2 - 1, 0)), 0, 0)
 
     return pl.BlockSpec((PAIR, TOK, D), index)
 
 
-def slot_out(first=0):
-    return pl.BlockSpec((PAIR, TOK, D), lambda j, info: (j + first, 0, 0))
+def slot_out():
+    return pl.BlockSpec((PAIR, TOK, D), lambda j, info: (j, 0, 0))
 
 
 def held():
@@ -515,38 +503,32 @@
     )(info, far(latents), far(conditions), stay(mixed), far(grad_out), stay(bias), *pieces)
 
 
-def run_backward(first, count, info, latents, shared, carried=None):
-    last = carried is not None
-
-    in_specs = [slot_spec(first), whole(CAP, D)] + [held()] * 9
-    out_specs = [slot_out(first)]
-    out_shape = [jax.ShapeDtypeStruct((CAP, TOK, D), BF)]
-    state = [(D, QKV_W), (8, QKV_W), (CAP, MOD_ONE)]
-    if last:
-        in_specs += [held()] * 5 + [pl.BlockSpec(memory_space=pl.ANY)]
-        out_specs += [whole(CAP, D), held(), held()]
-        out_shape += [jax.ShapeDtypeStruct((CAP, D), BF)]
-        out_shape += [pltpu.VMEM((192, LANES_ONE), BF)] * 2
-    else:
-        out_specs += [held()] * 3
-        out_shape += [pltpu.VMEM(shape, F32) for shape in state]
+def run_backward(info, latents, conditions, *values):
     return pl.pallas_call(
-        functools.partial(backward_kernel, first, last),
+        backward_kernel,
         grid_spec=pltpu.PrefetchScalarGridSpec(
             num_scalar_prefetch=1,
-            grid=(count,),
-            in_specs=in_specs,
-            out_specs=out_specs,
-            scratch_shapes=[pltpu.VMEM(shape, F32) for shape in state] if last else [],
+            grid=(STEPS,),
+            in_specs=[slot_spec(), whole(CAP, D)] + [held()] * 11,
+            out_specs=[slot_out(), whole(CAP, D), held(), held()],
+            scratch_shapes=[
+                pltpu.VMEM((D, QKV_W), F32),
+                pltpu.VMEM((8, QKV_W), F32),
+                pltpu.VMEM((CAP, MOD_ONE), F32),
+            ],
         ),
-        out_shape=out_shape,
-        input_output_aliases={17: 0} if last else {},
+        out_shape=[
+            jax.ShapeDtypeStruct((CAP, TOK, D), BF),
+            jax.ShapeDtypeStruct((CAP, D), BF),
+            pltpu.VMEM((192, LANES_ONE), BF),
+            pltpu.VMEM((192, LANES_ONE), BF),
+        ],
         compiler_params=params(10),
-        name="attention_backward_rest" if last else "attention_backward_start",
+        name="attention_backward",
         cost_estimate=pl.CostEstimate(
-            flops=2_200_000_000 * count, bytes_accessed=8_000_000 * count, transcendentals=1_000
+            flops=25_000_000_000, bytes_accessed=20_000_000, transcendentals=1_000
         ),
-    )(info, far(latents), far(shared[0]), *map(stay, shared[1:]), *map(stay, (carried or ())[:-1]), *(carried or ())[-1:])
+    )(info, far(latents), far(conditions), *map(stay, values))
 
 
 def place(index):
@@ -773,20 +755,15 @@
     weights_two, out, grad_mid, grad_mixed, grad_mod_two, keep_two, send_two = run_middle(
         info, latents, conditions, mixed, grad_out, bias, mine_two + other_two
     )
-    swapped_two = move(send_two, CORE_SWAP)
-    shared = (
-        conditions, qkv, expo, mixed, rinv, hidden, grad_mid, grad_mixed, mod, weights,
-    )
-    grad_latents, acc_qkv, acc_bias, grad_mod = run_backward(0, 1, info, latents, shared)
-    held_two = add_blocks(keep_two, after(swapped_two, acc_bias))
+    held_two = add_blocks(keep_two, move(send_two, CORE_SWAP))
     arrived_two = scatter(held_two)
     grad_latents, grad_cond, keep_one, send_one = run_backward(
-        1, 3, info, latents, shared,
-        (weights_two, grad_mod_two, acc_qkv, acc_bias, after(grad_mod, held_two[0]), grad_latents),
+        info, latents, conditions, qkv, expo, mixed, rinv, hidden, grad_mid, grad_mixed, mod,
+        weights, weights_two, after(grad_mod_two, held_two[0]),
     )
     held_one = add_blocks(keep_one, move(after(send_one, *arrived_two), CORE_SWAP))
     arrived_one = scatter(held_one)
-    two = sum_replicas(arrived_two, info)
+    two = sum_replicas([after(arrived_two[0], arrived_one[1]), *arrived_two[1:]], info)
     one = sum_replicas(arrived_one, info)
     return (out, grad_latents, grad_cond, *finish(info, one + two))
 

time: 169 us -> 175 us (1.036)
  Pallas kernels: 73 us -> 44.6 us
  waiting for transfers between devices: 46.4 us -> 68.7 us
  starting transfers between devices: 48 us -> 59.6 us
    ppermute x38, waiting for transfers between devices: 46.4 us -> 68.7 us  [move(): return lax.ppermute(value, BOTH, pairs)]
    pallas_call x1, Pallas kernels: 32.3 us -> 18.9 us  [run_middle(): pl.pallas_call(middle_kernel, grid_spec=pltpu.PrefetchScalarGridSpec(num_...]
    ppermute x38, starting transfers between devices: 48 us -> 59.6 us  [move(): return lax.ppermute(value, BOTH, pairs)]
    pallas_call x2 -> x1, Pallas kernels: 23.8 us -> 13 us  [run_backward(): pl.pallas_call(backward_kernel, grid_spec=pltpu.PrefetchScalarGridSpec(nu...]
    pallas_call x1, Pallas kernels: 10.5 us -> 6.23 us  [run_forward(): pl.pallas_call(forward_kernel, grid_spec=pltpu.PrefetchScalarGridSpec(num...]
  transfers between devices with their start and end apart: 38 -> 38, of which waited for: 20 -> 22; matrix products, arithmetic and copies ran while one was open for 0% -> 0% of each run, Pallas kernels for 22% -> 12%
where the time goes in v2:
time: 175 us; the launch traced here: 174 us
  waiting for transfers between devices  68.7 us (39%)
  starting transfers between devices  59.6 us (34%)
  Pallas kernels  44.6 us (25%)
    ppermute x38, waiting for transfers between devices, move(): return lax.ppermute(value, BOTH, pairs)  68.7 us
    ppermute x38, starting transfers between devices, move(): return lax.ppermute(value, BOTH, pairs)  59.6 us
    pallas_call x1, Pallas kernels, run_middle(): pl.pallas_call(middle_kernel, grid_spec=pltpu.PrefetchScalarGridSpec(num_...  18.9 us
    pallas_call x1, Pallas kernels, run_backward(): pl.pallas_call(backward_kernel, grid_spec=pltpu.PrefetchScalarGridSpec(nu...  13 us
    pallas_call x1, Pallas kernels, run_forward(): pl.pallas_call(forward_kernel, grid_spec=pltpu.PrefetchScalarGridSpec(num...  6.23 us
  transfers between devices with their start and end apart: 38, of which 22 were waited for; matrix products, arithmetic and copies ran while one was open for 0% of the time, Pallas kernels for 12%

profile of v2, /device:TPU:1, one launch (start us, length us, event | category | flops | bytes accessed | tf_op | source)
XLA Modules:
  0.0 174.5 jit_solution(18281909254212404132)
XLA Ops:
  2.5 6.5 %collective-permute-start = (bf16[48,2048]{1,0:T(8,128)(2,1)S(1)}, bf16[48,2048]{1,0:T(8,128)(2,1)S(1)}, u32[]{:S(2)}, u32[]{:S(2)}) collective-permute-start(bf16[48,2048]{1,0:T(8,128)(2,1)S(1)} %pack_attention_weights.1), channel_id=1, source_target_pairs={{0,0},{67,1},{2,2},{65,3},{4,4},{71,5},{6,6},{69,7},{8,8},{75,9},{... | collective-permute-start | bytes 589832 | tf_op jit(solution)/shard_map/ppermute | solution.py:562
  9.0 2.3 %collective-permute-start.1 = (bf16[48,2048]{1,0:T(8,128)(2,1)S(1)}, bf16[48,2048]{1,0:T(8,128)(2,1)S(1)}, u32[]{:S(2)}, u32[]{:S(2)}) collective-permute-start(bf16[48,2048]{1,0:T(8,128)(2,1)S(1)} %pack_attention_weights.1), channel_id=1, source_target_pairs={{16,0},{83,1},{18,2},{81,3},{20,4},{87,5},{22,6},{85,7},{24,8},{91... | collective-permute-start | bytes 589832 | tf_op jit(solution)/shard_map/ppermute | solution.py:562
  11.2 2.9 %collective-permute-start.2 = (bf16[48,2048]{1,0:T(8,128)(2,1)S(1)}, bf16[48,2048]{1,0:T(8,128)(2,1)S(1)}, u32[]{:S(2)}, u32[]{:S(2)}) collective-permute-start(bf16[48,2048]{1,0:T(8,128)(2,1)S(1)} %pack_attention_weights.1), channel_id=1, source_target_pairs={{32,0},{99,1},{34,2},{97,3},{36,4},{103,5},{38,6},{101,7},{40,8},{... | collective-permute-start | bytes 589832 | tf_op jit(solution)/shard_map/ppermute | solution.py:562
  17.8 3.8 %collective-permute-done.2.p2 = bf16[48,2048]{1,0:T(8,128)(2,1)S(1)} collective-permute-done((bf16[48,2048]{1,0:T(8,128)(2,1)S(1)}, bf16[48,2048]{1,0:T(8,128)(2,1)S(1)}, u32[]{:S(2)}, u32[]{:S(2)}) %collective-permute-start.2) | collective-permute-done | bytes 196640 | tf_op jit(solution)/shard_map/ppermute | solution.py:562
  21.6 2.5 %collective-permute-start.8 = (bf16[48,5120]{1,0:T(8,128)(2,1)S(1)}, bf16[48,5120]{1,0:T(8,128)(2,1)S(1)}, u32[]{:S(2)}, u32[]{:S(2)}) collective-permute-start(bf16[48,5120]{1,0:T(8,128)(2,1)S(1)} %pack_feed_forward_weights.1), channel_id=1, source_target_pairs={{0,0},{67,1},{2,2},{65,3},{4,4},{71,5},{6,6},{69,7},{8,8},{75,9},{... | collective-permute-start | bytes 1474568 | tf_op jit(solution)/shard_map/ppermute | solution.py:562
  24.1 2.9 %collective-permute-start.11 = (bf16[48,5120]{1,0:T(8,128)(2,1)S(1)}, bf16[48,5120]{1,0:T(8,128)(2,1)S(1)}, u32[]{:S(2)}, u32[]{:S(2)}) collective-permute-start(bf16[48,5120]{1,0:T(8,128)(2,1)S(1)} %pack_feed_forward_weights.1), channel_id=1, source_target_pairs={{48,0},{115,1},{50,2},{113,3},{52,4},{119,5},{54,6},{117,7},{56,8}... | collective-permute-start | bytes 1474568 | tf_op jit(solution)/shard_map/ppermute | solution.py:562
  27.0 3.1 %collective-permute-start.10 = (bf16[48,5120]{1,0:T(8,128)(2,1)S(1)}, bf16[48,5120]{1,0:T(8,128)(2,1)S(1)}, u32[]{:S(2)}, u32[]{:S(2)}) collective-permute-start(bf16[48,5120]{1,0:T(8,128)(2,1)S(1)} %pack_feed_forward_weights.1), channel_id=1, source_target_pairs={{32,0},{99,1},{34,2},{97,3},{36,4},{103,5},{38,6},{101,7},{40,8},{... | collective-permute-start | bytes 1474568 | tf_op jit(solution)/shard_map/ppermute | solution.py:562
  32.2 6.2 %attention_forward.1 = (bf16[384,2048]{1,0:T(8,128)(2,1)S(1)}, f32[48,128]{1,0:T(8,128)S(1)}, f32[8,768]{1,0:T(8,128)S(1)}, bf16[8,256,1152]{2,1,0:T(8,128)(2,1)...) custom-call(s32[4]{0:T(128)S(1)} %pad_add_fusion.info, ...), custom_call_target="tpu_custom_call" | custom-call | flops 3000000000 | bytes 20000000 | tf_op jit(solution)/shard_map/attention_forward/pallas_call | solution.py:439
  38.5 13.1 %collective-permute-done.11.p3 = bf16[48,5120]{1,0:T(8,128)(2,1)S(1)} collective-permute-done((bf16[48,5120]{1,0:T(8,128)(2,1)S(1)}, bf16[48,5120]{1,0:T(8,128)(2,1)S(1)}, u32[]{:S(2)}, u32[]{:S(2)}) %collective-permute-start.11) | collective-permute-done | bytes 491552 | tf_op jit(solution)/shard_map/ppermute | solution.py:562
  56.9 18.9 %feed_forward_both_ways.1 = (bf16[384,5120]{1,0:T(8,128)(2,1)S(1)}, bf16[8,256,384]{2,1,0:T(8,128)(2,1)}, f32[8,256,384]{2,1,0:T(8,128)S(1)}, bf16[8,256,384]{2,...) custom-call(s32[4]{0:T(128)S(1)} %pad_add_fusion.info, ...), custom_call_target="tpu_custom_call" | custom-call | flops 16000000000 | bytes 30000000 | tf_op jit(solution)/shard_map/feed_forward_both_ways/pallas_call | solution.py:466
  75.8 4.0 %collective-permute-done.16.right = bf16[192,5120]{1,0:T(8,128)(2,1)S(1)} collective-permute-done((bf16[192,5120]{1,0:T(8,128)(2,1)S(1)}, bf16[192,5120]{1,0:T(8,128)(2,1)S(1)}, u32[]{:S(2)}, u32[]{:S(2)}) %collective-permute-start.16) | collective-permute-done | bytes 1966112 | tf_op jit(solution)/shard_map/ppermute | solution.py:562
  80.3 15.9 %collective-permute-start.17 = (bf16[48,5120]{1,0:T(8,128)(2,1)S(1)}, bf16[48,5120]{1,0:T(8,128)(2,1)S(1)}, u32[]{:S(2)}, u32[]{:S(2)}) collective-permute-start(bf16[48,5120]{1,0:T(8,128)(2,1)S(1)} %get-tuple-element.90), channel_id=1, source_target_pairs={{0,0},{1,67},{2,2},{3,65},{4,4},{5,71},{6,6},{7,69},{8,8},{9,75},{... | collective-permute-start | bytes 1474568 | tf_op jit(solution)/shard_map/ppermute | solution.py:562
  97.3 4.1 %collective-permute-start.20 = (bf16[48,5120]{1,0:T(8,128)(2,1)S(1)}, bf16[48,5120]{1,0:T(8,128)(2,1)S(1)}, u32[]{:S(2)}, u32[]{:S(2)}) collective-permute-start(bf16[48,5120]{1,0:T(8,128)(2,1)S(1)} %get-tuple-element.98), channel_id=1, source_target_pairs={{0,48},{1,115},{2,50},{3,113},{4,52},{5,119},{6,54},{7,117},{8,56}... | collective-permute-start | bytes 1474568 | tf_op jit(solution)/shard_map/ppermute | solution.py:562
  101.3 13.0 %attention_backward.1 = (bf16[8,256,384]{2,1,0:T(8,128)(2,1)}, bf16[8,384]{1,0:T(8,128)(2,1)}, bf16[192,2048]{1,0:T(8,128)(2,1)S(1)}, bf16[192,2048]{1,0:T(8,128)(2,1)S(1)}) custom-call(s32[4]{0:T(128)S(1)} %pad_add_fusion.info, bf16[8,256,384]{2,1,0:T(8,128)(2,1)} %latents.5, bf16[8,384]{1,0:T(8,128)(2,1)} %conditions.5, ...), custom_call_target="tpu_custom_call" | custom-call | flops 24999999488 | bytes 20000000 | tf_op jit(solution)/shard_map/attention_backward/pallas_call | solution.py:507
  114.4 8.5 %collective-permute-done.18.refs_1_ = bf16[48,5120]{1,0:T(8,128)(2,1)S(1)} collective-permute-done((bf16[48,5120]{1,0:T(8,128)(2,1)S(1)}, bf16[48,5120]{1,0:T(8,128)(2,1)S(1)}, u32[]{:S(2)}, u32[]{:S(2)}) %collective-permute-start.18) | collective-permute-done | bytes 491552 | tf_op jit(solution)/shard_map/ppermute | solution.py:562
  124.1 2.3 %collective-permute-done.21.right = bf16[192,2048]{1,0:T(8,128)(2,1)S(1)} collective-permute-done((bf16[192,2048]{1,0:T(8,128)(2,1)S(1)}, bf16[192,2048]{1,0:T(8,128)(2,1)S(1)}, u32[]{:S(2)}, u32[]{:S(2)}) %collective-permute-start.21) | collective-permute-done | bytes 786464 | tf_op jit(solution)/shard_map/ppermute | solution.py:562
  126.6 7.8 %collective-permute-done.23.refs_1_ = bf16[48,2048]{1,0:T(8,128)(2,1)S(1)} collective-permute-done((bf16[48,2048]{1,0:T(8,128)(2,1)S(1)}, bf16[48,2048]{1,0:T(8,128)(2,1)S(1)}, u32[]{:S(2)}, u32[]{:S(2)}) %collective-permute-start.23) | collective-permute-done | bytes 196640 | tf_op jit(solution)/shard_map/ppermute | solution.py:562
  138.9 2.7 %collective-permute-start.24 = (bf16[48,2048]{1,0:T(8,128)(2,1)S(1)}, bf16[48,2048]{1,0:T(8,128)(2,1)S(1)}, u32[]{:S(2)}, u32[]{:S(2)}) collective-permute-start(bf16[48,2048]{1,0:T(8,128)(2,1)S(1)} %get-tuple-element.102), channel_id=1, source_target_pairs={{0,32},{1,99},{2,34},{3,97},{4,36},{5,103},{6,38},{7,101},{8,40},{... | collective-permute-start | bytes 589832 | tf_op jit(solution)/shard_map/ppermute | solution.py:562
  141.6 2.7 %collective-permute-start.25 = (bf16[48,2048]{1,0:T(8,128)(2,1)S(1)}, bf16[48,2048]{1,0:T(8,128)(2,1)S(1)}, u32[]{:S(2)}, u32[]{:S(2)}) collective-permute-start(bf16[48,2048]{1,0:T(8,128)(2,1)S(1)} %get-tuple-element.103), channel_id=1, source_target_pairs={{0,48},{1,115},{2,50},{3,113},{4,52},{5,119},{6,54},{7,117},{8,56}... | collective-permute-start | bytes 589832 | tf_op jit(solution)/shard_map/ppermute | solution.py:562
  144.5 3.4 %collective-permute-start.36 = (bf16[48,2560]{1,0:T(8,128)(2,1)S(1)}, bf16[48,2560]{1,0:T(8,128)(2,1)S(1)}, u32[]{:S(2)}, u32[]{:S(2)}) collective-permute-start(bf16[48,2560]{1,0:T(8,128)(2,1)S(1)} %add.26.refs_0_), channel_id=1, source_target_pairs={{0,12},{1,13},{2,14},{3,15},{4,0},{5,1},{6,2},{7,3},{8,4},{9,5},{1... | collective-permute-start | bytes 737288 | tf_op jit(solution)/shard_map/ppermute | solution.py:562
  152.4 5.6 %collective-permute-done.36.refs_3_ = bf16[48,2560]{1,0:T(8,128)(2,1)S(1)} collective-permute-done((bf16[48,2560]{1,0:T(8,128)(2,1)S(1)}, bf16[48,2560]{1,0:T(8,128)(2,1)S(1)}, u32[]{:S(2)}, u32[]{:S(2)}) %collective-permute-start.36) | collective-permute-done | bytes 245792 | tf_op jit(solution)/shard_map/ppermute | solution.py:562
  158.0 3.9 %collective-permute-done.34.refs_1_ = bf16[48,2560]{1,0:T(8,128)(2,1)S(1)} collective-permute-done((bf16[48,2560]{1,0:T(8,128)(2,1)S(1)}, bf16[48,2560]{1,0:T(8,128)(2,1)S(1)}, u32[]{:S(2)}, u32[]{:S(2)}) %collective-permute-start.34) | collective-permute-done | bytes 245792 | tf_op jit(solution)/shard_map/ppermute | solution.py:562
  164.7 2.4 %collective-permute-done.30.refs_3_ = bf16[48,1024]{1,0:T(8,128)(2,1)S(1)} collective-permute-done((bf16[48,1024]{1,0:T(8,128)(2,1)S(1)}, bf16[48,1024]{1,0:T(8,128)(2,1)S(1)}, u32[]{:S(2)}, u32[]{:S(2)}) %collective-permute-start.30) | collective-permute-done | bytes 98336 | tf_op jit(solution)/shard_map/ppermute | solution.py:562
  168.4 2.8 %collective-permute-done.28.refs_1_ = bf16[48,1024]{1,0:T(8,128)(2,1)S(1)} collective-permute-done((bf16[48,1024]{1,0:T(8,128)(2,1)S(1)}, bf16[48,1024]{1,0:T(8,128)(2,1)S(1)}, u32[]{:S(2)}, u32[]{:S(2)}) %collective-permute-start.28) | collective-permute-done | bytes 98336 | tf_op jit(solution)/shard_map/ppermute | solution.py:562
  (69 shorter events, 31.6 us)
Async XLA Ops:
  2.5 13.2 %collective-permute-start = (bf16[48,2048]{1,0:T(8,128)(2,1)S(1)}, bf16[48,2048]{1,0:T(8,128)(2,1)S(1)}, u32[]{:S(2)}, u32[]{:S(2)}) collective-permute-start(bf16[48,2048]{1,0:T(8,128)(2,1)S(1)} %pack_attention_weights.1), channel_id=1, source_target_pairs={{0,0},{67,1},{2,2},{65,3},{4,4},{71,5},{6,6},{69,7},{8,8},{75,9},{... | collective-permute-start | bytes 589832 | tf_op jit(solution)/shard_map/ppermute | solution.py:562
  9.0 8.8 %collective-permute-start.1 = (bf16[48,2048]{1,0:T(8,128)(2,1)S(1)}, bf16[48,2048]{1,0:T(8,128)(2,1)S(1)}, u32[]{:S(2)}, u32[]{:S(2)}) collective-permute-start(bf16[48,2048]{1,0:T(8,128)(2,1)S(1)} %pack_attention_weights.1), channel_id=1, source_target_pairs={{16,0},{83,1},{18,2},{81,3},{20,4},{87,5},{22,6},{85,7},{24,8},{91... | collective-permute-start | bytes 589832 | tf_op jit(solution)/shard_map/ppermute | solution.py:562
  11.2 10.3 %collective-permute-start.2 = (bf16[48,2048]{1,0:T(8,128)(2,1)S(1)}, bf16[48,2048]{1,0:T(8,128)(2,1)S(1)}, u32[]{:S(2)}, u32[]{:S(2)}) collective-permute-start(bf16[48,2048]{1,0:T(8,128)(2,1)S(1)} %pack_attention_weights.1), channel_id=1, source_target_pairs={{32,0},{99,1},{34,2},{97,3},{36,4},{103,5},{38,6},{101,7},{40,8},{... | collective-permute-start | bytes 589832 | tf_op jit(solution)/shard_map/ppermute | solution.py:562
  14.1 9.9 %collective-permute-start.3 = (bf16[48,2048]{1,0:T(8,128)(2,1)S(1)}, bf16[48,2048]{1,0:T(8,128)(2,1)S(1)}, u32[]{:S(2)}, u32[]{:S(2)}) collective-permute-start(bf16[48,2048]{1,0:T(8,128)(2,1)S(1)} %pack_attention_weights.1), channel_id=1, source_target_pairs={{48,0},{115,1},{50,2},{113,3},{52,4},{119,5},{54,6},{117,7},{56,8}... | collective-permute-start | bytes 589832 | tf_op jit(solution)/shard_map/ppermute | solution.py:562
  15.6 11.3 %collective-permute-start.4 = (bf16[48,2048]{1,0:T(8,128)(2,1)S(1)}, bf16[48,2048]{1,0:T(8,128)(2,1)S(1)}, u32[]{:S(2)}, u32[]{:S(2)}) collective-permute-start(bf16[48,2048]{1,0:T(8,128)(2,1)S(1)} %collective-permute-done.p0), channel_id=1, source_target_pairs={{0,1},{1,0},{2,3},{3,2},{4,5},{5,4},{6,7},{7,6},{8,9},{9,8},{10,11... | collective-permute-start | bytes 589832 | tf_op jit(solution)/shard_map/ppermute | solution.py:562
  17.8 12.3 %collective-permute-start.5 = (bf16[48,2048]{1,0:T(8,128)(2,1)S(1)}, bf16[48,2048]{1,0:T(8,128)(2,1)S(1)}, u32[]{:S(2)}, u32[]{:S(2)}) collective-permute-start(bf16[48,2048]{1,0:T(8,128)(2,1)S(1)} %collective-permute-done.1.p1), channel_id=1, source_target_pairs={{0,1},{1,0},{2,3},{3,2},{4,5},{5,4},{6,7},{7,6},{8,9},{9,8},{10,11... | collective-permute-start | bytes 589832 | tf_op jit(solution)/shard_map/ppermute | solution.py:562
  21.6 9.2 %collective-permute-start.6 = (bf16[48,2048]{1,0:T(8,128)(2,1)S(1)}, bf16[48,2048]{1,0:T(8,128)(2,1)S(1)}, u32[]{:S(2)}, u32[]{:S(2)}) collective-permute-start(bf16[48,2048]{1,0:T(8,128)(2,1)S(1)} %collective-permute-done.2.p2), channel_id=1, source_target_pairs={{0,1},{1,0},{2,3},{3,2},{4,5},{5,4},{6,7},{7,6},{8,9},{9,8},{10,11... | collective-permute-start | bytes 589832 | tf_op jit(solution)/shard_map/ppermute | solution.py:562
  21.6 16.9 %collective-permute-start.8 = (bf16[48,5120]{1,0:T(8,128)(2,1)S(1)}, bf16[48,5120]{1,0:T(8,128)(2,1)S(1)}, u32[]{:S(2)}, u32[]{:S(2)}) collective-permute-start(bf16[48,5120]{1,0:T(8,128)(2,1)S(1)} %pack_feed_forward_weights.1), channel_id=1, source_target_pairs={{0,0},{67,1},{2,2},{65,3},{4,4},{71,5},{6,6},{69,7},{8,8},{75,9},{... | collective-permute-start | bytes 1474568 | tf_op jit(solution)/shard_map/ppermute | solution.py:562
  24.1 27.5 %collective-permute-start.11 = (bf16[48,5120]{1,0:T(8,128)(2,1)S(1)}, bf16[48,5120]{1,0:T(8,128)(2,1)S(1)}, u32[]{:S(2)}, u32[]{:S(2)}) collective-permute-start(bf16[48,5120]{1,0:T(8,128)(2,1)S(1)} %pack_feed_forward_weights.1), channel_id=1, source_target_pairs={{48,0},{115,1},{50,2},{113,3},{52,4},{119,5},{54,6},{117,7},{56,8}... | collective-permute-start | bytes 1474568 | tf_op jit(solution)/shard_map/ppermute | solution.py:562
  27.0 24.6 %collective-permute-start.10 = (bf16[48,5120]{1,0:T(8,128)(2,1)S(1)}, bf16[48,5120]{1,0:T(8,128)(2,1)S(1)}, u32[]{:S(2)}, u32[]{:S(2)}) collective-permute-start(bf16[48,5120]{1,0:T(8,128)(2,1)S(1)} %pack_feed_forward_weights.1), channel_id=1, source_target_pairs={{32,0},{99,1},{34,2},{97,3},{36,4},{103,5},{38,6},{101,7},{40,8},{... | collective-permute-start | bytes 1474568 | tf_op jit(solution)/shard_map/ppermute | solution.py:562
  30.1 23.5 %collective-permute-start.9 = (bf16[48,5120]{1,0:T(8,128)(2,1)S(1)}, bf16[48,5120]{1,0:T(8,128)(2,1)S(1)}, u32[]{:S(2)}, u32[]{:S(2)}) collective-permute-start(bf16[48,5120]{1,0:T(8,128)(2,1)S(1)} %pack_feed_forward_weights.1), channel_id=1, source_target_pairs={{16,0},{83,1},{18,2},{81,3},{20,4},{87,5},{22,6},{85,7},{24,8},{91... | collective-permute-start | bytes 1474568 | tf_op jit(solution)/shard_map/ppermute | solution.py:562
  38.4 15.7 %collective-permute-start.12 = (bf16[48,5120]{1,0:T(8,128)(2,1)S(1)}, bf16[48,5120]{1,0:T(8,128)(2,1)S(1)}, u32[]{:S(2)}, u32[]{:S(2)}) collective-permute-start(bf16[48,5120]{1,0:T(8,128)(2,1)S(1)} %collective-permute-done.8.p0), channel_id=1, source_target_pairs={{0,1},{1,0},{2,3},{3,2},{4,5},{5,4},{6,7},{7,6},{8,9},{9,8},{10,11... | collective-permute-start | bytes 1474568 | tf_op jit(solution)/shard_map/ppermute | solution.py:562
  80.3 43.7 %collective-permute-start.17 = (bf16[48,5120]{1,0:T(8,128)(2,1)S(1)}, bf16[48,5120]{1,0:T(8,128)(2,1)S(1)}, u32[]{:S(2)}, u32[]{:S(2)}) collective-permute-start(bf16[48,5120]{1,0:T(8,128)(2,1)S(1)} %get-tuple-element.90), channel_id=1, source_target_pairs={{0,0},{1,67},{2,2},{3,65},{4,4},{5,71},{6,6},{7,69},{8,8},{9,75},{... | collective-permute-start | bytes 1474568 | tf_op jit(solution)/shard_map/ppermute | solution.py:562
  96.2 26.7 %collective-permute-start.18 = (bf16[48,5120]{1,0:T(8,128)(2,1)S(1)}, bf16[48,5120]{1,0:T(8,128)(2,1)S(1)}, u32[]{:S(2)}, u32[]{:S(2)}) collective-permute-start(bf16[48,5120]{1,0:T(8,128)(2,1)S(1)} %get-tuple-element.96), channel_id=1, source_target_pairs={{0,16},{1,83},{2,18},{3,81},{4,20},{5,87},{6,22},{7,85},{8,24},{9,... | collective-permute-start | bytes 1474568 | tf_op jit(solution)/shard_map/ppermute | solution.py:562
  96.3 26.6 %collective-permute-start.19 = (bf16[48,5120]{1,0:T(8,128)(2,1)S(1)}, bf16[48,5120]{1,0:T(8,128)(2,1)S(1)}, u32[]{:S(2)}, u32[]{:S(2)}) collective-permute-start(bf16[48,5120]{1,0:T(8,128)(2,1)S(1)} %get-tuple-element.97), channel_id=1, source_target_pairs={{0,32},{1,99},{2,34},{3,97},{4,36},{5,103},{6,38},{7,101},{8,40},{... | collective-permute-start | bytes 1474568 | tf_op jit(solution)/shard_map/ppermute | solution.py:562
  97.3 26.8 %collective-permute-start.20 = (bf16[48,5120]{1,0:T(8,128)(2,1)S(1)}, bf16[48,5120]{1,0:T(8,128)(2,1)S(1)}, u32[]{:S(2)}, u32[]{:S(2)}) collective-permute-start(bf16[48,5120]{1,0:T(8,128)(2,1)S(1)} %get-tuple-element.98), channel_id=1, source_target_pairs={{0,48},{1,115},{2,50},{3,113},{4,52},{5,119},{6,54},{7,117},{8,56}... | collective-permute-start | bytes 1474568 | tf_op jit(solution)/shard_map/ppermute | solution.py:562
  126.6 7.9 %collective-permute-start.23 = (bf16[48,2048]{1,0:T(8,128)(2,1)S(1)}, bf16[48,2048]{1,0:T(8,128)(2,1)S(1)}, u32[]{:S(2)}, u32[]{:S(2)}) collective-permute-start(bf16[48,2048]{1,0:T(8,128)(2,1)S(1)} %get-tuple-element.101), channel_id=1, source_target_pairs={{0,16},{1,83},{2,18},{3,81},{4,20},{5,87},{6,22},{7,85},{8,24},{9,... | collective-permute-start | bytes 589832 | tf_op jit(solution)/shard_map/ppermute | solution.py:562
  137.0 11.4 %collective-permute-start.22 = (bf16[48,2048]{1,0:T(8,128)(2,1)S(1)}, bf16[48,2048]{1,0:T(8,128)(2,1)S(1)}, u32[]{:S(2)}, u32[]{:S(2)}) collective-permute-start(bf16[48,2048]{1,0:T(8,128)(2,1)S(1)} %get-tuple-element.100), channel_id=1, source_target_pairs={{0,0},{1,67},{2,2},{3,65},{4,4},{5,71},{6,6},{7,69},{8,8},{9,75},{... | collective-permute-start | bytes 589832 | tf_op jit(solution)/shard_map/ppermute | solution.py:562
  138.9 9.9 %collective-permute-start.24 = (bf16[48,2048]{1,0:T(8,128)(2,1)S(1)}, bf16[48,2048]{1,0:T(8,128)(2,1)S(1)}, u32[]{:S(2)}, u32[]{:S(2)}) collective-permute-start(bf16[48,2048]{1,0:T(8,128)(2,1)S(1)} %get-tuple-element.102), channel_id=1, source_target_pairs={{0,32},{1,99},{2,34},{3,97},{4,36},{5,103},{6,38},{7,101},{8,40},{... | collective-permute-start | bytes 589832 | tf_op jit(solution)/shard_map/ppermute | solution.py:562
  144.5 13.6 %collective-permute-start.36 = (bf16[48,2560]{1,0:T(8,128)(2,1)S(1)}, bf16[48,2560]{1,0:T(8,128)(2,1)S(1)}, u32[]{:S(2)}, u32[]{:S(2)}) collective-permute-start(bf16[48,2560]{1,0:T(8,128)(2,1)S(1)} %add.26.refs_0_), channel_id=1, source_target_pairs={{0,12},{1,13},{2,14},{3,15},{4,0},{5,1},{6,2},{7,3},{8,4},{9,5},{1... | collective-permute-start | bytes 737288 | tf_op jit(solution)/shard_map/ppermute | solution.py:562
  147.9 10.2 %collective-permute-start.35 = (bf16[48,2560]{1,0:T(8,128)(2,1)S(1)}, bf16[48,2560]{1,0:T(8,128)(2,1)S(1)}, u32[]{:S(2)}, u32[]{:S(2)}) collective-permute-start(bf16[48,2560]{1,0:T(8,128)(2,1)S(1)} %add.26.refs_0_), channel_id=1, source_target_pairs={{0,8},{1,9},{2,10},{3,11},{4,12},{5,13},{6,14},{7,15},{8,0},{9,1},... | collective-permute-start | bytes 737288 | tf_op jit(solution)/shard_map/ppermute | solution.py:562
  148.4 13.5 %collective-permute-start.34 = (bf16[48,2560]{1,0:T(8,128)(2,1)S(1)}, bf16[48,2560]{1,0:T(8,128)(2,1)S(1)}, u32[]{:S(2)}, u32[]{:S(2)}) collective-permute-start(bf16[48,2560]{1,0:T(8,128)(2,1)S(1)} %add.26.refs_0_), channel_id=1, source_target_pairs={{0,4},{1,5},{2,6},{3,7},{4,8},{5,9},{6,10},{7,11},{8,12},{9,13},{1... | collective-permute-start | bytes 737288 | tf_op jit(solution)/shard_map/ppermute | solution.py:562
  152.4 10.3 %collective-permute-start.27 = (bf16[48,1024]{1,0:T(8,128)(2,1)S(1)}, bf16[48,1024]{1,0:T(8,128)(2,1)S(1)}, u32[]{:S(2)}, u32[]{:S(2)}) collective-permute-start(bf16[48,1024]{1,0:T(8,128)(2,1)S(1)} %add.22.refs_0_), channel_id=1, source_target_pairs={{0,2},{1,3},{2,0},{3,1},{4,6},{5,7},{6,4},{7,5},{8,10},{9,11},{10,... | collective-permute-start | bytes 294920 | tf_op jit(solution)/shard_map/ppermute | solution.py:562
  162.1 10.7 %collective-permute-start.37 = (bf16[48,2560]{1,0:T(8,128)(2,1)S(1)}, bf16[48,2560]{1,0:T(8,128)(2,1)S(1)}, u32[]{:S(2)}, u32[]{:S(2)}) collective-permute-start(bf16[48,2560]{1,0:T(8,128)(2,1)S(1)} %add.27.two_a), channel_id=1, source_target_pairs={{0,1},{1,0},{2,3},{3,2},{4,5},{5,4},{6,7},{7,6},{8,9},{9,8},{10,11... | collective-permute-start | bytes 737288 | tf_op jit(solution)/shard_map/ppermute | solution.py:562
  (14 other events, 52.6 us)

commit v3 on v2

--- a/solution.py
+++ b/solution.py
@@ -14,6 +14,7 @@
 TOK = 256
 CAP = 8
 PAIR = 2
+QUAD = 4
 CHUNK = 768
 STEPS = CAP // PAIR
 TWIN = 128
@@ -131,20 +132,20 @@
             total, ROW_MOD, 6
         )
 
-    @pl.when(PAIR * step < info[0])
+    @pl.when(QUAD * step < info[0])
     def _():
         hidden = []
-        for i in range(PAIR):
-            mod = mod_out[pl.ds(PAIR * step + i, 1), :]
+        for i in range(QUAD):
+            mod = mod_out[pl.ds(QUAD * step + i, 1), :]
             normed, _ = normalize(latents[i].astype(F32))
             hidden.append((normed * (1.0 + mod[:, D : 2 * D]) + mod[:, :D]).astype(BF))
-            hidden_out[PAIR * step + i] = hidden[i]
+            hidden_out[QUAD * step + i] = hidden[i]
         full_bias = bias_row(bias_out[0:16, :], ROW_QKV, 9)
         qkv_all = dot(jnp.concatenate(hidden, axis=0), weights[:, :QKV_W])
         qkv_all = (qkv_all + full_bias).astype(BF)
         low = lax.broadcasted_iota(jnp.int32, (TOK, 128), 1) < HEAD_DIM
-        for i in range(PAIR):
-            slot = PAIR * step + i
+        for i in range(QUAD):
+            slot = QUAD * step + i
             qkv = qkv_all[TOK * i : TOK * i + TOK]
             qkv_out[slot] = qkv
             for pair in range(HEADS // 2):
@@ -196,6 +197,8 @@
     @pl.when(PAIR * step >= info[0])
     def _():
         out[...] = jnp.zeros((PAIR, TOK, D), BF)
+        grad_mid_out[pl.ds(PAIR * step, PAIR)] = jnp.zeros((PAIR, TOK, D), F32)
+        grad_mixed_out[pl.ds(PAIR * step, PAIR)] = jnp.zeros((PAIR, TOK, D), BF)
 
     @pl.when(PAIR * step < info[0])
     def _():
@@ -310,7 +313,7 @@
     acc_qkv, acc_bias, grad_mod,
 ):
     step = pl.program_id(0)
-    slot = PAIR * step
+    slot = QUAD * step
 
     @pl.when(step == 0)
     def _():
@@ -320,14 +323,14 @@
 
     @pl.when(slot >= info[0])
     def _():
-        out[...] = jnp.zeros((PAIR, TOK, D), BF)
+        out[...] = jnp.zeros((QUAD, TOK, D), BF)
 
     @pl.when(slot < info[0])
     def _():
         low = lax.broadcasted_iota(jnp.int32, (TOK, 128), 1) < HEAD_DIM
         factor = HEAD_DIM**-0.5
         g_all = []
-        for i in range(PAIR):
+        for i in range(QUAD):
             qkv = qkv_in[slot + i]
             scaled = (grad_mixed_in[slot + i].astype(F32) * rinv_in[slot + i]).astype(BF)
             product = scaled.astype(F32) * mixed_in[slot + i].astype(F32)
@@ -356,11 +359,11 @@
                 g_value.append(jnp.where(low, d_value[:TOK], d_value[TOK:]).astype(BF))
             g_all.append(jnp.concatenate(g_query + g_key + g_value, axis=1))
         g_qkv = jnp.concatenate(g_all, axis=0)
-        hidden = hidden_in[pl.ds(slot, PAIR)].reshape(PAIR * TOK, D)
+        hidden = hidden_in[pl.ds(slot, QUAD)].reshape(QUAD * TOK, D)
         acc_qkv[...] += dot_tn(hidden, g_qkv)
         acc_bias[0:1, :] += jnp.sum(g_qkv.astype(F32), axis=0, keepdims=True)
         d_all = dot_nt(g_qkv, weights[:, :QKV_W])
-        for i in range(PAIR):
+        for i in range(QUAD):
             row = mod_in[pl.ds(slot + i, 1), :]
             normed, inverse = normalize(latents[i].astype(F32))
             d_hidden = d_all[TOK * i : TOK * i + TOK]
@@ -369,7 +372,7 @@
             back = norm_back(d_hidden * (1.0 + row[:, D : 2 * D]), normed, inverse)
             out[i] = (grad_mid_in[slot + i] + back).astype(BF)
 
-    @pl.when(step == STEPS - 1)
+    @pl.when(step == CAP // QUAD - 1)
     def _():
         cond = conditions[...].astype(F32)
         sig = 1.0 / (1.0 + jnp.exp(-cond))
@@ -401,15 +404,15 @@
             pl.when(jnp.logical_not(is_mine))(functools.partial(put, send))
 
 
-def slot_spec():
+def slot_spec(group):
     def index(j, info):
-        return (jnp.minimum(j, jnp.maximum((info[0] + 1) // 2 - 1, 0)), 0, 0)
-
-    return pl.BlockSpec((PAIR, TOK, D), index)
-
-
-def slot_out():
-    return pl.BlockSpec((PAIR, TOK, D), lambda j, info: (j, 0, 0))
+        return (jnp.minimum(j, jnp.maximum((info[0] + group - 1) // group - 1, 0)), 0, 0)
+
+    return pl.BlockSpec((group, TOK, D), index)
+
+
+def slot_out(group):
+    return pl.BlockSpec((group, TOK, D), lambda j, info: (j, 0, 0))
 
 
 def held():
@@ -440,8 +443,8 @@
         forward_kernel,
         grid_spec=pltpu.PrefetchScalarGridSpec(
             num_scalar_prefetch=1,
-            grid=(STEPS,),
-            in_specs=[slot_spec(), whole(CAP, D)] + [held()] * 8,
+            grid=(CAP // QUAD,),
+            in_specs=[slot_spec(QUAD), whole(CAP, D)] + [held()] * 8,
             out_specs=[held()] * 8,
         ),
         out_shape=[
@@ -454,7 +457,7 @@
             pltpu.VMEM((CAP, TOK, D), F32),
             pltpu.VMEM((CAP, TOK, D), BF),
         ],
-        compiler_params=params(10),
+        compiler_params=params(12),
         name="attention_forward",
         cost_estimate=pl.CostEstimate(
             flops=3_000_000_000, bytes_accessed=20_000_000, transcendentals=3_000_000
@@ -467,16 +470,16 @@
         middle_kernel,
         grid_spec=pltpu.PrefetchScalarGridSpec(
             num_scalar_prefetch=1,
-            grid=(STEPS,),
+            grid=(CAP // PAIR,),
             in_specs=[
-                slot_spec(),
+                slot_spec(PAIR),
                 whole(CAP, D),
                 held(),
-                slot_spec(),
+                slot_spec(PAIR),
                 held(),
             ]
             + [held()] * 8,
-            out_specs=[held(), slot_out()] + [held()] * 5,
+            out_specs=[held(), slot_out(PAIR)] + [held()] * 5,
             scratch_shapes=[
                 pltpu.VMEM((CAP, MOD_TWO), F32),
                 pltpu.VMEM((D, FF), F32),
@@ -508,9 +511,9 @@
         backward_kernel,
         grid_spec=pltpu.PrefetchScalarGridSpec(
             num_scalar_prefetch=1,
-            grid=(STEPS,),
-            in_specs=[slot_spec(), whole(CAP, D)] + [held()] * 11,
-            out_specs=[slot_out(), whole(CAP, D), held(), held()],
+            grid=(CAP // QUAD,),
+            in_specs=[slot_spec(QUAD), whole(CAP, D)] + [held()] * 11,
+            out_specs=[slot_out(QUAD), whole(CAP, D), held(), held()],
             scratch_shapes=[
                 pltpu.VMEM((D, QKV_W), F32),
                 pltpu.VMEM((8, QKV_W), F32),
@@ -523,7 +526,7 @@
             pltpu.VMEM((192, LANES_ONE), BF),
             pltpu.VMEM((192, LANES_ONE), BF),
         ],
-        compiler_params=params(10),
+        compiler_params=params(12),
         name="attention_backward",
         cost_estimate=pl.CostEstimate(
             flops=25_000_000_000, bytes_accessed=20_000_000, transcendentals=1_000
@@ -627,9 +630,11 @@
     return [move(block, pairs) for block, pairs in zip(blocks, back)]
 
 
-def sum_replicas(arrived, info):
+def sum_replicas(arrived, info, *earlier):
     mine, other = add_halves(info, arrived)
     total = add(mine, move(other, CORE_SWAP))
+    if earlier:
+        total = after(total, *earlier)
     total = add(total, move(total, ZLOW_SWAP))
     total = add(total, *(move(total, y_route(k)) for k in (1, 2, 3)))
     return [total, move(total, CORE_SWAP)]
@@ -676,55 +681,73 @@
     )(*map(far, values))
 
 
-def finish_kernel(
-    info, one_a, one_b, two_a, two_b, g_mod, g_mod_bias, g_qkv, g_qv_bias, g_proj, g_proj_bias,
-    g_up, g_up_bias, g_down, g_down_bias,
-):
-    shard, first = info[1] + 4 * info[2], info[3] == 0
-
-    def joined(mine, other):
-        mine, other = mine[...].astype(F32), other[...].astype(F32)
-        return jnp.concatenate(
-            [jnp.where(first, mine, other), jnp.where(first, other, mine)], axis=1
-        )
-
-    one, two = joined(one_a, one_b), joined(two_a, two_b)
-    g_mod[:, :MOD_ONE] = one[:, QKV_W:BIAS_ONE]
+def joined(info, mine, other):
+    first = info[3] == 0
+    mine, other = mine[...].astype(F32), other[...].astype(F32)
+    return jnp.concatenate([jnp.where(first, mine, other), jnp.where(first, other, mine)], axis=1)
+
+
+def unpack_two_kernel(info, mine, other, g_mod, g_proj, g_up, g_down, bias):
+    two = joined(info, mine, other)
     g_mod[:, MOD_ONE:] = two[:, AT_MOD:AT_PROJ]
-    g_qkv[...] = one[:, :QKV_W]
     g_proj[...] = two[:, AT_PROJ:AT_DOWN]
     g_up[...] = two[:, :FF]
     for q in range(4):
         g_down[48 * q : 48 * q + 48, :] = two[:, AT_DOWN + D * q : AT_DOWN + D * q + D]
-    bias = one[:, BIAS_ONE:] + two[:, BIAS_TWO:]
-
-    def own(first_row, count, size, out):
-        row = bias_row(bias, first_row, count)
-        row = jnp.broadcast_to(row, (8, 128 * count))
+    bias[...] = two[:, BIAS_TWO:]
+
+
+def unpack_one_kernel(
+    info, mine, other, bias_two, _, g_mod, g_mod_bias, g_qkv, g_qv_bias, g_proj_bias, g_up_bias,
+    g_down_bias,
+):
+    shard = info[1] + 4 * info[2]
+    one = joined(info, mine, other)
+    g_mod[...] = one[:, QKV_W:BIAS_ONE]
+    g_qkv[...] = one[:, :QKV_W]
+    bias = one[:, BIAS_ONE:] + bias_two[...]
+
+    def own(row, size, out):
+        row = jnp.broadcast_to(row, (8, row.shape[1]))
         turn = lax.rem(8 * size - shard * size, 8 * size)
         out[...] = pltpu.roll(row, turn, 1)[0:1, :size].reshape(size)
 
-    own(ROW_MOD, 18, 288, g_mod_bias)
-    query, value = bias_row(bias, 0, 3), bias_row(bias, 6, 3)
-    row = jnp.broadcast_to(jnp.concatenate([query, value], axis=1), (8, 2 * D))
-    turn = lax.rem(2 * D - shard * 96, 2 * D)
-    g_qv_bias[...] = pltpu.roll(row, turn, 1)[0:1, :96].reshape(96)
-    own(ROW_PROJ, 3, 48, g_proj_bias)
-    own(ROW_UP, 12, 192, g_up_bias)
-    own(ROW_DOWN, 3, 48, g_down_bias)
-
-
-def finish(info, parts):
-    shapes = [
-        (48, 6 * D), (288,), (48, QKV_W), (96,), (48, D), (48,), (48, FF), (192,), (192, D), (48,),
-    ]
-    return pl.pallas_call(
-        finish_kernel,
-        in_specs=[pl.BlockSpec(memory_space=pltpu.SMEM)] + [held()] * 4,
+    own(bias_row(bias, ROW_MOD, 18), 288, g_mod_bias)
+    own(jnp.concatenate([bias_row(bias, 0, 3), bias_row(bias, 6, 3)], axis=1), 96, g_qv_bias)
+    own(bias_row(bias, ROW_PROJ, 3), 48, g_proj_bias)
+    own(bias_row(bias, ROW_UP, 12), 192, g_up_bias)
+    own(bias_row(bias, ROW_DOWN, 3), 48, g_down_bias)
+
+
+def finish(info, one, two):
+    scalars = pl.BlockSpec(memory_space=pltpu.SMEM)
+    shapes = [(48, 6 * D), (48, D), (48, FF), (192, D), (48, 128)]
+    g_mod, g_proj, g_up, g_down, bias_two = pl.pallas_call(
+        unpack_two_kernel,
+        in_specs=[scalars] + [held()] * 2,
         out_shape=[jax.ShapeDtypeStruct(shape, F32) for shape in shapes],
         compiler_params=pltpu.CompilerParams(vmem_limit_bytes=12 * MIB),
-        name="unpack_gradients",
-    )(info, *parts)
+        name="unpack_second_batch",
+    )(info, *two)
+    shapes = [(48, 6 * D), (288,), (48, QKV_W), (96,), (48,), (192,), (48,)]
+
+    def once(shape):
+        return pl.BlockSpec(shape, lambda j: (0,) * len(shape))
+
+    g_mod, g_mod_bias, g_qkv, g_qv_bias, g_proj_bias, g_up_bias, g_down_bias = pl.pallas_call(
+        unpack_one_kernel,
+        grid=(1,),
+        in_specs=[scalars] + [held()] * 3 + [pl.BlockSpec(memory_space=pl.ANY)],
+        out_specs=[once((48, MOD_ONE))] + [once(shape) for shape in shapes[1:]],
+        out_shape=[jax.ShapeDtypeStruct(shape, F32) for shape in shapes],
+        input_output_aliases={4: 0},
+        compiler_params=pltpu.CompilerParams(vmem_limit_bytes=8 * MIB),
+        name="unpack_first_batch",
+    )(info, *one, bias_two, g_mod)
+    return (
+        g_mod, g_mod_bias, g_qkv, g_qv_bias, g_proj, g_proj_bias, g_up, g_up_bias, g_down,
+        g_down_bias,
+    )
 
 
 def on_device(
@@ -763,9 +786,9 @@
     )
     held_one = add_blocks(keep_one, move(after(send_one, *arrived_two), CORE_SWAP))
     arrived_one = scatter(held_one)
-    two = sum_replicas([after(arrived_two[0], arrived_one[1]), *arrived_two[1:]], info)
+    two = sum_replicas(arrived_two, info, *held_one)
     one = sum_replicas(arrived_one, info)
-    return (out, grad_latents, grad_cond, *finish(info, one + two))
+    return (out, grad_latents, grad_cond, *finish(info, one, two))
 
 
 def solution(mesh):

time: 175 us -> 166 us (0.949)
  Pallas kernels: 44.6 us -> 70.8 us
  waiting for transfers between devices: 68.7 us -> 43.4 us
  starting transfers between devices: 59.6 us -> 50.2 us
    ppermute x38, waiting for transfers between devices: 68.7 us -> 43.4 us  [move(): return lax.ppermute(value, BOTH, pairs)]
    pallas_call x1, Pallas kernels: 18.9 us -> 32.3 us  [run_middle(): pl.pallas_call(middle_kernel, grid_spec=pltpu.PrefetchScalarGridSpec(num_...]
    ppermute x38, starting transfers between devices: 59.6 us -> 50.2 us  [move(): return lax.ppermute(value, BOTH, pairs)]
    pallas_call x1, Pallas kernels: 13 us -> 21.3 us  [run_backward(): pl.pallas_call(backward_kernel, grid_spec=pltpu.PrefetchScalarGridSpec(nu...]
    pallas_call x1, Pallas kernels: 6.23 us -> 9.63 us  [run_forward(): pl.pallas_call(forward_kernel, grid_spec=pltpu.PrefetchScalarGridSpec(num...]
  transfers between devices with their start and end apart: 38 -> 38, of which waited for: 22 -> 18; matrix products, arithmetic and copies ran while one was open for 0% -> 0% of each run, Pallas kernels for 12% -> 21%
where the time goes in v3:
time: 166 us
  Pallas kernels  70.8 us (43%)
  starting transfers between devices  50.2 us (30%)
  waiting for transfers between devices  43.4 us (26%)
    ppermute x38, starting transfers between devices, move(): return lax.ppermute(value, BOTH, pairs)  50.2 us
    ppermute x38, waiting for transfers between devices, move(): return lax.ppermute(value, BOTH, pairs)  43.4 us
    pallas_call x1, Pallas kernels, run_middle(): pl.pallas_call(middle_kernel, grid_spec=pltpu.PrefetchScalarGridSpec(num_...  32.3 us
    pallas_call x1, Pallas kernels, run_backward(): pl.pallas_call(backward_kernel, grid_spec=pltpu.PrefetchScalarGridSpec(nu...  21.3 us
    pallas_call x1, Pallas kernels, run_forward(): pl.pallas_call(forward_kernel, grid_spec=pltpu.PrefetchScalarGridSpec(num...  9.63 us
  transfers between devices with their start and end apart: 38, of which 18 were waited for; matrix products, arithmetic and copies ran while one was open for 0% of the time, Pallas kernels for 21%

profile of v3, /device:TPU:1, one launch (start us, length us, event | category | flops | bytes accessed | tf_op | source)
XLA Modules:
  0.0 166.0 jit_solution(5149890092152184105)
XLA Ops:
  2.5 6.5 %collective-permute-start = (bf16[48,2048]{1,0:T(8,128)(2,1)S(1)}, bf16[48,2048]{1,0:T(8,128)(2,1)S(1)}, u32[]{:S(2)}, u32[]{:S(2)}) collective-permute-start(bf16[48,2048]{1,0:T(8,128)(2,1)S(1)} %pack_attention_weights.1), channel_id=1, source_target_pairs={{0,0},{67,1},{2,2},{65,3},{4,4},{71,5},{6,6},{69,7},{8,8},{75,9},{... | collective-permute-start | bytes 589832 | tf_op jit(solution)/shard_map/ppermute | solution.py:565
  9.0 2.3 %collective-permute-start.1 = (bf16[48,2048]{1,0:T(8,128)(2,1)S(1)}, bf16[48,2048]{1,0:T(8,128)(2,1)S(1)}, u32[]{:S(2)}, u32[]{:S(2)}) collective-permute-start(bf16[48,2048]{1,0:T(8,128)(2,1)S(1)} %pack_attention_weights.1), channel_id=1, source_target_pairs={{16,0},{83,1},{18,2},{81,3},{20,4},{87,5},{22,6},{85,7},{24,8},{91... | collective-permute-start | bytes 589832 | tf_op jit(solution)/shard_map/ppermute | solution.py:565
  11.2 2.9 %collective-permute-start.2 = (bf16[48,2048]{1,0:T(8,128)(2,1)S(1)}, bf16[48,2048]{1,0:T(8,128)(2,1)S(1)}, u32[]{:S(2)}, u32[]{:S(2)}) collective-permute-start(bf16[48,2048]{1,0:T(8,128)(2,1)S(1)} %pack_attention_weights.1), channel_id=1, source_target_pairs={{32,0},{99,1},{34,2},{97,3},{36,4},{103,5},{38,6},{101,7},{40,8},{... | collective-permute-start | bytes 589832 | tf_op jit(solution)/shard_map/ppermute | solution.py:565
  15.7 2.0 %collective-permute-done.1.p1 = bf16[48,2048]{1,0:T(8,128)(2,1)S(1)} collective-permute-done((bf16[48,2048]{1,0:T(8,128)(2,1)S(1)}, bf16[48,2048]{1,0:T(8,128)(2,1)S(1)}, u32[]{:S(2)}, u32[]{:S(2)}) %collective-permute-start.1) | collective-permute-done | bytes 196640 | tf_op jit(solution)/shard_map/ppermute | solution.py:565
  17.8 3.8 %collective-permute-done.2.p2 = bf16[48,2048]{1,0:T(8,128)(2,1)S(1)} collective-permute-done((bf16[48,2048]{1,0:T(8,128)(2,1)S(1)}, bf16[48,2048]{1,0:T(8,128)(2,1)S(1)}, u32[]{:S(2)}, u32[]{:S(2)}) %collective-permute-start.2) | collective-permute-done | bytes 196640 | tf_op jit(solution)/shard_map/ppermute | solution.py:565
  21.6 2.5 %collective-permute-start.8 = (bf16[48,5120]{1,0:T(8,128)(2,1)S(1)}, bf16[48,5120]{1,0:T(8,128)(2,1)S(1)}, u32[]{:S(2)}, u32[]{:S(2)}) collective-permute-start(bf16[48,5120]{1,0:T(8,128)(2,1)S(1)} %pack_feed_forward_weights.1), channel_id=1, source_target_pairs={{0,0},{67,1},{2,2},{65,3},{4,4},{71,5},{6,6},{69,7},{8,8},{75,9},{... | collective-permute-start | bytes 1474568 | tf_op jit(solution)/shard_map/ppermute | solution.py:565
  24.1 2.9 %collective-permute-start.11 = (bf16[48,5120]{1,0:T(8,128)(2,1)S(1)}, bf16[48,5120]{1,0:T(8,128)(2,1)S(1)}, u32[]{:S(2)}, u32[]{:S(2)}) collective-permute-start(bf16[48,5120]{1,0:T(8,128)(2,1)S(1)} %pack_feed_forward_weights.1), channel_id=1, source_target_pairs={{48,0},{115,1},{50,2},{113,3},{52,4},{119,5},{54,6},{117,7},{56,8}... | collective-permute-start | bytes 1474568 | tf_op jit(solution)/shard_map/ppermute | solution.py:565
  27.0 3.1 %collective-permute-start.10 = (bf16[48,5120]{1,0:T(8,128)(2,1)S(1)}, bf16[48,5120]{1,0:T(8,128)(2,1)S(1)}, u32[]{:S(2)}, u32[]{:S(2)}) collective-permute-start(bf16[48,5120]{1,0:T(8,128)(2,1)S(1)} %pack_feed_forward_weights.1), channel_id=1, source_target_pairs={{32,0},{99,1},{34,2},{97,3},{36,4},{103,5},{38,6},{101,7},{40,8},{... | collective-permute-start | bytes 1474568 | tf_op jit(solution)/shard_map/ppermute | solution.py:565
  32.2 9.6 %attention_forward.1 = (bf16[384,2048]{1,0:T(8,128)(2,1)S(1)}, f32[48,128]{1,0:T(8,128)S(1)}, f32[8,768]{1,0:T(8,128)S(1)}, bf16[8,256,1152]{2,1,0:T(8,128)(2,1)...) custom-call(s32[4]{0:T(128)S(1)} %pad_add_fusion.info, ...), custom_call_target="tpu_custom_call" | custom-call | flops 3000000000 | bytes 20000000 | tf_op jit(solution)/shard_map/attention_forward/pallas_call | solution.py:442
  41.9 9.7 %collective-permute-done.11.p3 = bf16[48,5120]{1,0:T(8,128)(2,1)S(1)} collective-permute-done((bf16[48,5120]{1,0:T(8,128)(2,1)S(1)}, bf16[48,5120]{1,0:T(8,128)(2,1)S(1)}, u32[]{:S(2)}, u32[]{:S(2)}) %collective-permute-start.11) | collective-permute-done | bytes 491552 | tf_op jit(solution)/shard_map/ppermute | solution.py:565
  51.6 2.0 %collective-permute-done.9.p1 = bf16[48,5120]{1,0:T(8,128)(2,1)S(1)} collective-permute-done((bf16[48,5120]{1,0:T(8,128)(2,1)S(1)}, bf16[48,5120]{1,0:T(8,128)(2,1)S(1)}, u32[]{:S(2)}, u32[]{:S(2)}) %collective-permute-start.9) | collective-permute-done | bytes 491552 | tf_op jit(solution)/shard_map/ppermute | solution.py:565
  56.9 32.3 %feed_forward_both_ways.1 = (bf16[384,5120]{1,0:T(8,128)(2,1)S(1)}, bf16[8,256,384]{2,1,0:T(8,128)(2,1)}, f32[8,256,384]{2,1,0:T(8,128)S(1)}, bf16[8,256,384]{2,...) custom-call(s32[4]{0:T(128)S(1)} %pad_add_fusion.info, ...), custom_call_target="tpu_custom_call" | custom-call | flops 16000000000 | bytes 30000000 | tf_op jit(solution)/shard_map/feed_forward_both_ways/pallas_call | solution.py:469
  89.2 4.0 %collective-permute-done.16.right = bf16[192,5120]{1,0:T(8,128)(2,1)S(1)} collective-permute-done((bf16[192,5120]{1,0:T(8,128)(2,1)S(1)}, bf16[192,5120]{1,0:T(8,128)(2,1)S(1)}, u32[]{:S(2)}, u32[]{:S(2)}) %collective-permute-start.16) | collective-permute-done | bytes 1966112 | tf_op jit(solution)/shard_map/ppermute | solution.py:565
  93.6 2.9 %collective-permute-start.17 = (bf16[48,5120]{1,0:T(8,128)(2,1)S(1)}, bf16[48,5120]{1,0:T(8,128)(2,1)S(1)}, u32[]{:S(2)}, u32[]{:S(2)}) collective-permute-start(bf16[48,5120]{1,0:T(8,128)(2,1)S(1)} %get-tuple-element.92), channel_id=1, source_target_pairs={{0,0},{1,67},{2,2},{3,65},{4,4},{5,71},{6,6},{7,69},{8,8},{9,75},{... | collective-permute-start | bytes 1474568 | tf_op jit(solution)/shard_map/ppermute | solution.py:565
  97.6 3.8 %collective-permute-start.20 = (bf16[48,5120]{1,0:T(8,128)(2,1)S(1)}, bf16[48,5120]{1,0:T(8,128)(2,1)S(1)}, u32[]{:S(2)}, u32[]{:S(2)}) collective-permute-start(bf16[48,5120]{1,0:T(8,128)(2,1)S(1)} %get-tuple-element.100), channel_id=1, source_target_pairs={{0,48},{1,115},{2,50},{3,113},{4,52},{5,119},{6,54},{7,117},{8,56}... | collective-permute-start | bytes 1474568 | tf_op jit(solution)/shard_map/ppermute | solution.py:565
  101.4 21.3 %attention_backward.1 = (bf16[8,256,384]{2,1,0:T(8,128)(2,1)}, bf16[8,384]{1,0:T(8,128)(2,1)}, bf16[192,2048]{1,0:T(8,128)(2,1)S(1)}, bf16[192,2048]{1,0:T(8,128)(2,1)S(1)}) custom-call(s32[4]{0:T(128)S(1)} %pad_add_fusion.info, bf16[8,256,384]{2,1,0:T(8,128)(2,1)} %latents.5, bf16[8,384]{1,0:T(8,128)(2,1)} %conditions.5, ...), custom_call_target="tpu_custom_call" | custom-call | flops 24999999488 | bytes 20000000 | tf_op jit(solution)/shard_map/attention_backward/pallas_call | solution.py:510
  126.8 5.3 %collective-permute-start.22 = (bf16[48,2048]{1,0:T(8,128)(2,1)S(1)}, bf16[48,2048]{1,0:T(8,128)(2,1)S(1)}, u32[]{:S(2)}, u32[]{:S(2)}) collective-permute-start(bf16[48,2048]{1,0:T(8,128)(2,1)S(1)} %get-tuple-element.102), channel_id=1, source_target_pairs={{0,0},{1,67},{2,2},{3,65},{4,4},{5,71},{6,6},{7,69},{8,8},{9,75},{... | collective-permute-start | bytes 589832 | tf_op jit(solution)/shard_map/ppermute | solution.py:565
  133.5 3.5 %collective-permute-start.25 = (bf16[48,2048]{1,0:T(8,128)(2,1)S(1)}, bf16[48,2048]{1,0:T(8,128)(2,1)S(1)}, u32[]{:S(2)}, u32[]{:S(2)}) collective-permute-start(bf16[48,2048]{1,0:T(8,128)(2,1)S(1)} %get-tuple-element.105), channel_id=1, source_target_pairs={{0,48},{1,115},{2,50},{3,113},{4,52},{5,119},{6,54},{7,117},{8,56}... | collective-permute-start | bytes 589832 | tf_op jit(solution)/shard_map/ppermute | solution.py:565
  138.1 2.0 %collective-permute-start.35 = (bf16[48,2560]{1,0:T(8,128)(2,1)S(1)}, bf16[48,2560]{1,0:T(8,128)(2,1)S(1)}, u32[]{:S(2)}, u32[]{:S(2)}) collective-permute-start(bf16[48,2560]{1,0:T(8,128)(2,1)S(1)} %add.26.refs_0_), channel_id=1, source_target_pairs={{0,8},{1,9},{2,10},{3,11},{4,12},{5,13},{6,14},{7,15},{8,0},{9,1},... | collective-permute-start | bytes 737288 | tf_op jit(solution)/shard_map/ppermute | solution.py:565
  140.1 4.5 %collective-permute-done.23.refs_1_ = bf16[48,2048]{1,0:T(8,128)(2,1)S(1)} collective-permute-done((bf16[48,2048]{1,0:T(8,128)(2,1)S(1)}, bf16[48,2048]{1,0:T(8,128)(2,1)S(1)}, u32[]{:S(2)}, u32[]{:S(2)}) %collective-permute-start.23) | collective-permute-done | bytes 196640 | tf_op jit(solution)/shard_map/ppermute | solution.py:565
  148.6 2.9 %collective-permute-done.34.refs_1_ = bf16[48,2560]{1,0:T(8,128)(2,1)S(1)} collective-permute-done((bf16[48,2560]{1,0:T(8,128)(2,1)S(1)}, bf16[48,2560]{1,0:T(8,128)(2,1)S(1)}, u32[]{:S(2)}, u32[]{:S(2)}) %collective-permute-start.34) | collective-permute-done | bytes 245792 | tf_op jit(solution)/shard_map/ppermute | solution.py:565
  153.7 1.8 %collective-permute-start.29 = (bf16[48,1024]{1,0:T(8,128)(2,1)S(1)}, bf16[48,1024]{1,0:T(8,128)(2,1)S(1)}, u32[]{:S(2)}, u32[]{:S(2)}) collective-permute-start(bf16[48,1024]{1,0:T(8,128)(2,1)S(1)} %add.23.refs_0_), channel_id=1, source_target_pairs={{0,8},{1,9},{2,10},{3,11},{4,12},{5,13},{6,14},{7,15},{8,0},{9,1},... | collective-permute-start | bytes 294920 | tf_op jit(solution)/shard_map/ppermute | solution.py:565
  155.7 3.0 %collective-permute-done.29.refs_2_ = bf16[48,1024]{1,0:T(8,128)(2,1)S(1)} collective-permute-done((bf16[48,1024]{1,0:T(8,128)(2,1)S(1)}, bf16[48,1024]{1,0:T(8,128)(2,1)S(1)}, u32[]{:S(2)}, u32[]{:S(2)}) %collective-permute-start.29) | collective-permute-done | bytes 98336 | tf_op jit(solution)/shard_map/ppermute | solution.py:565
  158.7 3.1 %collective-permute-done.28.refs_1_ = bf16[48,1024]{1,0:T(8,128)(2,1)S(1)} collective-permute-done((bf16[48,1024]{1,0:T(8,128)(2,1)S(1)}, bf16[48,1024]{1,0:T(8,128)(2,1)S(1)}, u32[]{:S(2)}, u32[]{:S(2)}) %collective-permute-start.28) | collective-permute-done | bytes 98336 | tf_op jit(solution)/shard_map/ppermute | solution.py:565
  (70 shorter events, 26.9 us)
Async XLA Ops:
  2.5 13.2 %collective-permute-start = (bf16[48,2048]{1,0:T(8,128)(2,1)S(1)}, bf16[48,2048]{1,0:T(8,128)(2,1)S(1)}, u32[]{:S(2)}, u32[]{:S(2)}) collective-permute-start(bf16[48,2048]{1,0:T(8,128)(2,1)S(1)} %pack_attention_weights.1), channel_id=1, source_target_pairs={{0,0},{67,1},{2,2},{65,3},{4,4},{71,5},{6,6},{69,7},{8,8},{75,9},{... | collective-permute-start | bytes 589832 | tf_op jit(solution)/shard_map/ppermute | solution.py:565
  9.0 8.8 %collective-permute-start.1 = (bf16[48,2048]{1,0:T(8,128)(2,1)S(1)}, bf16[48,2048]{1,0:T(8,128)(2,1)S(1)}, u32[]{:S(2)}, u32[]{:S(2)}) collective-permute-start(bf16[48,2048]{1,0:T(8,128)(2,1)S(1)} %pack_attention_weights.1), channel_id=1, source_target_pairs={{16,0},{83,1},{18,2},{81,3},{20,4},{87,5},{22,6},{85,7},{24,8},{91... | collective-permute-start | bytes 589832 | tf_op jit(solution)/shard_map/ppermute | solution.py:565
  11.2 10.3 %collective-permute-start.2 = (bf16[48,2048]{1,0:T(8,128)(2,1)S(1)}, bf16[48,2048]{1,0:T(8,128)(2,1)S(1)}, u32[]{:S(2)}, u32[]{:S(2)}) collective-permute-start(bf16[48,2048]{1,0:T(8,128)(2,1)S(1)} %pack_attention_weights.1), channel_id=1, source_target_pairs={{32,0},{99,1},{34,2},{97,3},{36,4},{103,5},{38,6},{101,7},{40,8},{... | collective-permute-start | bytes 589832 | tf_op jit(solution)/shard_map/ppermute | solution.py:565
  14.1 9.9 %collective-permute-start.3 = (bf16[48,2048]{1,0:T(8,128)(2,1)S(1)}, bf16[48,2048]{1,0:T(8,128)(2,1)S(1)}, u32[]{:S(2)}, u32[]{:S(2)}) collective-permute-start(bf16[48,2048]{1,0:T(8,128)(2,1)S(1)} %pack_attention_weights.1), channel_id=1, source_target_pairs={{48,0},{115,1},{50,2},{113,3},{52,4},{119,5},{54,6},{117,7},{56,8}... | collective-permute-start | bytes 589832 | tf_op jit(solution)/shard_map/ppermute | solution.py:565
  15.6 11.3 %collective-permute-start.4 = (bf16[48,2048]{1,0:T(8,128)(2,1)S(1)}, bf16[48,2048]{1,0:T(8,128)(2,1)S(1)}, u32[]{:S(2)}, u32[]{:S(2)}) collective-permute-start(bf16[48,2048]{1,0:T(8,128)(2,1)S(1)} %collective-permute-done.p0), channel_id=1, source_target_pairs={{0,1},{1,0},{2,3},{3,2},{4,5},{5,4},{6,7},{7,6},{8,9},{9,8},{10,11... | collective-permute-start | bytes 589832 | tf_op jit(solution)/shard_map/ppermute | solution.py:565
  17.8 12.3 %collective-permute-start.5 = (bf16[48,2048]{1,0:T(8,128)(2,1)S(1)}, bf16[48,2048]{1,0:T(8,128)(2,1)S(1)}, u32[]{:S(2)}, u32[]{:S(2)}) collective-permute-start(bf16[48,2048]{1,0:T(8,128)(2,1)S(1)} %collective-permute-done.1.p1), channel_id=1, source_target_pairs={{0,1},{1,0},{2,3},{3,2},{4,5},{5,4},{6,7},{7,6},{8,9},{9,8},{10,11... | collective-permute-start | bytes 589832 | tf_op jit(solution)/shard_map/ppermute | solution.py:565
  21.6 9.2 %collective-permute-start.6 = (bf16[48,2048]{1,0:T(8,128)(2,1)S(1)}, bf16[48,2048]{1,0:T(8,128)(2,1)S(1)}, u32[]{:S(2)}, u32[]{:S(2)}) collective-permute-start(bf16[48,2048]{1,0:T(8,128)(2,1)S(1)} %collective-permute-done.2.p2), channel_id=1, source_target_pairs={{0,1},{1,0},{2,3},{3,2},{4,5},{5,4},{6,7},{7,6},{8,9},{9,8},{10,11... | collective-permute-start | bytes 589832 | tf_op jit(solution)/shard_map/ppermute | solution.py:565
  21.6 20.3 %collective-permute-start.8 = (bf16[48,5120]{1,0:T(8,128)(2,1)S(1)}, bf16[48,5120]{1,0:T(8,128)(2,1)S(1)}, u32[]{:S(2)}, u32[]{:S(2)}) collective-permute-start(bf16[48,5120]{1,0:T(8,128)(2,1)S(1)} %pack_feed_forward_weights.1), channel_id=1, source_target_pairs={{0,0},{67,1},{2,2},{65,3},{4,4},{71,5},{6,6},{69,7},{8,8},{75,9},{... | collective-permute-start | bytes 1474568 | tf_op jit(solution)/shard_map/ppermute | solution.py:565
  24.1 27.5 %collective-permute-start.11 = (bf16[48,5120]{1,0:T(8,128)(2,1)S(1)}, bf16[48,5120]{1,0:T(8,128)(2,1)S(1)}, u32[]{:S(2)}, u32[]{:S(2)}) collective-permute-start(bf16[48,5120]{1,0:T(8,128)(2,1)S(1)} %pack_feed_forward_weights.1), channel_id=1, source_target_pairs={{48,0},{115,1},{50,2},{113,3},{52,4},{119,5},{54,6},{117,7},{56,8}... | collective-permute-start | bytes 1474568 | tf_op jit(solution)/shard_map/ppermute | solution.py:565
  27.0 24.6 %collective-permute-start.10 = (bf16[48,5120]{1,0:T(8,128)(2,1)S(1)}, bf16[48,5120]{1,0:T(8,128)(2,1)S(1)}, u32[]{:S(2)}, u32[]{:S(2)}) collective-permute-start(bf16[48,5120]{1,0:T(8,128)(2,1)S(1)} %pack_feed_forward_weights.1), channel_id=1, source_target_pairs={{32,0},{99,1},{34,2},{97,3},{36,4},{103,5},{38,6},{101,7},{40,8},{... | collective-permute-start | bytes 1474568 | tf_op jit(solution)/shard_map/ppermute | solution.py:565
  30.1 23.5 %collective-permute-start.9 = (bf16[48,5120]{1,0:T(8,128)(2,1)S(1)}, bf16[48,5120]{1,0:T(8,128)(2,1)S(1)}, u32[]{:S(2)}, u32[]{:S(2)}) collective-permute-start(bf16[48,5120]{1,0:T(8,128)(2,1)S(1)} %pack_feed_forward_weights.1), channel_id=1, source_target_pairs={{16,0},{83,1},{18,2},{81,3},{20,4},{87,5},{22,6},{85,7},{24,8},{91... | collective-permute-start | bytes 1474568 | tf_op jit(solution)/shard_map/ppermute | solution.py:565
  41.8 12.3 %collective-permute-start.12 = (bf16[48,5120]{1,0:T(8,128)(2,1)S(1)}, bf16[48,5120]{1,0:T(8,128)(2,1)S(1)}, u32[]{:S(2)}, u32[]{:S(2)}) collective-permute-start(bf16[48,5120]{1,0:T(8,128)(2,1)S(1)} %collective-permute-done.8.p0), channel_id=1, source_target_pairs={{0,1},{1,0},{2,3},{3,2},{4,5},{5,4},{6,7},{7,6},{8,9},{9,8},{10,11... | collective-permute-start | bytes 1474568 | tf_op jit(solution)/shard_map/ppermute | solution.py:565
  93.6 30.2 %collective-permute-start.17 = (bf16[48,5120]{1,0:T(8,128)(2,1)S(1)}, bf16[48,5120]{1,0:T(8,128)(2,1)S(1)}, u32[]{:S(2)}, u32[]{:S(2)}) collective-permute-start(bf16[48,5120]{1,0:T(8,128)(2,1)S(1)} %get-tuple-element.92), channel_id=1, source_target_pairs={{0,0},{1,67},{2,2},{3,65},{4,4},{5,71},{6,6},{7,69},{8,8},{9,75},{... | collective-permute-start | bytes 1474568 | tf_op jit(solution)/shard_map/ppermute | solution.py:565
  96.5 26.2 %collective-permute-start.18 = (bf16[48,5120]{1,0:T(8,128)(2,1)S(1)}, bf16[48,5120]{1,0:T(8,128)(2,1)S(1)}, u32[]{:S(2)}, u32[]{:S(2)}) collective-permute-start(bf16[48,5120]{1,0:T(8,128)(2,1)S(1)} %get-tuple-element.98), channel_id=1, source_target_pairs={{0,16},{1,83},{2,18},{3,81},{4,20},{5,87},{6,22},{7,85},{8,24},{9,... | collective-permute-start | bytes 1474568 | tf_op jit(solution)/shard_map/ppermute | solution.py:565
  96.6 26.1 %collective-permute-start.19 = (bf16[48,5120]{1,0:T(8,128)(2,1)S(1)}, bf16[48,5120]{1,0:T(8,128)(2,1)S(1)}, u32[]{:S(2)}, u32[]{:S(2)}) collective-permute-start(bf16[48,5120]{1,0:T(8,128)(2,1)S(1)} %get-tuple-element.99), channel_id=1, source_target_pairs={{0,32},{1,99},{2,34},{3,97},{4,36},{5,103},{6,38},{7,101},{8,40},{... | collective-permute-start | bytes 1474568 | tf_op jit(solution)/shard_map/ppermute | solution.py:565
  97.6 26.3 %collective-permute-start.20 = (bf16[48,5120]{1,0:T(8,128)(2,1)S(1)}, bf16[48,5120]{1,0:T(8,128)(2,1)S(1)}, u32[]{:S(2)}, u32[]{:S(2)}) collective-permute-start(bf16[48,5120]{1,0:T(8,128)(2,1)S(1)} %get-tuple-element.100), channel_id=1, source_target_pairs={{0,48},{1,115},{2,50},{3,113},{4,52},{5,119},{6,54},{7,117},{8,56}... | collective-permute-start | bytes 1474568 | tf_op jit(solution)/shard_map/ppermute | solution.py:565
  126.8 10.2 %collective-permute-start.33 = (bf16[48,2560]{1,0:T(8,128)(2,1)S(1)}, bf16[48,2560]{1,0:T(8,128)(2,1)S(1)}, u32[]{:S(2)}, u32[]{:S(2)}) collective-permute-start(bf16[48,2560]{1,0:T(8,128)(2,1)S(1)} %add.25.refs_0_), channel_id=1, source_target_pairs={{0,2},{1,3},{2,0},{3,1},{4,6},{5,7},{6,4},{7,5},{8,10},{9,11},{10,... | collective-permute-start | bytes 737288 | tf_op jit(solution)/shard_map/ppermute | solution.py:565
  126.8 11.3 %collective-permute-start.22 = (bf16[48,2048]{1,0:T(8,128)(2,1)S(1)}, bf16[48,2048]{1,0:T(8,128)(2,1)S(1)}, u32[]{:S(2)}, u32[]{:S(2)}) collective-permute-start(bf16[48,2048]{1,0:T(8,128)(2,1)S(1)} %get-tuple-element.102), channel_id=1, source_target_pairs={{0,0},{1,67},{2,2},{3,65},{4,4},{5,71},{6,6},{7,69},{8,8},{9,75},{... | collective-permute-start | bytes 589832 | tf_op jit(solution)/shard_map/ppermute | solution.py:565
  132.1 12.4 %collective-permute-start.23 = (bf16[48,2048]{1,0:T(8,128)(2,1)S(1)}, bf16[48,2048]{1,0:T(8,128)(2,1)S(1)}, u32[]{:S(2)}, u32[]{:S(2)}) collective-permute-start(bf16[48,2048]{1,0:T(8,128)(2,1)S(1)} %get-tuple-element.103), channel_id=1, source_target_pairs={{0,16},{1,83},{2,18},{3,81},{4,20},{5,87},{6,22},{7,85},{8,24},{9,... | collective-permute-start | bytes 589832 | tf_op jit(solution)/shard_map/ppermute | solution.py:565
  132.2 13.5 %collective-permute-start.24 = (bf16[48,2048]{1,0:T(8,128)(2,1)S(1)}, bf16[48,2048]{1,0:T(8,128)(2,1)S(1)}, u32[]{:S(2)}, u32[]{:S(2)}) collective-permute-start(bf16[48,2048]{1,0:T(8,128)(2,1)S(1)} %get-tuple-element.104), channel_id=1, source_target_pairs={{0,32},{1,99},{2,34},{3,97},{4,36},{5,103},{6,38},{7,101},{8,40},{... | collective-permute-start | bytes 589832 | tf_op jit(solution)/shard_map/ppermute | solution.py:565
  133.5 12.3 %collective-permute-start.25 = (bf16[48,2048]{1,0:T(8,128)(2,1)S(1)}, bf16[48,2048]{1,0:T(8,128)(2,1)S(1)}, u32[]{:S(2)}, u32[]{:S(2)}) collective-permute-start(bf16[48,2048]{1,0:T(8,128)(2,1)S(1)} %get-tuple-element.105), channel_id=1, source_target_pairs={{0,48},{1,115},{2,50},{3,113},{4,52},{5,119},{6,54},{7,117},{8,56}... | collective-permute-start | bytes 589832 | tf_op jit(solution)/shard_map/ppermute | solution.py:565
  137.0 11.6 %collective-permute-start.36 = (bf16[48,2560]{1,0:T(8,128)(2,1)S(1)}, bf16[48,2560]{1,0:T(8,128)(2,1)S(1)}, u32[]{:S(2)}, u32[]{:S(2)}) collective-permute-start(bf16[48,2560]{1,0:T(8,128)(2,1)S(1)} %add.26.refs_0_), channel_id=1, source_target_pairs={{0,12},{1,13},{2,14},{3,15},{4,0},{5,1},{6,2},{7,3},{8,4},{9,5},{1... | collective-permute-start | bytes 737288 | tf_op jit(solution)/shard_map/ppermute | solution.py:565
  138.1 10.5 %collective-permute-start.35 = (bf16[48,2560]{1,0:T(8,128)(2,1)S(1)}, bf16[48,2560]{1,0:T(8,128)(2,1)S(1)}, u32[]{:S(2)}, u32[]{:S(2)}) collective-permute-start(bf16[48,2560]{1,0:T(8,128)(2,1)S(1)} %add.26.refs_0_), channel_id=1, source_target_pairs={{0,8},{1,9},{2,10},{3,11},{4,12},{5,13},{6,14},{7,15},{8,0},{9,1},... | collective-permute-start | bytes 737288 | tf_op jit(solution)/shard_map/ppermute | solution.py:565
  151.7 11.4 %collective-permute-start.37 = (bf16[48,2560]{1,0:T(8,128)(2,1)S(1)}, bf16[48,2560]{1,0:T(8,128)(2,1)S(1)}, u32[]{:S(2)}, u32[]{:S(2)}) collective-permute-start(bf16[48,2560]{1,0:T(8,128)(2,1)S(1)} %add.27.mine), channel_id=1, source_target_pairs={{0,1},{1,0},{2,3},{3,2},{4,5},{5,4},{6,7},{7,6},{8,9},{9,8},{10,11... | collective-permute-start | bytes 737288 | tf_op jit(solution)/shard_map/ppermute | solution.py:565
  (14 other events, 47.5 us)

commit v4 on v3

--- a/solution.py
+++ b/solution.py
@@ -460,7 +460,7 @@
         compiler_params=params(12),
         name="attention_forward",
         cost_estimate=pl.CostEstimate(
-            flops=3_000_000_000, bytes_accessed=20_000_000, transcendentals=3_000_000
+            flops=12_000_000_000, bytes_accessed=60_000_000, transcendentals=3_000_000
         ),
     )(info, far(latents), far(conditions), *pieces)
 
@@ -774,7 +774,9 @@
         info, latents, conditions, mine_one + other_one
     )
     mine_two = [after(piece, mod) for piece in mine_two]
-    other_two = swap_all(mine_two)
+    other_two = swap_all([mine_two[0], mine_two[1], mine_two[3]])
+    mine_two[2] = after(mine_two[2], *other_two)
+    other_two.insert(2, move(mine_two[2], CORE_SWAP))
     weights_two, out, grad_mid, grad_mixed, grad_mod_two, keep_two, send_two = run_middle(
         info, latents, conditions, mixed, grad_out, bias, mine_two + other_two
     )

time: 166 us -> 167 us (level)
  Pallas kernels: 70.8 us -> 38.3 us
  starting transfers between devices: 50.2 us -> 75.7 us
  waiting for transfers between devices: 43.4 us -> 50.4 us
    ppermute x38, starting transfers between devices: 50.2 us -> 75.7 us  [move(): return lax.ppermute(value, BOTH, pairs)]
    pallas_call x1, Pallas kernels: 32.3 us -> 12.3 us  [run_middle(): pl.pallas_call(middle_kernel, grid_spec=pltpu.PrefetchScalarGridSpec(num_...]
    pallas_call x1, Pallas kernels: 21.3 us -> 12.6 us  [run_backward(): pl.pallas_call(backward_kernel, grid_spec=pltpu.PrefetchScalarGridSpec(nu...]
    ppermute x38, waiting for transfers between devices: 43.4 us -> 50.4 us  [move(): return lax.ppermute(value, BOTH, pairs)]
    pallas_call x1, Pallas kernels: 9.63 us -> 5.85 us  [run_forward(): pl.pallas_call(forward_kernel, grid_spec=pltpu.PrefetchScalarGridSpec(num...]
  transfers between devices with their start and end apart: 38 -> 38, of which waited for: 18 -> 19; matrix products, arithmetic and copies ran while one was open for 0% -> 0% of each run, Pallas kernels for 21% -> 14%
where the time goes in v4:
time: 167 us; the launch traced here: 166 us
  starting transfers between devices  75.7 us (45%)
  waiting for transfers between devices  50.4 us (30%)
  Pallas kernels  38.3 us (23%)
    ppermute x38, starting transfers between devices, move(): return lax.ppermute(value, BOTH, pairs)  75.7 us
    ppermute x38, waiting for transfers between devices, move(): return lax.ppermute(value, BOTH, pairs)  50.4 us
    pallas_call x1, Pallas kernels, run_backward(): pl.pallas_call(backward_kernel, grid_spec=pltpu.PrefetchScalarGridSpec(nu...  12.6 us
    pallas_call x1, Pallas kernels, run_middle(): pl.pallas_call(middle_kernel, grid_spec=pltpu.PrefetchScalarGridSpec(num_...  12.3 us
    pallas_call x1, Pallas kernels, run_forward(): pl.pallas_call(forward_kernel, grid_spec=pltpu.PrefetchScalarGridSpec(num...  5.85 us
  transfers between devices with their start and end apart: 38, of which 19 were waited for; matrix products, arithmetic and copies ran while one was open for 0% of the time, Pallas kernels for 14%

profile of v4, /device:TPU:1, one launch (start us, length us, event | category | flops | bytes accessed | tf_op | source)
XLA Modules:
  0.0 166.0 jit_solution(6586221949239652183)
XLA Ops:
  2.5 5.6 %collective-permute-start.3 = (bf16[48,2048]{1,0:T(8,128)(2,1)S(1)}, bf16[48,2048]{1,0:T(8,128)(2,1)S(1)}, u32[]{:S(2)}, u32[]{:S(2)}) collective-permute-start(bf16[48,2048]{1,0:T(8,128)(2,1)S(1)} %pack_attention_weights.1), channel_id=1, source_target_pairs={{48,0},{115,1},{50,2},{113,3},{52,4},{119,5},{54,6},{117,7},{56,8}... | collective-permute-start | bytes 589832 | tf_op jit(solution)/shard_map/ppermute | solution.py:565
  9.7 5.1 %collective-permute-start = (bf16[48,2048]{1,0:T(8,128)(2,1)S(1)}, bf16[48,2048]{1,0:T(8,128)(2,1)S(1)}, u32[]{:S(2)}, u32[]{:S(2)}) collective-permute-start(bf16[48,2048]{1,0:T(8,128)(2,1)S(1)} %pack_attention_weights.1), channel_id=1, source_target_pairs={{0,0},{67,1},{2,2},{65,3},{4,4},{71,5},{6,6},{69,7},{8,8},{75,9},{... | collective-permute-start | bytes 589832 | tf_op jit(solution)/shard_map/ppermute | solution.py:565
  18.4 2.7 %collective-permute-done.p0 = bf16[48,2048]{1,0:T(8,128)(2,1)S(1)} collective-permute-done((bf16[48,2048]{1,0:T(8,128)(2,1)S(1)}, bf16[48,2048]{1,0:T(8,128)(2,1)S(1)}, u32[]{:S(2)}, u32[]{:S(2)}) %collective-permute-start) | collective-permute-done | bytes 196640 | tf_op jit(solution)/shard_map/ppermute | solution.py:565
  22.1 5.0 %collective-permute-start.8 = (bf16[48,5120]{1,0:T(8,128)(2,1)S(1)}, bf16[48,5120]{1,0:T(8,128)(2,1)S(1)}, u32[]{:S(2)}, u32[]{:S(2)}) collective-permute-start(bf16[48,5120]{1,0:T(8,128)(2,1)S(1)} %pack_feed_forward_weights.1), channel_id=1, source_target_pairs={{0,0},{67,1},{2,2},{65,3},{4,4},{71,5},{6,6},{69,7},{8,8},{75,9},{... | collective-permute-start | bytes 1474568 | tf_op jit(solution)/shard_map/ppermute | solution.py:565
  29.7 3.1 %collective-permute-start.9 = (bf16[48,5120]{1,0:T(8,128)(2,1)S(1)}, bf16[48,5120]{1,0:T(8,128)(2,1)S(1)}, u32[]{:S(2)}, u32[]{:S(2)}) collective-permute-start(bf16[48,5120]{1,0:T(8,128)(2,1)S(1)} %pack_feed_forward_weights.1), channel_id=1, source_target_pairs={{16,0},{83,1},{18,2},{81,3},{20,4},{87,5},{22,6},{85,7},{24,8},{91... | collective-permute-start | bytes 1474568 | tf_op jit(solution)/shard_map/ppermute | solution.py:565
  32.8 5.9 %attention_forward.1 = (bf16[384,2048]{1,0:T(8,128)(2,1)S(1)}, f32[48,128]{1,0:T(8,128)S(1)}, f32[8,768]{1,0:T(8,128)S(1)}, bf16[8,256,1152]{2,1,0:T(8,128)(2,1)...) custom-call(s32[4]{0:T(128)S(1)} %pad_add_fusion.info, ...), custom_call_target="tpu_custom_call" | custom-call | flops 12000000000 | bytes 60000000 | tf_op jit(solution)/shard_map/attention_forward/pallas_call | solution.py:442
  38.7 14.7 %collective-permute-done.13.p3 = bf16[48,5120]{1,0:T(8,128)(2,1)S(1)} collective-permute-done((bf16[48,5120]{1,0:T(8,128)(2,1)S(1)}, bf16[48,5120]{1,0:T(8,128)(2,1)S(1)}, u32[]{:S(2)}, u32[]{:S(2)}) %collective-permute-start.13) | collective-permute-done | bytes 491552 | tf_op jit(solution)/shard_map/ppermute | solution.py:565
  59.2 12.3 %feed_forward_both_ways.1 = (bf16[384,5120]{1,0:T(8,128)(2,1)S(1)}, bf16[8,256,384]{2,1,0:T(8,128)(2,1)}, f32[8,256,384]{2,1,0:T(8,128)S(1)}, bf16[8,256,384]{2,...) custom-call(s32[4]{0:T(128)S(1)} %pad_add_fusion.info, ...), custom_call_target="tpu_custom_call" | custom-call | flops 16000000000 | bytes 30000000 | tf_op jit(solution)/shard_map/feed_forward_both_ways/pallas_call | solution.py:469
  71.5 4.0 %collective-permute-done.16.right = bf16[192,5120]{1,0:T(8,128)(2,1)S(1)} collective-permute-done((bf16[192,5120]{1,0:T(8,128)(2,1)S(1)}, bf16[192,5120]{1,0:T(8,128)(2,1)S(1)}, u32[]{:S(2)}, u32[]{:S(2)}) %collective-permute-start.16) | collective-permute-done | bytes 1966112 | tf_op jit(solution)/shard_map/ppermute | solution.py:565
  75.9 2.6 %collective-permute-start.17 = (bf16[48,5120]{1,0:T(8,128)(2,1)S(1)}, bf16[48,5120]{1,0:T(8,128)(2,1)S(1)}, u32[]{:S(2)}, u32[]{:S(2)}) collective-permute-start(bf16[48,5120]{1,0:T(8,128)(2,1)S(1)} %get-tuple-element.94), channel_id=1, source_target_pairs={{0,0},{1,67},{2,2},{3,65},{4,4},{5,71},{6,6},{7,69},{8,8},{9,75},{... | collective-permute-start | bytes 1474568 | tf_op jit(solution)/shard_map/ppermute | solution.py:565
  78.6 12.7 %collective-permute-start.18 = (bf16[48,5120]{1,0:T(8,128)(2,1)S(1)}, bf16[48,5120]{1,0:T(8,128)(2,1)S(1)}, u32[]{:S(2)}, u32[]{:S(2)}) collective-permute-start(bf16[48,5120]{1,0:T(8,128)(2,1)S(1)} %get-tuple-element.100), channel_id=1, source_target_pairs={{0,16},{1,83},{2,18},{3,81},{4,20},{5,87},{6,22},{7,85},{8,24},{9,... | collective-permute-start | bytes 1474568 | tf_op jit(solution)/shard_map/ppermute | solution.py:565
  91.3 8.2 %collective-permute-start.19 = (bf16[48,5120]{1,0:T(8,128)(2,1)S(1)}, bf16[48,5120]{1,0:T(8,128)(2,1)S(1)}, u32[]{:S(2)}, u32[]{:S(2)}) collective-permute-start(bf16[48,5120]{1,0:T(8,128)(2,1)S(1)} %get-tuple-element.101), channel_id=1, source_target_pairs={{0,32},{1,99},{2,34},{3,97},{4,36},{5,103},{6,38},{7,101},{8,40},{... | collective-permute-start | bytes 1474568 | tf_op jit(solution)/shard_map/ppermute | solution.py:565
  99.5 4.1 %collective-permute-start.20 = (bf16[48,5120]{1,0:T(8,128)(2,1)S(1)}, bf16[48,5120]{1,0:T(8,128)(2,1)S(1)}, u32[]{:S(2)}, u32[]{:S(2)}) collective-permute-start(bf16[48,5120]{1,0:T(8,128)(2,1)S(1)} %get-tuple-element.102), channel_id=1, source_target_pairs={{0,48},{1,115},{2,50},{3,113},{4,52},{5,119},{6,54},{7,117},{8,56}... | collective-permute-start | bytes 1474568 | tf_op jit(solution)/shard_map/ppermute | solution.py:565
  103.6 12.6 %attention_backward.1 = (bf16[8,256,384]{2,1,0:T(8,128)(2,1)}, bf16[8,384]{1,0:T(8,128)(2,1)}, bf16[192,2048]{1,0:T(8,128)(2,1)S(1)}, bf16[192,2048]{1,0:T(8,128)(2,1)S(1)}) custom-call(s32[4]{0:T(128)S(1)} %pad_add_fusion.info, bf16[8,256,384]{2,1,0:T(8,128)(2,1)} %latents.5, bf16[8,384]{1,0:T(8,128)(2,1)} %conditions.5, ...), custom_call_target="tpu_custom_call" | custom-call | flops 24999999488 | bytes 20000000 | tf_op jit(solution)/shard_map/attention_backward/pallas_call | solution.py:510
  116.2 5.6 %collective-permute-done.19.refs_2_ = bf16[48,5120]{1,0:T(8,128)(2,1)S(1)} collective-permute-done((bf16[48,5120]{1,0:T(8,128)(2,1)S(1)}, bf16[48,5120]{1,0:T(8,128)(2,1)S(1)}, u32[]{:S(2)}, u32[]{:S(2)}) %collective-permute-start.19) | collective-permute-done | bytes 491552 | tf_op jit(solution)/shard_map/ppermute | solution.py:565
  125.5 1.9 %collective-permute-start.22 = (bf16[48,2048]{1,0:T(8,128)(2,1)S(1)}, bf16[48,2048]{1,0:T(8,128)(2,1)S(1)}, u32[]{:S(2)}, u32[]{:S(2)}) collective-permute-start(bf16[48,2048]{1,0:T(8,128)(2,1)S(1)} %get-tuple-element.104), channel_id=1, source_target_pairs={{0,0},{1,67},{2,2},{3,65},{4,4},{5,71},{6,6},{7,69},{8,8},{9,75},{... | collective-permute-start | bytes 589832 | tf_op jit(solution)/shard_map/ppermute | solution.py:565
  127.5 2.2 %collective-permute-start.23 = (bf16[48,2048]{1,0:T(8,128)(2,1)S(1)}, bf16[48,2048]{1,0:T(8,128)(2,1)S(1)}, u32[]{:S(2)}, u32[]{:S(2)}) collective-permute-start(bf16[48,2048]{1,0:T(8,128)(2,1)S(1)} %get-tuple-element.105), channel_id=1, source_target_pairs={{0,16},{1,83},{2,18},{3,81},{4,20},{5,87},{6,22},{7,85},{8,24},{9,... | collective-permute-start | bytes 589832 | tf_op jit(solution)/shard_map/ppermute | solution.py:565
  129.6 4.0 %collective-permute-start.24 = (bf16[48,2048]{1,0:T(8,128)(2,1)S(1)}, bf16[48,2048]{1,0:T(8,128)(2,1)S(1)}, u32[]{:S(2)}, u32[]{:S(2)}) collective-permute-start(bf16[48,2048]{1,0:T(8,128)(2,1)S(1)} %get-tuple-element.106), channel_id=1, source_target_pairs={{0,32},{1,99},{2,34},{3,97},{4,36},{5,103},{6,38},{7,101},{8,40},{... | collective-permute-start | bytes 589832 | tf_op jit(solution)/shard_map/ppermute | solution.py:565
  133.6 3.8 %collective-permute-start.25 = (bf16[48,2048]{1,0:T(8,128)(2,1)S(1)}, bf16[48,2048]{1,0:T(8,128)(2,1)S(1)}, u32[]{:S(2)}, u32[]{:S(2)}) collective-permute-start(bf16[48,2048]{1,0:T(8,128)(2,1)S(1)} %get-tuple-element.107), channel_id=1, source_target_pairs={{0,48},{1,115},{2,50},{3,113},{4,52},{5,119},{6,54},{7,117},{8,56}... | collective-permute-start | bytes 589832 | tf_op jit(solution)/shard_map/ppermute | solution.py:565
  138.1 2.6 %collective-permute-start.35 = (bf16[48,2560]{1,0:T(8,128)(2,1)S(1)}, bf16[48,2560]{1,0:T(8,128)(2,1)S(1)}, u32[]{:S(2)}, u32[]{:S(2)}) collective-permute-start(bf16[48,2560]{1,0:T(8,128)(2,1)S(1)} %add.26.refs_0_), channel_id=1, source_target_pairs={{0,8},{1,9},{2,10},{3,11},{4,12},{5,13},{6,14},{7,15},{8,0},{9,1},... | collective-permute-start | bytes 737288 | tf_op jit(solution)/shard_map/ppermute | solution.py:565
  144.4 4.6 %collective-permute-done.36.refs_3_ = bf16[48,2560]{1,0:T(8,128)(2,1)S(1)} collective-permute-done((bf16[48,2560]{1,0:T(8,128)(2,1)S(1)}, bf16[48,2560]{1,0:T(8,128)(2,1)S(1)}, u32[]{:S(2)}, u32[]{:S(2)}) %collective-permute-start.36) | collective-permute-done | bytes 245792 | tf_op jit(solution)/shard_map/ppermute | solution.py:565
  149.0 3.8 %collective-permute-done.34.refs_1_ = bf16[48,2560]{1,0:T(8,128)(2,1)S(1)} collective-permute-done((bf16[48,2560]{1,0:T(8,128)(2,1)S(1)}, bf16[48,2560]{1,0:T(8,128)(2,1)S(1)}, u32[]{:S(2)}, u32[]{:S(2)}) %collective-permute-start.34) | collective-permute-done | bytes 245792 | tf_op jit(solution)/shard_map/ppermute | solution.py:565
  153.5 2.1 %collective-permute-start.29 = (bf16[48,1024]{1,0:T(8,128)(2,1)S(1)}, bf16[48,1024]{1,0:T(8,128)(2,1)S(1)}, u32[]{:S(2)}, u32[]{:S(2)}) collective-permute-start(bf16[48,1024]{1,0:T(8,128)(2,1)S(1)} %add.23.refs_0_), channel_id=1, source_target_pairs={{0,8},{1,9},{2,10},{3,11},{4,12},{5,13},{6,14},{7,15},{8,0},{9,1},... | collective-permute-start | bytes 294920 | tf_op jit(solution)/shard_map/ppermute | solution.py:565
  160.7 2.4 %collective-permute-start.31 = (bf16[48,1024]{1,0:T(8,128)(2,1)S(1)}, bf16[48,1024]{1,0:T(8,128)(2,1)S(1)}, u32[]{:S(2)}, u32[]{:S(2)}) collective-permute-start(bf16[48,1024]{1,0:T(8,128)(2,1)S(1)} %add.24.mine), channel_id=1, source_target_pairs={{0,1},{1,0},{2,3},{3,2},{4,5},{5,4},{6,7},{7,6},{8,9},{9,8},{10,11... | collective-permute-start | bytes 294920 | tf_op jit(solution)/shard_map/ppermute | solution.py:565
  (70 shorter events, 33.2 us)
Async XLA Ops:
  2.5 14.4 %collective-permute-start.3 = (bf16[48,2048]{1,0:T(8,128)(2,1)S(1)}, bf16[48,2048]{1,0:T(8,128)(2,1)S(1)}, u32[]{:S(2)}, u32[]{:S(2)}) collective-permute-start(bf16[48,2048]{1,0:T(8,128)(2,1)S(1)} %pack_attention_weights.1), channel_id=1, source_target_pairs={{48,0},{115,1},{50,2},{113,3},{52,4},{119,5},{54,6},{117,7},{56,8}... | collective-permute-start | bytes 589832 | tf_op jit(solution)/shard_map/ppermute | solution.py:565
  8.1 10.3 %collective-permute-start.2 = (bf16[48,2048]{1,0:T(8,128)(2,1)S(1)}, bf16[48,2048]{1,0:T(8,128)(2,1)S(1)}, u32[]{:S(2)}, u32[]{:S(2)}) collective-permute-start(bf16[48,2048]{1,0:T(8,128)(2,1)S(1)} %pack_attention_weights.1), channel_id=1, source_target_pairs={{32,0},{99,1},{34,2},{97,3},{36,4},{103,5},{38,6},{101,7},{40,8},{... | collective-permute-start | bytes 589832 | tf_op jit(solution)/shard_map/ppermute | solution.py:565
  9.7 11.3 %collective-permute-start = (bf16[48,2048]{1,0:T(8,128)(2,1)S(1)}, bf16[48,2048]{1,0:T(8,128)(2,1)S(1)}, u32[]{:S(2)}, u32[]{:S(2)}) collective-permute-start(bf16[48,2048]{1,0:T(8,128)(2,1)S(1)} %pack_attention_weights.1), channel_id=1, source_target_pairs={{0,0},{67,1},{2,2},{65,3},{4,4},{71,5},{6,6},{69,7},{8,8},{75,9},{... | collective-permute-start | bytes 589832 | tf_op jit(solution)/shard_map/ppermute | solution.py:565
  21.5 8.1 %collective-permute-start.6 = (bf16[48,2048]{1,0:T(8,128)(2,1)S(1)}, bf16[48,2048]{1,0:T(8,128)(2,1)S(1)}, u32[]{:S(2)}, u32[]{:S(2)}) collective-permute-start(bf16[48,2048]{1,0:T(8,128)(2,1)S(1)} %collective-permute-done.2.p2), channel_id=1, source_target_pairs={{0,1},{1,0},{2,3},{3,2},{4,5},{5,4},{6,7},{7,6},{8,9},{9,8},{10,11... | collective-permute-start | bytes 589832 | tf_op jit(solution)/shard_map/ppermute | solution.py:565
  22.0 10.7 %collective-permute-start.7 = (bf16[48,2048]{1,0:T(8,128)(2,1)S(1)}, bf16[48,2048]{1,0:T(8,128)(2,1)S(1)}, u32[]{:S(2)}, u32[]{:S(2)}) collective-permute-start(bf16[48,2048]{1,0:T(8,128)(2,1)S(1)} %collective-permute-done.3.p3), channel_id=1, source_target_pairs={{0,1},{1,0},{2,3},{3,2},{4,5},{5,4},{6,7},{7,6},{8,9},{9,8},{10,11... | collective-permute-start | bytes 589832 | tf_op jit(solution)/shard_map/ppermute | solution.py:565
  22.1 16.6 %collective-permute-start.8 = (bf16[48,5120]{1,0:T(8,128)(2,1)S(1)}, bf16[48,5120]{1,0:T(8,128)(2,1)S(1)}, u32[]{:S(2)}, u32[]{:S(2)}) collective-permute-start(bf16[48,5120]{1,0:T(8,128)(2,1)S(1)} %pack_feed_forward_weights.1), channel_id=1, source_target_pairs={{0,0},{67,1},{2,2},{65,3},{4,4},{71,5},{6,6},{69,7},{8,8},{75,9},{... | collective-permute-start | bytes 1474568 | tf_op jit(solution)/shard_map/ppermute | solution.py:565
  27.1 26.4 %collective-permute-start.13 = (bf16[48,5120]{1,0:T(8,128)(2,1)S(1)}, bf16[48,5120]{1,0:T(8,128)(2,1)S(1)}, u32[]{:S(2)}, u32[]{:S(2)}) collective-permute-start(bf16[48,5120]{1,0:T(8,128)(2,1)S(1)} %pack_feed_forward_weights.1), channel_id=1, source_target_pairs={{48,0},{115,1},{50,2},{113,3},{52,4},{119,5},{54,6},{117,7},{56,8}... | collective-permute-start | bytes 1474568 | tf_op jit(solution)/shard_map/ppermute | solution.py:565
  27.9 27.4 %collective-permute-start.10 = (bf16[48,5120]{1,0:T(8,128)(2,1)S(1)}, bf16[48,5120]{1,0:T(8,128)(2,1)S(1)}, u32[]{:S(2)}, u32[]{:S(2)}) collective-permute-start(bf16[48,5120]{1,0:T(8,128)(2,1)S(1)} %pack_feed_forward_weights.1), channel_id=1, source_target_pairs={{32,0},{99,1},{34,2},{97,3},{36,4},{103,5},{38,6},{101,7},{40,8},{... | collective-permute-start | bytes 1474568 | tf_op jit(solution)/shard_map/ppermute | solution.py:565
  29.7 25.1 %collective-permute-start.9 = (bf16[48,5120]{1,0:T(8,128)(2,1)S(1)}, bf16[48,5120]{1,0:T(8,128)(2,1)S(1)}, u32[]{:S(2)}, u32[]{:S(2)}) collective-permute-start(bf16[48,5120]{1,0:T(8,128)(2,1)S(1)} %pack_feed_forward_weights.1), channel_id=1, source_target_pairs={{16,0},{83,1},{18,2},{81,3},{20,4},{87,5},{22,6},{85,7},{24,8},{91... | collective-permute-start | bytes 1474568 | tf_op jit(solution)/shard_map/ppermute | solution.py:565
  38.6 16.6 %collective-permute-start.11 = (bf16[48,5120]{1,0:T(8,128)(2,1)S(1)}, bf16[48,5120]{1,0:T(8,128)(2,1)S(1)}, u32[]{:S(2)}, u32[]{:S(2)}) collective-permute-start(bf16[48,5120]{1,0:T(8,128)(2,1)S(1)} %collective-permute-done.8.p0), channel_id=1, source_target_pairs={{0,1},{1,0},{2,3},{3,2},{4,5},{5,4},{6,7},{7,6},{8,9},{9,8},{10,11... | collective-permute-start | bytes 1474568 | tf_op jit(solution)/shard_map/ppermute | solution.py:565
  75.9 46.6 %collective-permute-start.17 = (bf16[48,5120]{1,0:T(8,128)(2,1)S(1)}, bf16[48,5120]{1,0:T(8,128)(2,1)S(1)}, u32[]{:S(2)}, u32[]{:S(2)}) collective-permute-start(bf16[48,5120]{1,0:T(8,128)(2,1)S(1)} %get-tuple-element.94), channel_id=1, source_target_pairs={{0,0},{1,67},{2,2},{3,65},{4,4},{5,71},{6,6},{7,69},{8,8},{9,75},{... | collective-permute-start | bytes 1474568 | tf_op jit(solution)/shard_map/ppermute | solution.py:565
  78.6 37.6 %collective-permute-start.18 = (bf16[48,5120]{1,0:T(8,128)(2,1)S(1)}, bf16[48,5120]{1,0:T(8,128)(2,1)S(1)}, u32[]{:S(2)}, u32[]{:S(2)}) collective-permute-start(bf16[48,5120]{1,0:T(8,128)(2,1)S(1)} %get-tuple-element.100), channel_id=1, source_target_pairs={{0,16},{1,83},{2,18},{3,81},{4,20},{5,87},{6,22},{7,85},{8,24},{9,... | collective-permute-start | bytes 1474568 | tf_op jit(solution)/shard_map/ppermute | solution.py:565
  91.3 30.5 %collective-permute-start.19 = (bf16[48,5120]{1,0:T(8,128)(2,1)S(1)}, bf16[48,5120]{1,0:T(8,128)(2,1)S(1)}, u32[]{:S(2)}, u32[]{:S(2)}) collective-permute-start(bf16[48,5120]{1,0:T(8,128)(2,1)S(1)} %get-tuple-element.101), channel_id=1, source_target_pairs={{0,32},{1,99},{2,34},{3,97},{4,36},{5,103},{6,38},{7,101},{8,40},{... | collective-permute-start | bytes 1474568 | tf_op jit(solution)/shard_map/ppermute | solution.py:565
  99.5 23.0 %collective-permute-start.20 = (bf16[48,5120]{1,0:T(8,128)(2,1)S(1)}, bf16[48,5120]{1,0:T(8,128)(2,1)S(1)}, u32[]{:S(2)}, u32[]{:S(2)}) collective-permute-start(bf16[48,5120]{1,0:T(8,128)(2,1)S(1)} %get-tuple-element.102), channel_id=1, source_target_pairs={{0,48},{1,115},{2,50},{3,113},{4,52},{5,119},{6,54},{7,117},{8,56}... | collective-permute-start | bytes 1474568 | tf_op jit(solution)/shard_map/ppermute | solution.py:565
  125.4 11.9 %collective-permute-start.33 = (bf16[48,2560]{1,0:T(8,128)(2,1)S(1)}, bf16[48,2560]{1,0:T(8,128)(2,1)S(1)}, u32[]{:S(2)}, u32[]{:S(2)}) collective-permute-start(bf16[48,2560]{1,0:T(8,128)(2,1)S(1)} %add.25.refs_0_), channel_id=1, source_target_pairs={{0,2},{1,3},{2,0},{3,1},{4,6},{5,7},{6,4},{7,5},{8,10},{9,11},{10,... | collective-permute-start | bytes 737288 | tf_op jit(solution)/shard_map/ppermute | solution.py:565
  125.5 12.5 %collective-permute-start.22 = (bf16[48,2048]{1,0:T(8,128)(2,1)S(1)}, bf16[48,2048]{1,0:T(8,128)(2,1)S(1)}, u32[]{:S(2)}, u32[]{:S(2)}) collective-permute-start(bf16[48,2048]{1,0:T(8,128)(2,1)S(1)} %get-tuple-element.104), channel_id=1, source_target_pairs={{0,0},{1,67},{2,2},{3,65},{4,4},{5,71},{6,6},{7,69},{8,8},{9,75},{... | collective-permute-start | bytes 589832 | tf_op jit(solution)/shard_map/ppermute | solution.py:565
  127.5 13.2 %collective-permute-start.23 = (bf16[48,2048]{1,0:T(8,128)(2,1)S(1)}, bf16[48,2048]{1,0:T(8,128)(2,1)S(1)}, u32[]{:S(2)}, u32[]{:S(2)}) collective-permute-start(bf16[48,2048]{1,0:T(8,128)(2,1)S(1)} %get-tuple-element.105), channel_id=1, source_target_pairs={{0,16},{1,83},{2,18},{3,81},{4,20},{5,87},{6,22},{7,85},{8,24},{9,... | collective-permute-start | bytes 589832 | tf_op jit(solution)/shard_map/ppermute | solution.py:565
  129.6 11.5 %collective-permute-start.24 = (bf16[48,2048]{1,0:T(8,128)(2,1)S(1)}, bf16[48,2048]{1,0:T(8,128)(2,1)S(1)}, u32[]{:S(2)}, u32[]{:S(2)}) collective-permute-start(bf16[48,2048]{1,0:T(8,128)(2,1)S(1)} %get-tuple-element.106), channel_id=1, source_target_pairs={{0,32},{1,99},{2,34},{3,97},{4,36},{5,103},{6,38},{7,101},{8,40},{... | collective-permute-start | bytes 589832 | tf_op jit(solution)/shard_map/ppermute | solution.py:565
  133.6 7.7 %collective-permute-start.25 = (bf16[48,2048]{1,0:T(8,128)(2,1)S(1)}, bf16[48,2048]{1,0:T(8,128)(2,1)S(1)}, u32[]{:S(2)}, u32[]{:S(2)}) collective-permute-start(bf16[48,2048]{1,0:T(8,128)(2,1)S(1)} %get-tuple-element.107), channel_id=1, source_target_pairs={{0,48},{1,115},{2,50},{3,113},{4,52},{5,119},{6,54},{7,117},{8,56}... | collective-permute-start | bytes 589832 | tf_op jit(solution)/shard_map/ppermute | solution.py:565
  137.4 11.6 %collective-permute-start.36 = (bf16[48,2560]{1,0:T(8,128)(2,1)S(1)}, bf16[48,2560]{1,0:T(8,128)(2,1)S(1)}, u32[]{:S(2)}, u32[]{:S(2)}) collective-permute-start(bf16[48,2560]{1,0:T(8,128)(2,1)S(1)} %add.26.refs_0_), channel_id=1, source_target_pairs={{0,12},{1,13},{2,14},{3,15},{4,0},{5,1},{6,2},{7,3},{8,4},{9,5},{1... | collective-permute-start | bytes 737288 | tf_op jit(solution)/shard_map/ppermute | solution.py:565
  138.1 10.9 %collective-permute-start.35 = (bf16[48,2560]{1,0:T(8,128)(2,1)S(1)}, bf16[48,2560]{1,0:T(8,128)(2,1)S(1)}, u32[]{:S(2)}, u32[]{:S(2)}) collective-permute-start(bf16[48,2560]{1,0:T(8,128)(2,1)S(1)} %add.26.refs_0_), channel_id=1, source_target_pairs={{0,8},{1,9},{2,10},{3,11},{4,12},{5,13},{6,14},{7,15},{8,0},{9,1},... | collective-permute-start | bytes 737288 | tf_op jit(solution)/shard_map/ppermute | solution.py:565
  140.6 12.1 %collective-permute-start.34 = (bf16[48,2560]{1,0:T(8,128)(2,1)S(1)}, bf16[48,2560]{1,0:T(8,128)(2,1)S(1)}, u32[]{:S(2)}, u32[]{:S(2)}) collective-permute-start(bf16[48,2560]{1,0:T(8,128)(2,1)S(1)} %add.26.refs_0_), channel_id=1, source_target_pairs={{0,4},{1,5},{2,6},{3,7},{4,8},{5,9},{6,10},{7,11},{8,12},{9,13},{1... | collective-permute-start | bytes 737288 | tf_op jit(solution)/shard_map/ppermute | solution.py:565
  143.3 10.0 %collective-permute-start.27 = (bf16[48,1024]{1,0:T(8,128)(2,1)S(1)}, bf16[48,1024]{1,0:T(8,128)(2,1)S(1)}, u32[]{:S(2)}, u32[]{:S(2)}) collective-permute-start(bf16[48,1024]{1,0:T(8,128)(2,1)S(1)} %add.22.refs_0_), channel_id=1, source_target_pairs={{0,2},{1,3},{2,0},{3,1},{4,6},{5,7},{6,4},{7,5},{8,10},{9,11},{10,... | collective-permute-start | bytes 294920 | tf_op jit(solution)/shard_map/ppermute | solution.py:565
  152.9 10.2 %collective-permute-start.37 = (bf16[48,2560]{1,0:T(8,128)(2,1)S(1)}, bf16[48,2560]{1,0:T(8,128)(2,1)S(1)}, u32[]{:S(2)}, u32[]{:S(2)}) collective-permute-start(bf16[48,2560]{1,0:T(8,128)(2,1)S(1)} %add.27.mine), channel_id=1, source_target_pairs={{0,1},{1,0},{2,3},{3,2},{4,5},{5,4},{6,7},{7,6},{8,9},{9,8},{10,11... | collective-permute-start | bytes 737288 | tf_op jit(solution)/shard_map/ppermute | solution.py:565
  (14 other events, 54.3 us)

commit v5 on v3

--- a/solution.py
+++ b/solution.py
@@ -32,6 +32,7 @@
 AT_PROJ = AT_MOD + MOD_TWO
 AT_DOWN = AT_PROJ + D
 BIAS_TWO = AT_DOWN + FF
+LANES_SENT = BIAS_TWO
 ROW_QKV, ROW_MOD, ROW_PROJ, ROW_UP, ROW_DOWN = 0, 9, 27, 30, 42
 
 
@@ -177,22 +178,28 @@
 
     @pl.when(step == 0)
     def _():
-        assemble(info, (p0, p1, p2, p3, p4, p5, p6, p7), weights)
+        pieces = (p0, p1, p2, p3, p4, p5, p6, p7)
+        assemble(info, [piece.at[:, :AT_DOWN] for piece in pieces], weights)
+        column, z_high, core = info[1], info[2], info[3]
+        for k in range(8):
+            layer = (z_high ^ core) if k < 4 else 1 - (z_high ^ core)
+            first = layer * 768 + lax.rem(column + k % 4, 4) * 192
+            for q in range(4):
+                down[pl.ds(pl.multiple_of(first + 48 * q, 16), 48), :] = pieces[k][
+                    :, AT_DOWN + D * q : AT_DOWN + D * q + D
+                ]
         cond_low = silu(conditions[...].astype(F32)).astype(BF)
         mod[...] = dot(cond_low, weights[:, AT_MOD : AT_MOD + MOD_TWO]) + bias_row(
             bias_in[...], ROW_MOD + 6, 12
         )
-        for owner in range(8):
-            for q in range(4):
-                at = 192 * owner + 48 * q
-                down[at : at + 48, :] = weights[
-                    48 * owner : 48 * owner + 48, AT_DOWN + D * q : AT_DOWN + D * q + D
-                ]
+        acc_bias[...] = jnp.zeros_like(acc_bias)
+        grad_mod[...] = jnp.zeros_like(grad_mod)
+
+    @pl.when((step == 0) & (info[0] == 0))
+    def _():
         acc_up[...] = jnp.zeros_like(acc_up)
         acc_down[...] = jnp.zeros_like(acc_down)
         acc_proj[...] = jnp.zeros_like(acc_proj)
-        acc_bias[...] = jnp.zeros_like(acc_bias)
-        grad_mod[...] = jnp.zeros_like(grad_mod)
 
     @pl.when(PAIR * step >= info[0])
     def _():
@@ -202,6 +209,9 @@
 
     @pl.when(PAIR * step < info[0])
     def _():
+        def so_far(total):
+            return jnp.where(step == 0, 0.0, total)
+
         bias = bias_in[...]
         w_proj = weights[:, AT_PROJ : AT_PROJ + D]
         up_bias = bias_row(bias, ROW_UP, 12)
@@ -238,9 +248,9 @@
             slope = half + act * (1.0 - bend) * (root + (3.0 * cube) * square)
             act_low = act.astype(BF)
             branch_two = branch_two + dot(act_low, w_down)
-            acc_down[at : at + CHUNK, :] += dot_tn(act_low, g_two)
+            acc_down[at : at + CHUNK, :] = so_far(acc_down[at : at + CHUNK, :]) + dot_tn(act_low, g_two)
             g_up = (slope * dot_nt(g_two, w_down)).astype(BF)
-            acc_up[:, at : at + CHUNK] += dot_tn(hidden, g_up)
+            acc_up[:, at : at + CHUNK] = so_far(acc_up[:, at : at + CHUNK]) + dot_tn(hidden, g_up)
             acc_bias[0:1, at : at + CHUNK] += jnp.sum(g_up.astype(F32), axis=0, keepdims=True)
             d_hidden = d_hidden + dot_nt(g_up, w_up)
         acc_bias[1:2, :D] += jnp.sum(g_two.astype(F32), axis=0, keepdims=True)
@@ -265,7 +275,7 @@
             g_one.append((grad_mid * row[:, :D]).astype(BF))
         g_one = jnp.concatenate(g_one, axis=0)
         acc_bias[2:3, :D] += jnp.sum(g_one.astype(F32), axis=0, keepdims=True)
-        acc_proj[...] += dot_tn(mixed, g_one)
+        acc_proj[...] = so_far(acc_proj[...]) + dot_tn(mixed, g_one)
         grad_mixed_out[pl.ds(PAIR * step, PAIR)] = (
             dot_nt(g_one, w_proj).astype(BF).reshape(PAIR, TOK, D)
         )
@@ -490,7 +500,7 @@
             ],
         ),
         out_shape=[
-            pltpu.VMEM((D, LANES_TWO), BF),
+            pltpu.VMEM((D, AT_DOWN), BF),
             jax.ShapeDtypeStruct((CAP, TOK, D), BF),
             pltpu.VMEM((CAP, TOK, D), F32),
             pltpu.VMEM((CAP, TOK, D), BF),
@@ -663,7 +673,6 @@
     out[:, AT_PROJ:AT_DOWN] = proj[...]
     for q in range(4):
         out[:, AT_DOWN + D * q : AT_DOWN + D * q + D] = down[48 * q : 48 * q + 48, :]
-    out[:, BIAS_TWO:] = jnp.zeros((48, 128), BF)
 
 
 def pack(kernel, name, lanes, *values):
@@ -762,7 +771,7 @@
         after(qkv_weight, info), mod_weight, qv_bias, mod_bias, proj_bias, up_bias, down_bias,
     )
     block_two = pack(
-        pack_two_kernel, "pack_feed_forward_weights", LANES_TWO,
+        pack_two_kernel, "pack_feed_forward_weights", LANES_SENT,
         up_weight, mod_weight, proj_weight, down_weight,
     )
     mine_one = fetch_all(block_one)

time: 166 us -> 164 us (0.988)
  Pallas kernels: 70.8 us -> 44.7 us
  starting transfers between devices: 50.2 us -> 62.7 us
  waiting for transfers between devices: 43.4 us -> 55 us
    pallas_call x1, Pallas kernels: 32.3 us -> 18.7 us  [run_middle(): pl.pallas_call(middle_kernel, grid_spec=pltpu.PrefetchScalarGridSpec(num_...]
    ppermute x38, starting transfers between devices: 50.2 us -> 62.7 us  [move(): return lax.ppermute(value, BOTH, pairs)]
    ppermute x38, waiting for transfers between devices: 43.4 us -> 55 us  [move(): return lax.ppermute(value, BOTH, pairs)]
    pallas_call x1, Pallas kernels: 21.3 us -> 12.5 us  [run_backward(): pl.pallas_call(backward_kernel, grid_spec=pltpu.PrefetchScalarGridSpec(nu...]
    pallas_call x1, Pallas kernels: 9.63 us -> 5.85 us  [run_forward(): pl.pallas_call(forward_kernel, grid_spec=pltpu.PrefetchScalarGridSpec(num...]
  transfers between devices with their start and end apart: 38 -> 38, of which waited for: 18 -> 17; matrix products, arithmetic and copies ran while one was open for 0% -> 0% of each run, Pallas kernels for 21% -> 14%
where the time goes in v5:
time: 164 us
  starting transfers between devices  62.7 us (38%)
  waiting for transfers between devices  55 us (34%)
  Pallas kernels  44.7 us (27%)
    ppermute x38, starting transfers between devices, move(): return lax.ppermute(value, BOTH, pairs)  62.7 us
    ppermute x38, waiting for transfers between devices, move(): return lax.ppermute(value, BOTH, pairs)  55 us
    pallas_call x1, Pallas kernels, run_middle(): pl.pallas_call(middle_kernel, grid_spec=pltpu.PrefetchScalarGridSpec(num_...  18.7 us
    pallas_call x1, Pallas kernels, run_backward(): pl.pallas_call(backward_kernel, grid_spec=pltpu.PrefetchScalarGridSpec(nu...  12.5 us
    pallas_call x1, Pallas kernels, run_forward(): pl.pallas_call(forward_kernel, grid_spec=pltpu.PrefetchScalarGridSpec(num...  5.85 us
  transfers between devices with their start and end apart: 38, of which 17 were waited for; matrix products, arithmetic and copies ran while one was open for 0% of the time, Pallas kernels for 14%

profile of v5, /device:TPU:1, one launch (start us, length us, event | category | flops | bytes accessed | tf_op | source)
XLA Modules:
  0.0 164.0 jit_solution(4348412011460923789)
XLA Ops:
  2.5 6.5 %collective-permute-start = (bf16[48,2048]{1,0:T(8,128)(2,1)S(1)}, bf16[48,2048]{1,0:T(8,128)(2,1)S(1)}, u32[]{:S(2)}, u32[]{:S(2)}) collective-permute-start(bf16[48,2048]{1,0:T(8,128)(2,1)S(1)} %pack_attention_weights.1), channel_id=1, source_target_pairs={{0,0},{67,1},{2,2},{65,3},{4,4},{71,5},{6,6},{69,7},{8,8},{75,9},{... | collective-permute-start | bytes 589832 | tf_op jit(solution)/shard_map/ppermute | solution.py:575
  9.0 2.3 %collective-permute-start.1 = (bf16[48,2048]{1,0:T(8,128)(2,1)S(1)}, bf16[48,2048]{1,0:T(8,128)(2,1)S(1)}, u32[]{:S(2)}, u32[]{:S(2)}) collective-permute-start(bf16[48,2048]{1,0:T(8,128)(2,1)S(1)} %pack_attention_weights.1), channel_id=1, source_target_pairs={{16,0},{83,1},{18,2},{81,3},{20,4},{87,5},{22,6},{85,7},{24,8},{91... | collective-permute-start | bytes 589832 | tf_op jit(solution)/shard_map/ppermute | solution.py:575
  11.2 2.9 %collective-permute-start.2 = (bf16[48,2048]{1,0:T(8,128)(2,1)S(1)}, bf16[48,2048]{1,0:T(8,128)(2,1)S(1)}, u32[]{:S(2)}, u32[]{:S(2)}) collective-permute-start(bf16[48,2048]{1,0:T(8,128)(2,1)S(1)} %pack_attention_weights.1), channel_id=1, source_target_pairs={{32,0},{99,1},{34,2},{97,3},{36,4},{103,5},{38,6},{101,7},{40,8},{... | collective-permute-start | bytes 589832 | tf_op jit(solution)/shard_map/ppermute | solution.py:575
  17.8 3.8 %collective-permute-done.2.p2 = bf16[48,2048]{1,0:T(8,128)(2,1)S(1)} collective-permute-done((bf16[48,2048]{1,0:T(8,128)(2,1)S(1)}, bf16[48,2048]{1,0:T(8,128)(2,1)S(1)}, u32[]{:S(2)}, u32[]{:S(2)}) %collective-permute-start.2) | collective-permute-done | bytes 196640 | tf_op jit(solution)/shard_map/ppermute | solution.py:575
  21.6 2.5 %collective-permute-start.8 = (bf16[48,4992]{1,0:T(8,128)(2,1)S(1)}, bf16[48,4992]{1,0:T(8,128)(2,1)S(1)}, u32[]{:S(2)}, u32[]{:S(2)}) collective-permute-start(bf16[48,4992]{1,0:T(8,128)(2,1)S(1)} %pack_feed_forward_weights.1), channel_id=1, source_target_pairs={{0,0},{67,1},{2,2},{65,3},{4,4},{71,5},{6,6},{69,7},{8,8},{75,9},{... | collective-permute-start | bytes 1437704 | tf_op jit(solution)/shard_map/ppermute | solution.py:575
  24.1 2.9 %collective-permute-start.11 = (bf16[48,4992]{1,0:T(8,128)(2,1)S(1)}, bf16[48,4992]{1,0:T(8,128)(2,1)S(1)}, u32[]{:S(2)}, u32[]{:S(2)}) collective-permute-start(bf16[48,4992]{1,0:T(8,128)(2,1)S(1)} %pack_feed_forward_weights.1), channel_id=1, source_target_pairs={{48,0},{115,1},{50,2},{113,3},{52,4},{119,5},{54,6},{117,7},{56,8}... | collective-permute-start | bytes 1437704 | tf_op jit(solution)/shard_map/ppermute | solution.py:575
  27.0 3.1 %collective-permute-start.10 = (bf16[48,4992]{1,0:T(8,128)(2,1)S(1)}, bf16[48,4992]{1,0:T(8,128)(2,1)S(1)}, u32[]{:S(2)}, u32[]{:S(2)}) collective-permute-start(bf16[48,4992]{1,0:T(8,128)(2,1)S(1)} %pack_feed_forward_weights.1), channel_id=1, source_target_pairs={{32,0},{99,1},{34,2},{97,3},{36,4},{103,5},{38,6},{101,7},{40,8},{... | collective-permute-start | bytes 1437704 | tf_op jit(solution)/shard_map/ppermute | solution.py:575
  32.2 5.9 %attention_forward.1 = (bf16[384,2048]{1,0:T(8,128)(2,1)S(1)}, f32[48,128]{1,0:T(8,128)S(1)}, f32[8,768]{1,0:T(8,128)S(1)}, bf16[8,256,1152]{2,1,0:T(8,128)(2,1)...) custom-call(s32[4]{0:T(128)S(1)} %pad_add_fusion.info, ...), custom_call_target="tpu_custom_call" | custom-call | flops 3000000000 | bytes 20000000 | tf_op jit(solution)/shard_map/attention_forward/pallas_call | solution.py:452
  38.3 12.7 %collective-permute-done.11.p3 = bf16[48,4992]{1,0:T(8,128)(2,1)S(1)} collective-permute-done((bf16[48,4992]{1,0:T(8,128)(2,1)S(1)}, bf16[48,4992]{1,0:T(8,128)(2,1)S(1)}, u32[]{:S(2)}, u32[]{:S(2)}) %collective-permute-start.11) | collective-permute-done | bytes 479264 | tf_op jit(solution)/shard_map/ppermute | solution.py:575
  56.2 18.7 %feed_forward_both_ways.1 = (bf16[384,3456]{1,0:T(8,128)(2,1)S(1)}, bf16[8,256,384]{2,1,0:T(8,128)(2,1)}, f32[8,256,384]{2,1,0:T(8,128)S(1)}, bf16[8,256,384]{2,...) custom-call(s32[4]{0:T(128)S(1)} %pad_add_fusion.info, ...), custom_call_target="tpu_custom_call" | custom-call | flops 16000000000 | bytes 30000000 | tf_op jit(solution)/shard_map/feed_forward_both_ways/pallas_call | solution.py:479
  75.0 3.9 %collective-permute-done.16.right = bf16[192,5120]{1,0:T(8,128)(2,1)S(1)} collective-permute-done((bf16[192,5120]{1,0:T(8,128)(2,1)S(1)}, bf16[192,5120]{1,0:T(8,128)(2,1)S(1)}, u32[]{:S(2)}, u32[]{:S(2)}) %collective-permute-start.16) | collective-permute-done | bytes 1966112 | tf_op jit(solution)/shard_map/ppermute | solution.py:575
  79.4 15.9 %collective-permute-start.17 = (bf16[48,5120]{1,0:T(8,128)(2,1)S(1)}, bf16[48,5120]{1,0:T(8,128)(2,1)S(1)}, u32[]{:S(2)}, u32[]{:S(2)}) collective-permute-start(bf16[48,5120]{1,0:T(8,128)(2,1)S(1)} %get-tuple-element.92), channel_id=1, source_target_pairs={{0,0},{1,67},{2,2},{3,65},{4,4},{5,71},{6,6},{7,69},{8,8},{9,75},{... | collective-permute-start | bytes 1474568 | tf_op jit(solution)/shard_map/ppermute | solution.py:575
  95.4 2.5 %collective-permute-start.19 = (bf16[48,5120]{1,0:T(8,128)(2,1)S(1)}, bf16[48,5120]{1,0:T(8,128)(2,1)S(1)}, u32[]{:S(2)}, u32[]{:S(2)}) collective-permute-start(bf16[48,5120]{1,0:T(8,128)(2,1)S(1)} %get-tuple-element.99), channel_id=1, source_target_pairs={{0,32},{1,99},{2,34},{3,97},{4,36},{5,103},{6,38},{7,101},{8,40},{... | collective-permute-start | bytes 1474568 | tf_op jit(solution)/shard_map/ppermute | solution.py:575
  97.9 2.6 %collective-permute-start.20 = (bf16[48,5120]{1,0:T(8,128)(2,1)S(1)}, bf16[48,5120]{1,0:T(8,128)(2,1)S(1)}, u32[]{:S(2)}, u32[]{:S(2)}) collective-permute-start(bf16[48,5120]{1,0:T(8,128)(2,1)S(1)} %get-tuple-element.100), channel_id=1, source_target_pairs={{0,48},{1,115},{2,50},{3,113},{4,52},{5,119},{6,54},{7,117},{8,56}... | collective-permute-start | bytes 1474568 | tf_op jit(solution)/shard_map/ppermute | solution.py:575
  100.5 12.5 %attention_backward.1 = (bf16[8,256,384]{2,1,0:T(8,128)(2,1)}, bf16[8,384]{1,0:T(8,128)(2,1)}, bf16[192,2048]{1,0:T(8,128)(2,1)S(1)}, bf16[192,2048]{1,0:T(8,128)(2,1)S(1)}) custom-call(s32[4]{0:T(128)S(1)} %pad_add_fusion.info, bf16[8,256,384]{2,1,0:T(8,128)(2,1)} %latents.5, bf16[8,384]{1,0:T(8,128)(2,1)} %conditions.5, ...), custom_call_target="tpu_custom_call" | custom-call | flops 24999999488 | bytes 20000000 | tf_op jit(solution)/shard_map/attention_backward/pallas_call | solution.py:520
  113.0 9.4 %collective-permute-done.18.refs_1_ = bf16[48,5120]{1,0:T(8,128)(2,1)S(1)} collective-permute-done((bf16[48,5120]{1,0:T(8,128)(2,1)S(1)}, bf16[48,5120]{1,0:T(8,128)(2,1)S(1)}, u32[]{:S(2)}, u32[]{:S(2)}) %collective-permute-start.18) | collective-permute-done | bytes 491552 | tf_op jit(solution)/shard_map/ppermute | solution.py:575
  126.5 2.1 %collective-permute-start.22 = (bf16[48,2048]{1,0:T(8,128)(2,1)S(1)}, bf16[48,2048]{1,0:T(8,128)(2,1)S(1)}, u32[]{:S(2)}, u32[]{:S(2)}) collective-permute-start(bf16[48,2048]{1,0:T(8,128)(2,1)S(1)} %get-tuple-element.102), channel_id=1, source_target_pairs={{0,0},{1,67},{2,2},{3,65},{4,4},{5,71},{6,6},{7,69},{8,8},{9,75},{... | collective-permute-start | bytes 589832 | tf_op jit(solution)/shard_map/ppermute | solution.py:575
  131.1 4.1 %collective-permute-start.25 = (bf16[48,2048]{1,0:T(8,128)(2,1)S(1)}, bf16[48,2048]{1,0:T(8,128)(2,1)S(1)}, u32[]{:S(2)}, u32[]{:S(2)}) collective-permute-start(bf16[48,2048]{1,0:T(8,128)(2,1)S(1)} %get-tuple-element.105), channel_id=1, source_target_pairs={{0,48},{1,115},{2,50},{3,113},{4,52},{5,119},{6,54},{7,117},{8,56}... | collective-permute-start | bytes 589832 | tf_op jit(solution)/shard_map/ppermute | solution.py:575
  135.3 3.3 %collective-permute-start.35 = (bf16[48,2560]{1,0:T(8,128)(2,1)S(1)}, bf16[48,2560]{1,0:T(8,128)(2,1)S(1)}, u32[]{:S(2)}, u32[]{:S(2)}) collective-permute-start(bf16[48,2560]{1,0:T(8,128)(2,1)S(1)} %add.26.refs_0_), channel_id=1, source_target_pairs={{0,8},{1,9},{2,10},{3,11},{4,12},{5,13},{6,14},{7,15},{8,0},{9,1},... | collective-permute-start | bytes 737288 | tf_op jit(solution)/shard_map/ppermute | solution.py:575
  138.6 3.4 %collective-permute-done.23.refs_1_ = bf16[48,2048]{1,0:T(8,128)(2,1)S(1)} collective-permute-done((bf16[48,2048]{1,0:T(8,128)(2,1)S(1)}, bf16[48,2048]{1,0:T(8,128)(2,1)S(1)}, u32[]{:S(2)}, u32[]{:S(2)}) %collective-permute-start.23) | collective-permute-done | bytes 196640 | tf_op jit(solution)/shard_map/ppermute | solution.py:575
  145.6 4.5 %collective-permute-done.34.refs_1_ = bf16[48,2560]{1,0:T(8,128)(2,1)S(1)} collective-permute-done((bf16[48,2560]{1,0:T(8,128)(2,1)S(1)}, bf16[48,2560]{1,0:T(8,128)(2,1)S(1)}, u32[]{:S(2)}, u32[]{:S(2)}) %collective-permute-start.34) | collective-permute-done | bytes 245792 | tf_op jit(solution)/shard_map/ppermute | solution.py:575
  151.7 2.1 %collective-permute-start.29 = (bf16[48,1024]{1,0:T(8,128)(2,1)S(1)}, bf16[48,1024]{1,0:T(8,128)(2,1)S(1)}, u32[]{:S(2)}, u32[]{:S(2)}) collective-permute-start(bf16[48,1024]{1,0:T(8,128)(2,1)S(1)} %add.23.refs_0_), channel_id=1, source_target_pairs={{0,8},{1,9},{2,10},{3,11},{4,12},{5,13},{6,14},{7,15},{8,0},{9,1},... | collective-permute-start | bytes 294920 | tf_op jit(solution)/shard_map/ppermute | solution.py:575
  154.5 2.2 %collective-permute-done.29.refs_2_ = bf16[48,1024]{1,0:T(8,128)(2,1)S(1)} collective-permute-done((bf16[48,1024]{1,0:T(8,128)(2,1)S(1)}, bf16[48,1024]{1,0:T(8,128)(2,1)S(1)}, u32[]{:S(2)}, u32[]{:S(2)}) %collective-permute-start.29) | collective-permute-done | bytes 98336 | tf_op jit(solution)/shard_map/ppermute | solution.py:575
  156.7 3.3 %collective-permute-done.28.refs_1_ = bf16[48,1024]{1,0:T(8,128)(2,1)S(1)} collective-permute-done((bf16[48,1024]{1,0:T(8,128)(2,1)S(1)}, bf16[48,1024]{1,0:T(8,128)(2,1)S(1)}, u32[]{:S(2)}, u32[]{:S(2)}) %collective-permute-start.28) | collective-permute-done | bytes 98336 | tf_op jit(solution)/shard_map/ppermute | solution.py:575
  (70 shorter events, 29.6 us)
Async XLA Ops:
  2.5 13.2 %collective-permute-start = (bf16[48,2048]{1,0:T(8,128)(2,1)S(1)}, bf16[48,2048]{1,0:T(8,128)(2,1)S(1)}, u32[]{:S(2)}, u32[]{:S(2)}) collective-permute-start(bf16[48,2048]{1,0:T(8,128)(2,1)S(1)} %pack_attention_weights.1), channel_id=1, source_target_pairs={{0,0},{67,1},{2,2},{65,3},{4,4},{71,5},{6,6},{69,7},{8,8},{75,9},{... | collective-permute-start | bytes 589832 | tf_op jit(solution)/shard_map/ppermute | solution.py:575
  9.0 8.8 %collective-permute-start.1 = (bf16[48,2048]{1,0:T(8,128)(2,1)S(1)}, bf16[48,2048]{1,0:T(8,128)(2,1)S(1)}, u32[]{:S(2)}, u32[]{:S(2)}) collective-permute-start(bf16[48,2048]{1,0:T(8,128)(2,1)S(1)} %pack_attention_weights.1), channel_id=1, source_target_pairs={{16,0},{83,1},{18,2},{81,3},{20,4},{87,5},{22,6},{85,7},{24,8},{91... | collective-permute-start | bytes 589832 | tf_op jit(solution)/shard_map/ppermute | solution.py:575
  11.2 10.3 %collective-permute-start.2 = (bf16[48,2048]{1,0:T(8,128)(2,1)S(1)}, bf16[48,2048]{1,0:T(8,128)(2,1)S(1)}, u32[]{:S(2)}, u32[]{:S(2)}) collective-permute-start(bf16[48,2048]{1,0:T(8,128)(2,1)S(1)} %pack_attention_weights.1), channel_id=1, source_target_pairs={{32,0},{99,1},{34,2},{97,3},{36,4},{103,5},{38,6},{101,7},{40,8},{... | collective-permute-start | bytes 589832 | tf_op jit(solution)/shard_map/ppermute | solution.py:575
  14.1 9.9 %collective-permute-start.3 = (bf16[48,2048]{1,0:T(8,128)(2,1)S(1)}, bf16[48,2048]{1,0:T(8,128)(2,1)S(1)}, u32[]{:S(2)}, u32[]{:S(2)}) collective-permute-start(bf16[48,2048]{1,0:T(8,128)(2,1)S(1)} %pack_attention_weights.1), channel_id=1, source_target_pairs={{48,0},{115,1},{50,2},{113,3},{52,4},{119,5},{54,6},{117,7},{56,8}... | collective-permute-start | bytes 589832 | tf_op jit(solution)/shard_map/ppermute | solution.py:575
  15.6 11.3 %collective-permute-start.4 = (bf16[48,2048]{1,0:T(8,128)(2,1)S(1)}, bf16[48,2048]{1,0:T(8,128)(2,1)S(1)}, u32[]{:S(2)}, u32[]{:S(2)}) collective-permute-start(bf16[48,2048]{1,0:T(8,128)(2,1)S(1)} %collective-permute-done.p0), channel_id=1, source_target_pairs={{0,1},{1,0},{2,3},{3,2},{4,5},{5,4},{6,7},{7,6},{8,9},{9,8},{10,11... | collective-permute-start | bytes 589832 | tf_op jit(solution)/shard_map/ppermute | solution.py:575
  17.8 12.3 %collective-permute-start.5 = (bf16[48,2048]{1,0:T(8,128)(2,1)S(1)}, bf16[48,2048]{1,0:T(8,128)(2,1)S(1)}, u32[]{:S(2)}, u32[]{:S(2)}) collective-permute-start(bf16[48,2048]{1,0:T(8,128)(2,1)S(1)} %collective-permute-done.1.p1), channel_id=1, source_target_pairs={{0,1},{1,0},{2,3},{3,2},{4,5},{5,4},{6,7},{7,6},{8,9},{9,8},{10,11... | collective-permute-start | bytes 589832 | tf_op jit(solution)/shard_map/ppermute | solution.py:575
  21.6 9.2 %collective-permute-start.6 = (bf16[48,2048]{1,0:T(8,128)(2,1)S(1)}, bf16[48,2048]{1,0:T(8,128)(2,1)S(1)}, u32[]{:S(2)}, u32[]{:S(2)}) collective-permute-start(bf16[48,2048]{1,0:T(8,128)(2,1)S(1)} %collective-permute-done.2.p2), channel_id=1, source_target_pairs={{0,1},{1,0},{2,3},{3,2},{4,5},{5,4},{6,7},{7,6},{8,9},{9,8},{10,11... | collective-permute-start | bytes 589832 | tf_op jit(solution)/shard_map/ppermute | solution.py:575
  21.6 16.5 %collective-permute-start.8 = (bf16[48,4992]{1,0:T(8,128)(2,1)S(1)}, bf16[48,4992]{1,0:T(8,128)(2,1)S(1)}, u32[]{:S(2)}, u32[]{:S(2)}) collective-permute-start(bf16[48,4992]{1,0:T(8,128)(2,1)S(1)} %pack_feed_forward_weights.1), channel_id=1, source_target_pairs={{0,0},{67,1},{2,2},{65,3},{4,4},{71,5},{6,6},{69,7},{8,8},{75,9},{... | collective-permute-start | bytes 1437704 | tf_op jit(solution)/shard_map/ppermute | solution.py:575
  24.1 26.9 %collective-permute-start.11 = (bf16[48,4992]{1,0:T(8,128)(2,1)S(1)}, bf16[48,4992]{1,0:T(8,128)(2,1)S(1)}, u32[]{:S(2)}, u32[]{:S(2)}) collective-permute-start(bf16[48,4992]{1,0:T(8,128)(2,1)S(1)} %pack_feed_forward_weights.1), channel_id=1, source_target_pairs={{48,0},{115,1},{50,2},{113,3},{52,4},{119,5},{54,6},{117,7},{56,8}... | collective-permute-start | bytes 1437704 | tf_op jit(solution)/shard_map/ppermute | solution.py:575
  27.0 24.0 %collective-permute-start.10 = (bf16[48,4992]{1,0:T(8,128)(2,1)S(1)}, bf16[48,4992]{1,0:T(8,128)(2,1)S(1)}, u32[]{:S(2)}, u32[]{:S(2)}) collective-permute-start(bf16[48,4992]{1,0:T(8,128)(2,1)S(1)} %pack_feed_forward_weights.1), channel_id=1, source_target_pairs={{32,0},{99,1},{34,2},{97,3},{36,4},{103,5},{38,6},{101,7},{40,8},{... | collective-permute-start | bytes 1437704 | tf_op jit(solution)/shard_map/ppermute | solution.py:575
  30.1 22.8 %collective-permute-start.9 = (bf16[48,4992]{1,0:T(8,128)(2,1)S(1)}, bf16[48,4992]{1,0:T(8,128)(2,1)S(1)}, u32[]{:S(2)}, u32[]{:S(2)}) collective-permute-start(bf16[48,4992]{1,0:T(8,128)(2,1)S(1)} %pack_feed_forward_weights.1), channel_id=1, source_target_pairs={{16,0},{83,1},{18,2},{81,3},{20,4},{87,5},{22,6},{85,7},{24,8},{91... | collective-permute-start | bytes 1437704 | tf_op jit(solution)/shard_map/ppermute | solution.py:575
  38.1 15.4 %collective-permute-start.12 = (bf16[48,4992]{1,0:T(8,128)(2,1)S(1)}, bf16[48,4992]{1,0:T(8,128)(2,1)S(1)}, u32[]{:S(2)}, u32[]{:S(2)}) collective-permute-start(bf16[48,4992]{1,0:T(8,128)(2,1)S(1)} %collective-permute-done.8.p0), channel_id=1, source_target_pairs={{0,1},{1,0},{2,3},{3,2},{4,5},{5,4},{6,7},{7,6},{8,9},{9,8},{10,11... | collective-permute-start | bytes 1437704 | tf_op jit(solution)/shard_map/ppermute | solution.py:575
  79.4 44.1 %collective-permute-start.17 = (bf16[48,5120]{1,0:T(8,128)(2,1)S(1)}, bf16[48,5120]{1,0:T(8,128)(2,1)S(1)}, u32[]{:S(2)}, u32[]{:S(2)}) collective-permute-start(bf16[48,5120]{1,0:T(8,128)(2,1)S(1)} %get-tuple-element.92), channel_id=1, source_target_pairs={{0,0},{1,67},{2,2},{3,65},{4,4},{5,71},{6,6},{7,69},{8,8},{9,75},{... | collective-permute-start | bytes 1474568 | tf_op jit(solution)/shard_map/ppermute | solution.py:575
  95.3 27.1 %collective-permute-start.18 = (bf16[48,5120]{1,0:T(8,128)(2,1)S(1)}, bf16[48,5120]{1,0:T(8,128)(2,1)S(1)}, u32[]{:S(2)}, u32[]{:S(2)}) collective-permute-start(bf16[48,5120]{1,0:T(8,128)(2,1)S(1)} %get-tuple-element.98), channel_id=1, source_target_pairs={{0,16},{1,83},{2,18},{3,81},{4,20},{5,87},{6,22},{7,85},{8,24},{9,... | collective-permute-start | bytes 1474568 | tf_op jit(solution)/shard_map/ppermute | solution.py:575
  95.4 27.0 %collective-permute-start.19 = (bf16[48,5120]{1,0:T(8,128)(2,1)S(1)}, bf16[48,5120]{1,0:T(8,128)(2,1)S(1)}, u32[]{:S(2)}, u32[]{:S(2)}) collective-permute-start(bf16[48,5120]{1,0:T(8,128)(2,1)S(1)} %get-tuple-element.99), channel_id=1, source_target_pairs={{0,32},{1,99},{2,34},{3,97},{4,36},{5,103},{6,38},{7,101},{8,40},{... | collective-permute-start | bytes 1474568 | tf_op jit(solution)/shard_map/ppermute | solution.py:575
  97.9 25.6 %collective-permute-start.20 = (bf16[48,5120]{1,0:T(8,128)(2,1)S(1)}, bf16[48,5120]{1,0:T(8,128)(2,1)S(1)}, u32[]{:S(2)}, u32[]{:S(2)}) collective-permute-start(bf16[48,5120]{1,0:T(8,128)(2,1)S(1)} %get-tuple-element.100), channel_id=1, source_target_pairs={{0,48},{1,115},{2,50},{3,113},{4,52},{5,119},{6,54},{7,117},{8,56}... | collective-permute-start | bytes 1474568 | tf_op jit(solution)/shard_map/ppermute | solution.py:575
  126.4 8.7 %collective-permute-start.33 = (bf16[48,2560]{1,0:T(8,128)(2,1)S(1)}, bf16[48,2560]{1,0:T(8,128)(2,1)S(1)}, u32[]{:S(2)}, u32[]{:S(2)}) collective-permute-start(bf16[48,2560]{1,0:T(8,128)(2,1)S(1)} %add.25.refs_0_), channel_id=1, source_target_pairs={{0,2},{1,3},{2,0},{3,1},{4,6},{5,7},{6,4},{7,5},{8,10},{9,11},{10,... | collective-permute-start | bytes 737288 | tf_op jit(solution)/shard_map/ppermute | solution.py:575
  126.5 8.8 %collective-permute-start.22 = (bf16[48,2048]{1,0:T(8,128)(2,1)S(1)}, bf16[48,2048]{1,0:T(8,128)(2,1)S(1)}, u32[]{:S(2)}, u32[]{:S(2)}) collective-permute-start(bf16[48,2048]{1,0:T(8,128)(2,1)S(1)} %get-tuple-element.102), channel_id=1, source_target_pairs={{0,0},{1,67},{2,2},{3,65},{4,4},{5,71},{6,6},{7,69},{8,8},{9,75},{... | collective-permute-start | bytes 589832 | tf_op jit(solution)/shard_map/ppermute | solution.py:575
  128.7 13.3 %collective-permute-start.23 = (bf16[48,2048]{1,0:T(8,128)(2,1)S(1)}, bf16[48,2048]{1,0:T(8,128)(2,1)S(1)}, u32[]{:S(2)}, u32[]{:S(2)}) collective-permute-start(bf16[48,2048]{1,0:T(8,128)(2,1)S(1)} %get-tuple-element.103), channel_id=1, source_target_pairs={{0,16},{1,83},{2,18},{3,81},{4,20},{5,87},{6,22},{7,85},{8,24},{9,... | collective-permute-start | bytes 589832 | tf_op jit(solution)/shard_map/ppermute | solution.py:575
  129.5 14.0 %collective-permute-start.24 = (bf16[48,2048]{1,0:T(8,128)(2,1)S(1)}, bf16[48,2048]{1,0:T(8,128)(2,1)S(1)}, u32[]{:S(2)}, u32[]{:S(2)}) collective-permute-start(bf16[48,2048]{1,0:T(8,128)(2,1)S(1)} %get-tuple-element.104), channel_id=1, source_target_pairs={{0,32},{1,99},{2,34},{3,97},{4,36},{5,103},{6,38},{7,101},{8,40},{... | collective-permute-start | bytes 589832 | tf_op jit(solution)/shard_map/ppermute | solution.py:575
  131.1 12.4 %collective-permute-start.25 = (bf16[48,2048]{1,0:T(8,128)(2,1)S(1)}, bf16[48,2048]{1,0:T(8,128)(2,1)S(1)}, u32[]{:S(2)}, u32[]{:S(2)}) collective-permute-start(bf16[48,2048]{1,0:T(8,128)(2,1)S(1)} %get-tuple-element.105), channel_id=1, source_target_pairs={{0,48},{1,115},{2,50},{3,113},{4,52},{5,119},{6,54},{7,117},{8,56}... | collective-permute-start | bytes 589832 | tf_op jit(solution)/shard_map/ppermute | solution.py:575
  135.2 10.4 %collective-permute-start.36 = (bf16[48,2560]{1,0:T(8,128)(2,1)S(1)}, bf16[48,2560]{1,0:T(8,128)(2,1)S(1)}, u32[]{:S(2)}, u32[]{:S(2)}) collective-permute-start(bf16[48,2560]{1,0:T(8,128)(2,1)S(1)} %add.26.refs_0_), channel_id=1, source_target_pairs={{0,12},{1,13},{2,14},{3,15},{4,0},{5,1},{6,2},{7,3},{8,4},{9,5},{1... | collective-permute-start | bytes 737288 | tf_op jit(solution)/shard_map/ppermute | solution.py:575
  135.3 10.3 %collective-permute-start.35 = (bf16[48,2560]{1,0:T(8,128)(2,1)S(1)}, bf16[48,2560]{1,0:T(8,128)(2,1)S(1)}, u32[]{:S(2)}, u32[]{:S(2)}) collective-permute-start(bf16[48,2560]{1,0:T(8,128)(2,1)S(1)} %add.26.refs_0_), channel_id=1, source_target_pairs={{0,8},{1,9},{2,10},{3,11},{4,12},{5,13},{6,14},{7,15},{8,0},{9,1},... | collective-permute-start | bytes 737288 | tf_op jit(solution)/shard_map/ppermute | solution.py:575
  150.2 10.9 %collective-permute-start.37 = (bf16[48,2560]{1,0:T(8,128)(2,1)S(1)}, bf16[48,2560]{1,0:T(8,128)(2,1)S(1)}, u32[]{:S(2)}, u32[]{:S(2)}) collective-permute-start(bf16[48,2560]{1,0:T(8,128)(2,1)S(1)} %add.27.mine), channel_id=1, source_target_pairs={{0,1},{1,0},{2,3},{3,2},{4,5},{5,4},{6,7},{7,6},{8,9},{9,8},{10,11... | collective-permute-start | bytes 737288 | tf_op jit(solution)/shard_map/ppermute | solution.py:575
  (14 other events, 49.3 us)

commit v6 on v5

--- a/solution.py
+++ b/solution.py
@@ -640,13 +640,17 @@
     return [move(block, pairs) for block, pairs in zip(blocks, back)]
 
 
-def sum_replicas(arrived, info, *earlier):
+def sum_low(arrived, info, *earlier):
     mine, other = add_halves(info, arrived)
     total = add(mine, move(other, CORE_SWAP))
     if earlier:
         total = after(total, *earlier)
-    total = add(total, move(total, ZLOW_SWAP))
-    total = add(total, *(move(total, y_route(k)) for k in (1, 2, 3)))
+    return add(total, move(total, ZLOW_SWAP))
+
+
+def sum_rows(total, *earlier):
+    rows = [move(total, y_route(k)) for k in (1, 2, 3)]
+    total = add(after(total, *earlier), *rows)
     return [total, move(total, CORE_SWAP)]
 
 
@@ -728,16 +732,22 @@
     own(bias_row(bias, ROW_DOWN, 3), 48, g_down_bias)
 
 
-def finish(info, one, two):
-    scalars = pl.BlockSpec(memory_space=pltpu.SMEM)
+SCALARS = pl.BlockSpec(memory_space=pltpu.SMEM)
+
+
+def unpack_two(info, parts):
     shapes = [(48, 6 * D), (48, D), (48, FF), (192, D), (48, 128)]
-    g_mod, g_proj, g_up, g_down, bias_two = pl.pallas_call(
+    return pl.pallas_call(
         unpack_two_kernel,
-        in_specs=[scalars] + [held()] * 2,
+        in_specs=[SCALARS] + [held()] * 2,
         out_shape=[jax.ShapeDtypeStruct(shape, F32) for shape in shapes],
         compiler_params=pltpu.CompilerParams(vmem_limit_bytes=12 * MIB),
         name="unpack_second_batch",
-    )(info, *two)
+    )(info, *parts)
+
+
+def unpack_one(info, parts, from_two):
+    g_mod, g_proj, g_up, g_down, bias_two = from_two
     shapes = [(48, 6 * D), (288,), (48, QKV_W), (96,), (48,), (192,), (48,)]
 
     def once(shape):
@@ -746,13 +756,13 @@
     g_mod, g_mod_bias, g_qkv, g_qv_bias, g_proj_bias, g_up_bias, g_down_bias = pl.pallas_call(
         unpack_one_kernel,
         grid=(1,),
-        in_specs=[scalars] + [held()] * 3 + [pl.BlockSpec(memory_space=pl.ANY)],
+        in_specs=[SCALARS] + [held()] * 3 + [pl.BlockSpec(memory_space=pl.ANY)],
         out_specs=[once((48, MOD_ONE))] + [once(shape) for shape in shapes[1:]],
         out_shape=[jax.ShapeDtypeStruct(shape, F32) for shape in shapes],
         input_output_aliases={4: 0},
         compiler_params=pltpu.CompilerParams(vmem_limit_bytes=8 * MIB),
         name="unpack_first_batch",
-    )(info, *one, bias_two, g_mod)
+    )(info, *parts, bias_two, g_mod)
     return (
         g_mod, g_mod_bias, g_qkv, g_qv_bias, g_proj, g_proj_bias, g_up, g_up_bias, g_down,
         g_down_bias,
@@ -795,9 +805,11 @@
     )
     held_one = add_blocks(keep_one, move(after(send_one, *arrived_two), CORE_SWAP))
     arrived_one = scatter(held_one)
-    two = sum_replicas(arrived_two, info, *held_one)
-    one = sum_replicas(arrived_one, info)
-    return (out, grad_latents, grad_cond, *finish(info, one, two))
+    low_two = sum_low(arrived_two, info, *held_one)
+    low_one = sum_low(arrived_one, info)
+    from_two = unpack_two(info, sum_rows(low_two, low_one))
+    one = sum_rows(low_one, from_two[1])
+    return (out, grad_latents, grad_cond, *unpack_one(info, one, from_two))
 
 
 def solution(mesh):

time: 164 us -> 165 us (level)
  Pallas kernels: 44.7 us -> 19 us
  starting transfers between devices: 62.7 us -> 84.5 us
  waiting for transfers between devices: 55 us -> 59.3 us
    ppermute x38, starting transfers between devices: 62.7 us -> 84.5 us  [move(): return lax.ppermute(value, BOTH, pairs)]
    pallas_call x1, Pallas kernels: 18.7 us -> 5.53 us  [run_middle(): pl.pallas_call(middle_kernel, grid_spec=pltpu.PrefetchScalarGridSpec(num_...]
    pallas_call x1, Pallas kernels: 12.5 us -> 3.83 us  [run_backward(): pl.pallas_call(backward_kernel, grid_spec=pltpu.PrefetchScalarGridSpec(nu...]
    ppermute x38, waiting for transfers between devices: 55 us -> 59.3 us  [move(): return lax.ppermute(value, BOTH, pairs)]
    pallas_call x1, Pallas kernels: 5.85 us -> 2.05 us  [run_forward(): pl.pallas_call(forward_kernel, grid_spec=pltpu.PrefetchScalarGridSpec(num...]
  transfers between devices with their start and end apart: 38 -> 38, of which waited for: 17 -> 18; matrix products, arithmetic and copies ran while one was open for 0% -> 0% of each run, Pallas kernels for 14% -> 6%
where the time goes in v6:
time: 165 us; the launch traced here: 164 us
  starting transfers between devices  84.5 us (51%)
  waiting for transfers between devices  59.3 us (36%)
  Pallas kernels  19 us (12%)
    ppermute x38, starting transfers between devices, move(): return lax.ppermute(value, BOTH, pairs)  84.5 us
    ppermute x38, waiting for transfers between devices, move(): return lax.ppermute(value, BOTH, pairs)  59.3 us
    pallas_call x1, Pallas kernels, run_middle(): pl.pallas_call(middle_kernel, grid_spec=pltpu.PrefetchScalarGridSpec(num_...  5.53 us
    pallas_call x1, Pallas kernels, run_backward(): pl.pallas_call(backward_kernel, grid_spec=pltpu.PrefetchScalarGridSpec(nu...  3.83 us
  transfers between devices with their start and end apart: 38, of which 18 were waited for; matrix products, arithmetic and copies ran while one was open for 0% of the time, Pallas kernels for 6%

profile of v6, /device:TPU:1, one launch (start us, length us, event | category | flops | bytes accessed | tf_op | source)
XLA Modules:
  0.0 164.4 jit_solution(751605475857953894)
XLA Ops:
  2.5 6.5 %collective-permute-start = (bf16[48,2048]{1,0:T(8,128)(2,1)S(1)}, bf16[48,2048]{1,0:T(8,128)(2,1)S(1)}, u32[]{:S(2)}, u32[]{:S(2)}) collective-permute-start(bf16[48,2048]{1,0:T(8,128)(2,1)S(1)} %pack_attention_weights.1), channel_id=1, source_target_pairs={{0,0},{67,1},{2,2},{65,3},{4,4},{71,5},{6,6},{69,7},{8,8},{75,9},{... | collective-permute-start | bytes 589832 | tf_op jit(solution)/shard_map/ppermute | solution.py:575
  11.2 2.9 %collective-permute-start.2 = (bf16[48,2048]{1,0:T(8,128)(2,1)S(1)}, bf16[48,2048]{1,0:T(8,128)(2,1)S(1)}, u32[]{:S(2)}, u32[]{:S(2)}) collective-permute-start(bf16[48,2048]{1,0:T(8,128)(2,1)S(1)} %pack_attention_weights.1), channel_id=1, source_target_pairs={{32,0},{99,1},{34,2},{97,3},{36,4},{103,5},{38,6},{101,7},{40,8},{... | collective-permute-start | bytes 589832 | tf_op jit(solution)/shard_map/ppermute | solution.py:575
  17.8 3.8 %collective-permute-done.2.p2 = bf16[48,2048]{1,0:T(8,128)(2,1)S(1)} collective-permute-done((bf16[48,2048]{1,0:T(8,128)(2,1)S(1)}, bf16[48,2048]{1,0:T(8,128)(2,1)S(1)}, u32[]{:S(2)}, u32[]{:S(2)}) %collective-permute-start.2) | collective-permute-done | bytes 196640 | tf_op jit(solution)/shard_map/ppermute | solution.py:575
  21.6 2.5 %collective-permute-start.8 = (bf16[48,4992]{1,0:T(8,128)(2,1)S(1)}, bf16[48,4992]{1,0:T(8,128)(2,1)S(1)}, u32[]{:S(2)}, u32[]{:S(2)}) collective-permute-start(bf16[48,4992]{1,0:T(8,128)(2,1)S(1)} %pack_feed_forward_weights.1), channel_id=1, source_target_pairs={{0,0},{67,1},{2,2},{65,3},{4,4},{71,5},{6,6},{69,7},{8,8},{75,9},{... | collective-permute-start | bytes 1437704 | tf_op jit(solution)/shard_map/ppermute | solution.py:575
  24.1 2.9 %collective-permute-start.11 = (bf16[48,4992]{1,0:T(8,128)(2,1)S(1)}, bf16[48,4992]{1,0:T(8,128)(2,1)S(1)}, u32[]{:S(2)}, u32[]{:S(2)}) collective-permute-start(bf16[48,4992]{1,0:T(8,128)(2,1)S(1)} %pack_feed_forward_weights.1), channel_id=1, source_target_pairs={{48,0},{115,1},{50,2},{113,3},{52,4},{119,5},{54,6},{117,7},{56,8}... | collective-permute-start | bytes 1437704 | tf_op jit(solution)/shard_map/ppermute | solution.py:575
  27.0 3.1 %collective-permute-start.10 = (bf16[48,4992]{1,0:T(8,128)(2,1)S(1)}, bf16[48,4992]{1,0:T(8,128)(2,1)S(1)}, u32[]{:S(2)}, u32[]{:S(2)}) collective-permute-start(bf16[48,4992]{1,0:T(8,128)(2,1)S(1)} %pack_feed_forward_weights.1), channel_id=1, source_target_pairs={{32,0},{99,1},{34,2},{97,3},{36,4},{103,5},{38,6},{101,7},{40,8},{... | collective-permute-start | bytes 1437704 | tf_op jit(solution)/shard_map/ppermute | solution.py:575
  34.3 7.8 %collective-permute-start.12 = (bf16[48,4992]{1,0:T(8,128)(2,1)S(1)}, bf16[48,4992]{1,0:T(8,128)(2,1)S(1)}, u32[]{:S(2)}, u32[]{:S(2)}) collective-permute-start(bf16[48,4992]{1,0:T(8,128)(2,1)S(1)} %collective-permute-done.8.p0), channel_id=1, source_target_pairs={{0,1},{1,0},{2,3},{3,2},{4,5},{5,4},{6,7},{7,6},{8,9},{9,8},{10,11... | collective-permute-start | bytes 1437704 | tf_op jit(solution)/shard_map/ppermute | solution.py:575
  42.1 8.9 %collective-permute-done.11.p3 = bf16[48,4992]{1,0:T(8,128)(2,1)S(1)} collective-permute-done((bf16[48,4992]{1,0:T(8,128)(2,1)S(1)}, bf16[48,4992]{1,0:T(8,128)(2,1)S(1)}, u32[]{:S(2)}, u32[]{:S(2)}) %collective-permute-start.11) | collective-permute-done | bytes 479264 | tf_op jit(solution)/shard_map/ppermute | solution.py:575
  56.2 5.5 %feed_forward_both_ways.1 = (bf16[384,3456]{1,0:T(8,128)(2,1)S(1)}, bf16[8,256,384]{2,1,0:T(8,128)(2,1)}, f32[8,256,384]{2,1,0:T(8,128)S(1)}, bf16[8,256,384]{2,...) custom-call(s32[4]{0:T(128)S(1)} %pad_add_fusion.info, ...), custom_call_target="tpu_custom_call" | custom-call | flops 16000000000 | bytes 30000000 | tf_op jit(solution)/shard_map/feed_forward_both_ways/pallas_call | solution.py:479
  61.7 19.7 %collective-permute-start.16 = (bf16[192,5120]{1,0:T(8,128)(2,1)S(1)}, bf16[192,5120]{1,0:T(8,128)(2,1)S(1)}, u32[]{:S(2)}, u32[]{:S(2)}) collective-permute-start(bf16[192,5120]{1,0:T(8,128)(2,1)S(1)} %get-tuple-element.93), channel_id=1, source_target_pairs={{0,1},{1,0},{2,3},{3,2},{4,5},{5,4},{6,7},{7,6},{8,9},{9,8},{10,11... | collective-permute-start | bytes 5898248 | tf_op jit(solution)/shard_map/ppermute | solution.py:575
  81.4 3.6 %collective-permute-done.16.right = bf16[192,5120]{1,0:T(8,128)(2,1)S(1)} collective-permute-done((bf16[192,5120]{1,0:T(8,128)(2,1)S(1)}, bf16[192,5120]{1,0:T(8,128)(2,1)S(1)}, u32[]{:S(2)}, u32[]{:S(2)}) %collective-permute-start.16) | collective-permute-done | bytes 1966112 | tf_op jit(solution)/shard_map/ppermute | solution.py:575
  85.5 3.3 %collective-permute-start.17 = (bf16[48,5120]{1,0:T(8,128)(2,1)S(1)}, bf16[48,5120]{1,0:T(8,128)(2,1)S(1)}, u32[]{:S(2)}, u32[]{:S(2)}) collective-permute-start(bf16[48,5120]{1,0:T(8,128)(2,1)S(1)} %get-tuple-element.94), channel_id=1, source_target_pairs={{0,0},{1,67},{2,2},{3,65},{4,4},{5,71},{6,6},{7,69},{8,8},{9,75},{... | collective-permute-start | bytes 1474568 | tf_op jit(solution)/shard_map/ppermute | solution.py:575
  88.9 2.4 %collective-permute-start.19 = (bf16[48,5120]{1,0:T(8,128)(2,1)S(1)}, bf16[48,5120]{1,0:T(8,128)(2,1)S(1)}, u32[]{:S(2)}, u32[]{:S(2)}) collective-permute-start(bf16[48,5120]{1,0:T(8,128)(2,1)S(1)} %get-tuple-element.101), channel_id=1, source_target_pairs={{0,32},{1,99},{2,34},{3,97},{4,36},{5,103},{6,38},{7,101},{8,40},{... | collective-permute-start | bytes 1474568 | tf_op jit(solution)/shard_map/ppermute | solution.py:575
  91.3 2.3 %collective-permute-start.20 = (bf16[48,5120]{1,0:T(8,128)(2,1)S(1)}, bf16[48,5120]{1,0:T(8,128)(2,1)S(1)}, u32[]{:S(2)}, u32[]{:S(2)}) collective-permute-start(bf16[48,5120]{1,0:T(8,128)(2,1)S(1)} %get-tuple-element.102), channel_id=1, source_target_pairs={{0,48},{1,115},{2,50},{3,113},{4,52},{5,119},{6,54},{7,117},{8,56}... | collective-permute-start | bytes 1474568 | tf_op jit(solution)/shard_map/ppermute | solution.py:575
  93.7 3.8 %attention_backward.1 = (bf16[8,256,384]{2,1,0:T(8,128)(2,1)}, bf16[8,384]{1,0:T(8,128)(2,1)}, bf16[192,2048]{1,0:T(8,128)(2,1)S(1)}, bf16[192,2048]{1,0:T(8,128)(2,1)S(1)}) custom-call(s32[4]{0:T(128)S(1)} %pad_add_fusion.info, bf16[8,256,384]{2,1,0:T(8,128)(2,1)} %latents.5, bf16[8,384]{1,0:T(8,128)(2,1)} %conditions.5, ...), custom_call_target="tpu_custom_call" | custom-call | flops 24999999488 | bytes 20000000 | tf_op jit(solution)/shard_map/attention_backward/pallas_call | solution.py:520
  97.5 18.4 %collective-permute-done.18.refs_1_ = bf16[48,5120]{1,0:T(8,128)(2,1)S(1)} collective-permute-done((bf16[48,5120]{1,0:T(8,128)(2,1)S(1)}, bf16[48,5120]{1,0:T(8,128)(2,1)S(1)}, u32[]{:S(2)}, u32[]{:S(2)}) %collective-permute-start.18) | collective-permute-done | bytes 491552 | tf_op jit(solution)/shard_map/ppermute | solution.py:575
  122.0 3.7 %collective-permute-start.22 = (bf16[48,2048]{1,0:T(8,128)(2,1)S(1)}, bf16[48,2048]{1,0:T(8,128)(2,1)S(1)}, u32[]{:S(2)}, u32[]{:S(2)}) collective-permute-start(bf16[48,2048]{1,0:T(8,128)(2,1)S(1)} %get-tuple-element.104), channel_id=1, source_target_pairs={{0,0},{1,67},{2,2},{3,65},{4,4},{5,71},{6,6},{7,69},{8,8},{9,75},{... | collective-permute-start | bytes 589832 | tf_op jit(solution)/shard_map/ppermute | solution.py:575
  125.8 3.4 %collective-permute-start.24 = (bf16[48,2048]{1,0:T(8,128)(2,1)S(1)}, bf16[48,2048]{1,0:T(8,128)(2,1)S(1)}, u32[]{:S(2)}, u32[]{:S(2)}) collective-permute-start(bf16[48,2048]{1,0:T(8,128)(2,1)S(1)} %get-tuple-element.106), channel_id=1, source_target_pairs={{0,32},{1,99},{2,34},{3,97},{4,36},{5,103},{6,38},{7,101},{8,40},{... | collective-permute-start | bytes 589832 | tf_op jit(solution)/shard_map/ppermute | solution.py:575
  130.7 6.7 %collective-permute-start.32 = (bf16[48,2560]{1,0:T(8,128)(2,1)S(1)}, bf16[48,2560]{1,0:T(8,128)(2,1)S(1)}, u32[]{:S(2)}, u32[]{:S(2)}) collective-permute-start(bf16[48,2560]{1,0:T(8,128)(2,1)S(1)} %add.25.refs_0_), channel_id=1, source_target_pairs={{0,12},{1,13},{2,14},{3,15},{4,0},{5,1},{6,2},{7,3},{8,4},{9,5},{1... | collective-permute-start | bytes 737288 | tf_op jit(solution)/shard_map/ppermute | solution.py:575
  137.5 2.6 %collective-permute-start.31 = (bf16[48,2560]{1,0:T(8,128)(2,1)S(1)}, bf16[48,2560]{1,0:T(8,128)(2,1)S(1)}, u32[]{:S(2)}, u32[]{:S(2)}) collective-permute-start(bf16[48,2560]{1,0:T(8,128)(2,1)S(1)} %add.25.refs_0_), channel_id=1, source_target_pairs={{0,8},{1,9},{2,10},{3,11},{4,12},{5,13},{6,14},{7,15},{8,0},{9,1},... | collective-permute-start | bytes 737288 | tf_op jit(solution)/shard_map/ppermute | solution.py:575
  143.7 3.3 %collective-permute-done.27.refs_1_ = bf16[48,1024]{1,0:T(8,128)(2,1)S(1)} collective-permute-done((bf16[48,1024]{1,0:T(8,128)(2,1)S(1)}, bf16[48,1024]{1,0:T(8,128)(2,1)S(1)}, u32[]{:S(2)}, u32[]{:S(2)}) %collective-permute-start.27) | collective-permute-done | bytes 98336 | tf_op jit(solution)/shard_map/ppermute | solution.py:575
  147.1 3.4 %collective-permute-done.30.refs_1_ = bf16[48,2560]{1,0:T(8,128)(2,1)S(1)} collective-permute-done((bf16[48,2560]{1,0:T(8,128)(2,1)S(1)}, bf16[48,2560]{1,0:T(8,128)(2,1)S(1)}, u32[]{:S(2)}, u32[]{:S(2)}) %collective-permute-start.30) | collective-permute-done | bytes 245792 | tf_op jit(solution)/shard_map/ppermute | solution.py:575
  150.7 2.5 %collective-permute-start.36 = (bf16[48,1024]{1,0:T(8,128)(2,1)S(1)}, bf16[48,1024]{1,0:T(8,128)(2,1)S(1)}, u32[]{:S(2)}, u32[]{:S(2)}) collective-permute-start(bf16[48,1024]{1,0:T(8,128)(2,1)S(1)} %add.23.refs_0_), channel_id=1, source_target_pairs={{0,12},{1,13},{2,14},{3,15},{4,0},{5,1},{6,2},{7,3},{8,4},{9,5},{1... | collective-permute-start | bytes 294920 | tf_op jit(solution)/shard_map/ppermute | solution.py:575
  158.7 2.4 %collective-permute-done.34.refs_1_ = bf16[48,1024]{1,0:T(8,128)(2,1)S(1)} collective-permute-done((bf16[48,1024]{1,0:T(8,128)(2,1)S(1)}, bf16[48,1024]{1,0:T(8,128)(2,1)S(1)}, u32[]{:S(2)}, u32[]{:S(2)}) %collective-permute-start.34) | collective-permute-done | bytes 98336 | tf_op jit(solution)/shard_map/ppermute | solution.py:575
  (70 shorter events, 37.4 us)
Async XLA Ops:
  2.5 13.2 %collective-permute-start = (bf16[48,2048]{1,0:T(8,128)(2,1)S(1)}, bf16[48,2048]{1,0:T(8,128)(2,1)S(1)}, u32[]{:S(2)}, u32[]{:S(2)}) collective-permute-start(bf16[48,2048]{1,0:T(8,128)(2,1)S(1)} %pack_attention_weights.1), channel_id=1, source_target_pairs={{0,0},{67,1},{2,2},{65,3},{4,4},{71,5},{6,6},{69,7},{8,8},{75,9},{... | collective-permute-start | bytes 589832 | tf_op jit(solution)/shard_map/ppermute | solution.py:575
  11.2 10.3 %collective-permute-start.2 = (bf16[48,2048]{1,0:T(8,128)(2,1)S(1)}, bf16[48,2048]{1,0:T(8,128)(2,1)S(1)}, u32[]{:S(2)}, u32[]{:S(2)}) collective-permute-start(bf16[48,2048]{1,0:T(8,128)(2,1)S(1)} %pack_attention_weights.1), channel_id=1, source_target_pairs={{32,0},{99,1},{34,2},{97,3},{36,4},{103,5},{38,6},{101,7},{40,8},{... | collective-permute-start | bytes 589832 | tf_op jit(solution)/shard_map/ppermute | solution.py:575
  14.1 9.9 %collective-permute-start.3 = (bf16[48,2048]{1,0:T(8,128)(2,1)S(1)}, bf16[48,2048]{1,0:T(8,128)(2,1)S(1)}, u32[]{:S(2)}, u32[]{:S(2)}) collective-permute-start(bf16[48,2048]{1,0:T(8,128)(2,1)S(1)} %pack_attention_weights.1), channel_id=1, source_target_pairs={{48,0},{115,1},{50,2},{113,3},{52,4},{119,5},{54,6},{117,7},{56,8}... | collective-permute-start | bytes 589832 | tf_op jit(solution)/shard_map/ppermute | solution.py:575
  15.6 11.3 %collective-permute-start.4 = (bf16[48,2048]{1,0:T(8,128)(2,1)S(1)}, bf16[48,2048]{1,0:T(8,128)(2,1)S(1)}, u32[]{:S(2)}, u32[]{:S(2)}) collective-permute-start(bf16[48,2048]{1,0:T(8,128)(2,1)S(1)} %collective-permute-done.p0), channel_id=1, source_target_pairs={{0,1},{1,0},{2,3},{3,2},{4,5},{5,4},{6,7},{7,6},{8,9},{9,8},{10,11... | collective-permute-start | bytes 589832 | tf_op jit(solution)/shard_map/ppermute | solution.py:575
  17.8 12.3 %collective-permute-start.5 = (bf16[48,2048]{1,0:T(8,128)(2,1)S(1)}, bf16[48,2048]{1,0:T(8,128)(2,1)S(1)}, u32[]{:S(2)}, u32[]{:S(2)}) collective-permute-start(bf16[48,2048]{1,0:T(8,128)(2,1)S(1)} %collective-permute-done.1.p1), channel_id=1, source_target_pairs={{0,1},{1,0},{2,3},{3,2},{4,5},{5,4},{6,7},{7,6},{8,9},{9,8},{10,11... | collective-permute-start | bytes 589832 | tf_op jit(solution)/shard_map/ppermute | solution.py:575
  21.6 9.2 %collective-permute-start.6 = (bf16[48,2048]{1,0:T(8,128)(2,1)S(1)}, bf16[48,2048]{1,0:T(8,128)(2,1)S(1)}, u32[]{:S(2)}, u32[]{:S(2)}) collective-permute-start(bf16[48,2048]{1,0:T(8,128)(2,1)S(1)} %collective-permute-done.2.p2), channel_id=1, source_target_pairs={{0,1},{1,0},{2,3},{3,2},{4,5},{5,4},{6,7},{7,6},{8,9},{9,8},{10,11... | collective-permute-start | bytes 589832 | tf_op jit(solution)/shard_map/ppermute | solution.py:575
  21.6 12.7 %collective-permute-start.8 = (bf16[48,4992]{1,0:T(8,128)(2,1)S(1)}, bf16[48,4992]{1,0:T(8,128)(2,1)S(1)}, u32[]{:S(2)}, u32[]{:S(2)}) collective-permute-start(bf16[48,4992]{1,0:T(8,128)(2,1)S(1)} %pack_feed_forward_weights.1), channel_id=1, source_target_pairs={{0,0},{67,1},{2,2},{65,3},{4,4},{71,5},{6,6},{69,7},{8,8},{75,9},{... | collective-permute-start | bytes 1437704 | tf_op jit(solution)/shard_map/ppermute | solution.py:575
  24.1 26.9 %collective-permute-start.11 = (bf16[48,4992]{1,0:T(8,128)(2,1)S(1)}, bf16[48,4992]{1,0:T(8,128)(2,1)S(1)}, u32[]{:S(2)}, u32[]{:S(2)}) collective-permute-start(bf16[48,4992]{1,0:T(8,128)(2,1)S(1)} %pack_feed_forward_weights.1), channel_id=1, source_target_pairs={{48,0},{115,1},{50,2},{113,3},{52,4},{119,5},{54,6},{117,7},{56,8}... | collective-permute-start | bytes 1437704 | tf_op jit(solution)/shard_map/ppermute | solution.py:575
  27.0 24.0 %collective-permute-start.10 = (bf16[48,4992]{1,0:T(8,128)(2,1)S(1)}, bf16[48,4992]{1,0:T(8,128)(2,1)S(1)}, u32[]{:S(2)}, u32[]{:S(2)}) collective-permute-start(bf16[48,4992]{1,0:T(8,128)(2,1)S(1)} %pack_feed_forward_weights.1), channel_id=1, source_target_pairs={{32,0},{99,1},{34,2},{97,3},{36,4},{103,5},{38,6},{101,7},{40,8},{... | collective-permute-start | bytes 1437704 | tf_op jit(solution)/shard_map/ppermute | solution.py:575
  30.1 22.8 %collective-permute-start.9 = (bf16[48,4992]{1,0:T(8,128)(2,1)S(1)}, bf16[48,4992]{1,0:T(8,128)(2,1)S(1)}, u32[]{:S(2)}, u32[]{:S(2)}) collective-permute-start(bf16[48,4992]{1,0:T(8,128)(2,1)S(1)} %pack_feed_forward_weights.1), channel_id=1, source_target_pairs={{16,0},{83,1},{18,2},{81,3},{20,4},{87,5},{22,6},{85,7},{24,8},{91... | collective-permute-start | bytes 1437704 | tf_op jit(solution)/shard_map/ppermute | solution.py:575
  34.3 19.2 %collective-permute-start.12 = (bf16[48,4992]{1,0:T(8,128)(2,1)S(1)}, bf16[48,4992]{1,0:T(8,128)(2,1)S(1)}, u32[]{:S(2)}, u32[]{:S(2)}) collective-permute-start(bf16[48,4992]{1,0:T(8,128)(2,1)S(1)} %collective-permute-done.8.p0), channel_id=1, source_target_pairs={{0,1},{1,0},{2,3},{3,2},{4,5},{5,4},{6,7},{7,6},{8,9},{9,8},{10,11... | collective-permute-start | bytes 1437704 | tf_op jit(solution)/shard_map/ppermute | solution.py:575
  61.7 23.3 %collective-permute-start.16 = (bf16[192,5120]{1,0:T(8,128)(2,1)S(1)}, bf16[192,5120]{1,0:T(8,128)(2,1)S(1)}, u32[]{:S(2)}, u32[]{:S(2)}) collective-permute-start(bf16[192,5120]{1,0:T(8,128)(2,1)S(1)} %get-tuple-element.93), channel_id=1, source_target_pairs={{0,1},{1,0},{2,3},{3,2},{4,5},{5,4},{6,7},{7,6},{8,9},{9,8},{10,11... | collective-permute-start | bytes 5898248 | tf_op jit(solution)/shard_map/ppermute | solution.py:575
  85.5 32.1 %collective-permute-start.17 = (bf16[48,5120]{1,0:T(8,128)(2,1)S(1)}, bf16[48,5120]{1,0:T(8,128)(2,1)S(1)}, u32[]{:S(2)}, u32[]{:S(2)}) collective-permute-start(bf16[48,5120]{1,0:T(8,128)(2,1)S(1)} %get-tuple-element.94), channel_id=1, source_target_pairs={{0,0},{1,67},{2,2},{3,65},{4,4},{5,71},{6,6},{7,69},{8,8},{9,75},{... | collective-permute-start | bytes 1474568 | tf_op jit(solution)/shard_map/ppermute | solution.py:575
  88.8 27.1 %collective-permute-start.18 = (bf16[48,5120]{1,0:T(8,128)(2,1)S(1)}, bf16[48,5120]{1,0:T(8,128)(2,1)S(1)}, u32[]{:S(2)}, u32[]{:S(2)}) collective-permute-start(bf16[48,5120]{1,0:T(8,128)(2,1)S(1)} %get-tuple-element.100), channel_id=1, source_target_pairs={{0,16},{1,83},{2,18},{3,81},{4,20},{5,87},{6,22},{7,85},{8,24},{9,... | collective-permute-start | bytes 1474568 | tf_op jit(solution)/shard_map/ppermute | solution.py:575
  88.9 27.0 %collective-permute-start.19 = (bf16[48,5120]{1,0:T(8,128)(2,1)S(1)}, bf16[48,5120]{1,0:T(8,128)(2,1)S(1)}, u32[]{:S(2)}, u32[]{:S(2)}) collective-permute-start(bf16[48,5120]{1,0:T(8,128)(2,1)S(1)} %get-tuple-element.101), channel_id=1, source_target_pairs={{0,32},{1,99},{2,34},{3,97},{4,36},{5,103},{6,38},{7,101},{8,40},{... | collective-permute-start | bytes 1474568 | tf_op jit(solution)/shard_map/ppermute | solution.py:575
  91.3 26.3 %collective-permute-start.20 = (bf16[48,5120]{1,0:T(8,128)(2,1)S(1)}, bf16[48,5120]{1,0:T(8,128)(2,1)S(1)}, u32[]{:S(2)}, u32[]{:S(2)}) collective-permute-start(bf16[48,5120]{1,0:T(8,128)(2,1)S(1)} %get-tuple-element.102), channel_id=1, source_target_pairs={{0,48},{1,115},{2,50},{3,113},{4,52},{5,119},{6,54},{7,117},{8,56}... | collective-permute-start | bytes 1474568 | tf_op jit(solution)/shard_map/ppermute | solution.py:575
  120.6 10.1 %collective-permute-start.29 = (bf16[48,2560]{1,0:T(8,128)(2,1)S(1)}, bf16[48,2560]{1,0:T(8,128)(2,1)S(1)}, u32[]{:S(2)}, u32[]{:S(2)}) collective-permute-start(bf16[48,2560]{1,0:T(8,128)(2,1)S(1)} %add.24.refs_0_), channel_id=1, source_target_pairs={{0,2},{1,3},{2,0},{3,1},{4,6},{5,7},{6,4},{7,5},{8,10},{9,11},{10,... | collective-permute-start | bytes 737288 | tf_op jit(solution)/shard_map/ppermute | solution.py:575
  122.0 15.5 %collective-permute-start.22 = (bf16[48,2048]{1,0:T(8,128)(2,1)S(1)}, bf16[48,2048]{1,0:T(8,128)(2,1)S(1)}, u32[]{:S(2)}, u32[]{:S(2)}) collective-permute-start(bf16[48,2048]{1,0:T(8,128)(2,1)S(1)} %get-tuple-element.104), channel_id=1, source_target_pairs={{0,0},{1,67},{2,2},{3,65},{4,4},{5,71},{6,6},{7,69},{8,8},{9,75},{... | collective-permute-start | bytes 589832 | tf_op jit(solution)/shard_map/ppermute | solution.py:575
  125.7 14.5 %collective-permute-start.23 = (bf16[48,2048]{1,0:T(8,128)(2,1)S(1)}, bf16[48,2048]{1,0:T(8,128)(2,1)S(1)}, u32[]{:S(2)}, u32[]{:S(2)}) collective-permute-start(bf16[48,2048]{1,0:T(8,128)(2,1)S(1)} %get-tuple-element.105), channel_id=1, source_target_pairs={{0,16},{1,83},{2,18},{3,81},{4,20},{5,87},{6,22},{7,85},{8,24},{9,... | collective-permute-start | bytes 589832 | tf_op jit(solution)/shard_map/ppermute | solution.py:575
  125.8 14.8 %collective-permute-start.24 = (bf16[48,2048]{1,0:T(8,128)(2,1)S(1)}, bf16[48,2048]{1,0:T(8,128)(2,1)S(1)}, u32[]{:S(2)}, u32[]{:S(2)}) collective-permute-start(bf16[48,2048]{1,0:T(8,128)(2,1)S(1)} %get-tuple-element.106), channel_id=1, source_target_pairs={{0,32},{1,99},{2,34},{3,97},{4,36},{5,103},{6,38},{7,101},{8,40},{... | collective-permute-start | bytes 589832 | tf_op jit(solution)/shard_map/ppermute | solution.py:575
  129.3 11.4 %collective-permute-start.25 = (bf16[48,2048]{1,0:T(8,128)(2,1)S(1)}, bf16[48,2048]{1,0:T(8,128)(2,1)S(1)}, u32[]{:S(2)}, u32[]{:S(2)}) collective-permute-start(bf16[48,2048]{1,0:T(8,128)(2,1)S(1)} %get-tuple-element.107), channel_id=1, source_target_pairs={{0,48},{1,115},{2,50},{3,113},{4,52},{5,119},{6,54},{7,117},{8,56}... | collective-permute-start | bytes 589832 | tf_op jit(solution)/shard_map/ppermute | solution.py:575
  130.7 16.3 %collective-permute-start.32 = (bf16[48,2560]{1,0:T(8,128)(2,1)S(1)}, bf16[48,2560]{1,0:T(8,128)(2,1)S(1)}, u32[]{:S(2)}, u32[]{:S(2)}) collective-permute-start(bf16[48,2560]{1,0:T(8,128)(2,1)S(1)} %add.25.refs_0_), channel_id=1, source_target_pairs={{0,12},{1,13},{2,14},{3,15},{4,0},{5,1},{6,2},{7,3},{8,4},{9,5},{1... | collective-permute-start | bytes 737288 | tf_op jit(solution)/shard_map/ppermute | solution.py:575
  137.5 9.6 %collective-permute-start.31 = (bf16[48,2560]{1,0:T(8,128)(2,1)S(1)}, bf16[48,2560]{1,0:T(8,128)(2,1)S(1)}, u32[]{:S(2)}, u32[]{:S(2)}) collective-permute-start(bf16[48,2560]{1,0:T(8,128)(2,1)S(1)} %add.25.refs_0_), channel_id=1, source_target_pairs={{0,8},{1,9},{2,10},{3,11},{4,12},{5,13},{6,14},{7,15},{8,0},{9,1},... | collective-permute-start | bytes 737288 | tf_op jit(solution)/shard_map/ppermute | solution.py:575
  140.1 10.3 %collective-permute-start.30 = (bf16[48,2560]{1,0:T(8,128)(2,1)S(1)}, bf16[48,2560]{1,0:T(8,128)(2,1)S(1)}, u32[]{:S(2)}, u32[]{:S(2)}) collective-permute-start(bf16[48,2560]{1,0:T(8,128)(2,1)S(1)} %add.25.refs_0_), channel_id=1, source_target_pairs={{0,4},{1,5},{2,6},{3,7},{4,8},{5,9},{6,10},{7,11},{8,12},{9,13},{1... | collective-permute-start | bytes 737288 | tf_op jit(solution)/shard_map/ppermute | solution.py:575
  (14 other events, 51.9 us)
